TPU v7x, 1024 devices: a whole 4x8x16 slice. The times are simulated.
1024 devices in a mesh: row: 64 (over y, z_lo, core), col: 16 (over x, z_hi).
Axes of the slice: x: 4, y: 8, z: 16 (z_hi: 4, z_lo: 4; z = z_hi * 4 + z_lo), core: 2. Of those that a mesh axis runs over, the one named last changes fastest.
Arguments:
- populations: float32 [19, 8, 512, 2048], P(None, None, 'row', 'col'), may hold values from 0 to 0.6, as said below
- order_tensor: float32 [5, 8, 512, 2048], P(None, None, 'row', 'col'), may hold values from -0.8 to 0.8
Outputs:
- new_populations: float32 [19, 8, 512, 2048], P(None, None, 'row', 'col')
- new_order: float32 [5, 8, 512, 2048], P(None, None, 'row', 'col')
Inputs may be any that keep to these rules, and one draw needn't show every extreme that they name: `populations`: each population lies between 0.3 and 1.7 times its lattice weight.
All inputs are finite; a program needn't handle non-finite values.
Results may differ from a plain program's by a relative error of at most 0.0001.
Values sent between devices are 32-bit elements; how exact they have to be, the bound alone decides.
No kernel may reach another device: no remote copies, remote signals or barrier semaphores. Data moves between devices by JAX's collectives and lax.ppermute only.
A program may use at most 32 MiB of HBM per device.

v0:
```python
import math

import jax
import jax.numpy as jnp
import numpy as np
from jax import lax
from jax.sharding import PartitionSpec as P

SUBSTEPS = 3


lattice = np.array(
    [
        [0, 0, 0],
        [1, 0, 0],
        [-1, 0, 0],
        [0, 1, 0],
        [0, -1, 0],
        [0, 0, 1],
        [0, 0, -1],
        [1, 1, 0],
        [-1, -1, 0],
        [1, -1, 0],
        [-1, 1, 0],
        [1, 0, 1],
        [-1, 0, -1],
        [1, 0, -1],
        [-1, 0, 1],
        [0, 1, 1],
        [0, -1, -1],
        [0, 1, -1],
        [0, -1, 1],
    ]
)
lattice_weights = np.array([1.0 / 3.0] + [1.0 / 18.0] * 6 + [1.0 / 36.0] * 12)
tau_rate = 1.25
a_zero = 0.1
gamma_bulk = 3.0
stiffness = 0.4
pitch_wave = math.pi / 8.0
mobility_dt = 0.3
levi_terms = (
    (0, 1, 2, 1.0),
    (1, 2, 0, 1.0),
    (2, 0, 1, 1.0),
    (0, 2, 1, -1.0),
    (2, 1, 0, -1.0),
    (1, 0, 2, -1.0),
)
index_pairs = ((0, 0), (0, 1), (0, 2), (1, 1), (1, 2))


def padded_2(block, sides, width):
    for axis, dim in sides:
        count = lax.axis_size(axis)
        forward = [(i, i + 1) for i in range(count - 1)]
        forward.append((count - 1, 0))
        backward = [(target, source) for source, target in forward]
        low = lax.ppermute(
            lax.slice_in_dim(block, block.shape[dim] - width, None, axis=dim), axis, forward
        )
        high = lax.ppermute(lax.slice_in_dim(block, 0, width, axis=dim), axis, backward)
        block = jnp.concatenate([low, block, high], axis=dim)
    return block


def full_tensor(components):
    trace_part = -components[0] - components[3]
    return [
        [components[0], components[1], components[2]],
        [components[1], components[3], components[4]],
        [components[2], components[4], trace_part],
    ]


def relax_step(center, laplace, gradient, velocity, want_force):
    tensor = full_tensor(center)
    slopes = [full_tensor(gradient[c]) for c in range(3)]
    square_sum = sum((tensor[a][b] * tensor[a][b] for a in range(3) for b in range(3)))
    fields = []
    updated = []
    for k, (a, b) in enumerate(index_pairs):
        product = (
            tensor[a][0] * tensor[0][b] + tensor[a][1] * tensor[1][b] + tensor[a][2] * tensor[2][b]
        )
        chiral = jnp.zeros_like(product)
        for i, c, d, s in levi_terms:
            if i == a:
                chiral = chiral + s * slopes[c][d][b]
            if i == b:
                chiral = chiral + s * slopes[c][d][a]
        isotropic = square_sum / 3.0 if a == b else 0.0
        bulk_term = (
            a_zero * (gamma_bulk / 3.0 - 1.0) * tensor[a][b]
            + a_zero * gamma_bulk * (product - isotropic)
            - a_zero * gamma_bulk * square_sum * tensor[a][b]
        )
        molecular = bulk_term + stiffness * (
            laplace[k] - 4.0 * pitch_wave**2 * tensor[a][b] - 2.0 * pitch_wave * chiral
        )
        fields.append(molecular)
        carried = (
            velocity[0] * gradient[0][k]
            + velocity[1] * gradient[1][k]
            + velocity[2] * gradient[2][k]
        )
        updated.append(center[k] + mobility_dt * molecular - carried)
    if not want_force:
        return (updated, None)
    field_full = full_tensor(fields)
    body_force = [
        sum((field_full[b][c] * slopes[a][b][c] for b in range(3) for c in range(3)))
        for a in range(3)
    ]
    return (updated, body_force)


def stencil_terms(center, x_ahead, x_behind, y_ahead, y_behind):
    z_ahead = jnp.roll(center, -1, axis=0)
    z_behind = jnp.roll(center, 1, axis=0)
    laplace = x_ahead + x_behind + y_ahead + y_behind + z_ahead + z_behind - 6.0 * center
    gradient = [0.5 * (x_ahead - x_behind), 0.5 * (y_ahead - y_behind), 0.5 * (z_ahead - z_behind)]
    return (laplace, gradient)


def moments(populations):
    lattice_table = jnp.asarray(lattice, jnp.float32)
    density = jnp.sum(populations, axis=0)
    momentum = jnp.einsum(
        "ia,izxy->azxy", lattice_table, populations, precision=lax.Precision.HIGHEST
    )
    return (density, momentum)


def collide(populations, density, momentum, body_force):
    lattice_table = jnp.asarray(lattice, jnp.float32)
    weight_column = jnp.asarray(lattice_weights, jnp.float32)[:, None, None, None]
    velocity = (momentum + 0.5 * body_force) / density[None]
    along_speed = jnp.einsum(
        "ia,azxy->izxy", lattice_table, velocity, precision=lax.Precision.HIGHEST
    )
    along_force = jnp.einsum(
        "ia,azxy->izxy", lattice_table, body_force, precision=lax.Precision.HIGHEST
    )
    speed_squared = jnp.sum(velocity * velocity, axis=0)
    speed_force = jnp.sum(velocity * body_force, axis=0)
    equilibrium = (
        weight_column
        * density[None]
        * (1.0 + 3.0 * along_speed + 4.5 * along_speed * along_speed - 1.5 * speed_squared[None])
    )
    source = weight_column * (
        3.0 * (along_force - speed_force[None]) + 9.0 * along_speed * along_force
    )
    return populations - tau_rate * (populations - equilibrium) + (1.0 - 0.5 * tau_rate) * source


def advance(padded, velocity, want_force):
    laplace = []
    per_component = []
    centers = []
    for k in range(5):
        plane = padded[k]
        center = plane[:, 1:-1, 1:-1]
        lap_term, grad_term = stencil_terms(
            center, plane[:, 2:, 1:-1], plane[:, :-2, 1:-1], plane[:, 1:-1, 2:], plane[:, 1:-1, :-2]
        )
        centers.append(center)
        laplace.append(lap_term)
        per_component.append(grad_term)
    gradient = [[per_component[k][c] for k in range(5)] for c in range(3)]
    return relax_step(centers, laplace, gradient, velocity, want_force)


def body(populations, order_tensor):
    density, momentum = moments(populations)
    velocity = momentum / density[None]
    body_force = None
    current = order_tensor
    for substep in range(SUBSTEPS):
        padded = padded_2(current, (("row", 2), ("col", 3)), 1)
        components, body_force = advance(
            padded, [velocity[0], velocity[1], velocity[2]], substep == SUBSTEPS - 1
        )
        current = jnp.stack(components)
    collided = collide(populations, density, momentum, jnp.stack(body_force))
    width_x = collided.shape[2]
    width_y = collided.shape[3]
    arrived = []
    widened_f = padded_2(collided, (("row", 2), ("col", 3)), 1)
    for i in range(19):
        a, b, c = (int(lattice[i][0]), int(lattice[i][1]), int(lattice[i][2]))
        window = widened_f[i, :, 1 - a : 1 - a + width_x, 1 - b : 1 - b + width_y]
        arrived.append(jnp.roll(window, c, axis=0))
    return (jnp.stack(arrived), current)


def solution(mesh):
    return jax.shard_map(
        body,
        mesh=mesh,
        in_specs=(P(None, None, "row", "col"), P(None, None, "row", "col")),
        out_specs=(P(None, None, "row", "col"), P(None, None, "row", "col")),
        check_vma=False,
    )
```

profile of v0, /device:TPU:6, one launch (start us, length us, event | category | flops | bytes accessed | tf_op | source)
XLA Modules:
  0.0 210.1 jit_solution(7706171043107215930)
XLA Ops:
  1.8 1.9 collective-permute-start
  3.7 10.2 %collective-permute-start.1 = (f32[5,8,1,128]{3,2,1,0:T(1,128)S(1)}, f32[5,8,1,128]{3,2,1,0:T(1,128)S(1)}, u32[]{:S(2)}, u32[]{:S(2)}) collective-permute-start(f32[5,8,1,128]{3,2,1,0:T(1,128)S(1)} %get-tuple-element.75), channel_id=1, source_target_pairs={{16,0},{32,16},{48,32},{64,48},{80,64},{96,80},{112,96},{128,112},... | collective-permute-start | bytes 61448 | tf_op jit(solution)/shard_map/ppermute | solution.py:62
  13.9 1.9 fusion
  16.2 10.9 %collective-permute-start.2 = (f32[5,8,10,1]{3,2,1,0:T(8,128)S(1)}, f32[5,8,10,1]{3,2,1,0:T(8,128)S(1)}, u32[]{:S(2)}, u32[]{:S(2)}) collective-permute-start(f32[5,8,10,1]{3,2,1,0:T(8,128)S(1)} %get-tuple-element.68), channel_id=1, source_target_pairs={{0,1},{1,2},{2,3},{3,4},{4,5},{5,6},{6,7},{7,8},{8,9},{9,10},{10,1... | collective-permute-start | bytes 4808 | tf_op jit(solution)/shard_map/ppermute | solution.py:59
  27.1 6.8 %collective-permute-start.3 = (f32[5,8,10,1]{3,2,1,0:T(8,128)S(1)}, f32[5,8,10,1]{3,2,1,0:T(8,128)S(1)}, u32[]{:S(2)}, u32[]{:S(2)}) collective-permute-start(f32[5,8,10,1]{3,2,1,0:T(8,128)S(1)} %get-tuple-element.69), channel_id=1, source_target_pairs={{1,0},{2,1},{3,2},{4,3},{5,4},{6,5},{7,6},{8,7},{9,8},{10,9},{11,1... | collective-permute-start | bytes 4808 | tf_op jit(solution)/shard_map/ppermute | solution.py:62
  33.9 6.9 %collective-permute-done.2 = f32[5,8,10,1]{3,2,1,0:T(8,128)S(1)} collective-permute-done((f32[5,8,10,1]{3,2,1,0:T(8,128)S(1)}, f32[5,8,10,1]{3,2,1,0:T(8,128)S(1)}, u32[]{:S(2)}, u32[]{:S(2)}) %collective-permute-start.2) | collective-permute-done | bytes 1632 | tf_op jit(solution)/shard_map/ppermute | solution.py:59
  40.8 20.6 %collective-permute-done.3 = f32[5,8,10,1]{3,2,1,0:T(8,128)S(1)} collective-permute-done((f32[5,8,10,1]{3,2,1,0:T(8,128)S(1)}, f32[5,8,10,1]{3,2,1,0:T(8,128)S(1)}, u32[]{:S(2)}, u32[]{:S(2)}) %collective-permute-start.3) | collective-permute-done | bytes 1632 | tf_op jit(solution)/shard_map/ppermute | solution.py:62
  63.5 1.9 collective-permute-start.4
  65.4 7.5 %collective-permute-start.5 = (f32[5,8,1,128]{3,2,1,0:T(1,128)S(1)}, f32[5,8,1,128]{3,2,1,0:T(1,128)S(1)}, u32[]{:S(2)}, u32[]{:S(2)}) collective-permute-start(f32[5,8,1,128]{3,2,1,0:T(1,128)S(1)} %get-tuple-element.73), channel_id=1, source_target_pairs={{16,0},{32,16},{48,32},{64,48},{80,64},{96,80},{112,96},{128,112},... | collective-permute-start | bytes 61448 | tf_op jit(solution)/shard_map/ppermute | solution.py:62
  74.7 7.5 %collective-permute-start.6 = (f32[5,8,10,1]{3,2,1,0:T(8,128)S(1)}, f32[5,8,10,1]{3,2,1,0:T(8,128)S(1)}, u32[]{:S(2)}, u32[]{:S(2)}) collective-permute-start(f32[5,8,10,1]{3,2,1,0:T(8,128)S(1)} %get-tuple-element.66), channel_id=1, source_target_pairs={{0,1},{1,2},{2,3},{3,4},{4,5},{5,6},{6,7},{7,8},{8,9},{9,10},{10,1... | collective-permute-start | bytes 4808 | tf_op jit(solution)/shard_map/ppermute | solution.py:59
  82.1 3.2 %collective-permute-start.7 = (f32[5,8,10,1]{3,2,1,0:T(8,128)S(1)}, f32[5,8,10,1]{3,2,1,0:T(8,128)S(1)}, u32[]{:S(2)}, u32[]{:S(2)}) collective-permute-start(f32[5,8,10,1]{3,2,1,0:T(8,128)S(1)} %get-tuple-element.67), channel_id=1, source_target_pairs={{1,0},{2,1},{3,2},{4,3},{5,4},{6,5},{7,6},{8,7},{9,8},{10,9},{11,1... | collective-permute-start | bytes 4808 | tf_op jit(solution)/shard_map/ppermute | solution.py:62
  85.3 22.6 %collective-permute-done.6 = f32[5,8,10,1]{3,2,1,0:T(8,128)S(1)} collective-permute-done((f32[5,8,10,1]{3,2,1,0:T(8,128)S(1)}, f32[5,8,10,1]{3,2,1,0:T(8,128)S(1)}, u32[]{:S(2)}, u32[]{:S(2)}) %collective-permute-start.6) | collective-permute-done | bytes 1632 | tf_op jit(solution)/shard_map/ppermute | solution.py:59
  110.2 1.9 collective-permute-start.8
  112.1 10.6 %collective-permute-start.9 = (f32[5,8,1,128]{3,2,1,0:T(1,128)S(1)}, f32[5,8,1,128]{3,2,1,0:T(1,128)S(1)}, u32[]{:S(2)}, u32[]{:S(2)}) collective-permute-start(f32[5,8,1,128]{3,2,1,0:T(1,128)S(1)} %get-tuple-element.71), channel_id=1, source_target_pairs={{16,0},{32,16},{48,32},{64,48},{80,64},{96,80},{112,96},{128,112},... | collective-permute-start | bytes 61448 | tf_op jit(solution)/shard_map/ppermute | solution.py:62
  124.4 7.8 %collective-permute-start.10 = (f32[5,8,10,1]{3,2,1,0:T(8,128)S(1)}, f32[5,8,10,1]{3,2,1,0:T(8,128)S(1)}, u32[]{:S(2)}, u32[]{:S(2)}) collective-permute-start(f32[5,8,10,1]{3,2,1,0:T(8,128)S(1)} %get-tuple-element.64), channel_id=1, source_target_pairs={{0,1},{1,2},{2,3},{3,4},{4,5},{5,6},{6,7},{7,8},{8,9},{9,10},{10,1... | collective-permute-start | bytes 4808 | tf_op jit(solution)/shard_map/ppermute | solution.py:59
  132.2 2.9 %collective-permute-start.11 = (f32[5,8,10,1]{3,2,1,0:T(8,128)S(1)}, f32[5,8,10,1]{3,2,1,0:T(8,128)S(1)}, u32[]{:S(2)}, u32[]{:S(2)}) collective-permute-start(f32[5,8,10,1]{3,2,1,0:T(8,128)S(1)} %get-tuple-element.65), channel_id=1, source_target_pairs={{1,0},{2,1},{3,2},{4,3},{5,4},{6,5},{7,6},{8,7},{9,8},{10,9},{11,1... | collective-permute-start | bytes 4808 | tf_op jit(solution)/shard_map/ppermute | solution.py:62
  135.1 20.6 %collective-permute-done.10 = f32[5,8,10,1]{3,2,1,0:T(8,128)S(1)} collective-permute-done((f32[5,8,10,1]{3,2,1,0:T(8,128)S(1)}, f32[5,8,10,1]{3,2,1,0:T(8,128)S(1)}, u32[]{:S(2)}, u32[]{:S(2)}) %collective-permute-start.10) | collective-permute-done | bytes 1632 | tf_op jit(solution)/shard_map/ppermute | solution.py:59
  155.7 4.2 %collective-permute-done.11 = f32[5,8,10,1]{3,2,1,0:T(8,128)S(1)} collective-permute-done((f32[5,8,10,1]{3,2,1,0:T(8,128)S(1)}, f32[5,8,10,1]{3,2,1,0:T(8,128)S(1)}, u32[]{:S(2)}, u32[]{:S(2)}) %collective-permute-start.11) | collective-permute-done | bytes 1632 | tf_op jit(solution)/shard_map/ppermute | solution.py:62
  165.1 1.9 collective-permute-start.12
  167.1 11.0 %collective-permute-start.13 = (f32[19,8,1,128]{3,2,1,0:T(1,128)S(1)}, f32[19,8,1,128]{3,2,1,0:T(1,128)S(1)}, u32[]{:S(2)}, u32[]{:S(2)}) collective-permute-start(f32[19,8,1,128]{3,2,1,0:T(1,128)S(1)} %get-tuple-element.62), channel_id=1, source_target_pairs={{16,0},{32,16},{48,32},{64,48},{80,64},{96,80},{112,96},{128,112},... | collective-permute-start | bytes 233480 | tf_op jit(solution)/shard_map/ppermute | solution.py:62
  180.4 1.5 fusion.84
  181.9 1.9 copy.52
  183.8 2.6 %collective-permute-start.14 = (f32[19,8,10,1]{0,1,3,2:T(8,128)S(1)}, f32[19,8,10,1]{0,1,3,2:T(8,128)S(1)}, u32[]{:S(2)}, u32[]{:S(2)}) collective-permute-start(f32[19,8,10,1]{0,1,3,2:T(8,128)S(1)} %copy.52), channel_id=1, source_target_pairs={{0,1},{1,2},{2,3},{3,4},{4,5},{5,6},{6,7},{7,8},{8,9},{9,10},{10,1... | collective-permute-start | bytes 18248 | tf_op jit(solution)/shard_map/ppermute | solution.py:59
  187.1 8.2 %collective-permute-start.15 = (f32[19,8,10,1]{0,1,3,2:T(8,128)S(1)}, f32[19,8,10,1]{0,1,3,2:T(8,128)S(1)}, u32[]{:S(2)}, u32[]{:S(2)}) collective-permute-start(f32[19,8,10,1]{0,1,3,2:T(8,128)S(1)} %copy.54), channel_id=1, source_target_pairs={{1,0},{2,1},{3,2},{4,3},{5,4},{6,5},{7,6},{8,7},{9,8},{10,9},{11,1... | collective-permute-start | bytes 18248 | tf_op jit(solution)/shard_map/ppermute | solution.py:62
  (115 shorter events, 31.6 us)
Async XLA Ops:
  0.6 15.3 %copy-start.1 = (f32[5,8,8,128]{3,2,1,0:T(8,128)S(1)}, f32[5,8,8,128]{3,2,1,0:T(8,128)}, u32[]{:S(2)}) copy-start(f32[5,8,8,128]{3,2,1,0:T(8,128)} %param.6) | copy-start | bytes 491524
  0.6 15.2 %copy-start = (f32[19,8,8,128]{3,2,1,0:T(8,128)S(1)}, f32[19,8,8,128]{3,2,1,0:T(8,128)}, u32[]{:S(2)}) copy-start(f32[19,8,8,128]{3,2,1,0:T(8,128)} %param.5) | copy-start | bytes 1867780
  1.8 14.2 %collective-permute-start = (f32[5,8,1,128]{3,2,1,0:T(1,128)S(1)}, f32[5,8,1,128]{3,2,1,0:T(1,128)S(1)}, u32[]{:S(2)}, u32[]{:S(2)}) collective-permute-start(f32[5,8,1,128]{3,2,1,0:T(1,128)S(1)} %get-tuple-element.74), channel_id=1, source_target_pairs={{0,16},{16,32},{32,48},{48,64},{64,80},{80,96},{96,112},{112,128},... | collective-permute-start | bytes 61448 | tf_op jit(solution)/shard_map/ppermute | solution.py:59
  3.7 12.3 %collective-permute-start.1 = (f32[5,8,1,128]{3,2,1,0:T(1,128)S(1)}, f32[5,8,1,128]{3,2,1,0:T(1,128)S(1)}, u32[]{:S(2)}, u32[]{:S(2)}) collective-permute-start(f32[5,8,1,128]{3,2,1,0:T(1,128)S(1)} %get-tuple-element.75), channel_id=1, source_target_pairs={{16,0},{32,16},{48,32},{64,48},{80,64},{96,80},{112,96},{128,112},... | collective-permute-start | bytes 61448 | tf_op jit(solution)/shard_map/ppermute | solution.py:62
  16.2 24.6 %collective-permute-start.2 = (f32[5,8,10,1]{3,2,1,0:T(8,128)S(1)}, f32[5,8,10,1]{3,2,1,0:T(8,128)S(1)}, u32[]{:S(2)}, u32[]{:S(2)}) collective-permute-start(f32[5,8,10,1]{3,2,1,0:T(8,128)S(1)} %get-tuple-element.68), channel_id=1, source_target_pairs={{0,1},{1,2},{2,3},{3,4},{4,5},{5,6},{6,7},{7,8},{8,9},{9,10},{10,1... | collective-permute-start | bytes 4808 | tf_op jit(solution)/shard_map/ppermute | solution.py:59
  27.1 34.4 %collective-permute-start.3 = (f32[5,8,10,1]{3,2,1,0:T(8,128)S(1)}, f32[5,8,10,1]{3,2,1,0:T(8,128)S(1)}, u32[]{:S(2)}, u32[]{:S(2)}) collective-permute-start(f32[5,8,10,1]{3,2,1,0:T(8,128)S(1)} %get-tuple-element.69), channel_id=1, source_target_pairs={{1,0},{2,1},{3,2},{4,3},{5,4},{6,5},{7,6},{8,7},{9,8},{10,9},{11,1... | collective-permute-start | bytes 4808 | tf_op jit(solution)/shard_map/ppermute | solution.py:62
  63.5 9.5 %collective-permute-start.4 = (f32[5,8,1,128]{3,2,1,0:T(1,128)S(1)}, f32[5,8,1,128]{3,2,1,0:T(1,128)S(1)}, u32[]{:S(2)}, u32[]{:S(2)}) collective-permute-start(f32[5,8,1,128]{3,2,1,0:T(1,128)S(1)} %get-tuple-element.72), channel_id=1, source_target_pairs={{0,16},{16,32},{32,48},{48,64},{64,80},{80,96},{96,112},{112,128},... | collective-permute-start | bytes 61448 | tf_op jit(solution)/shard_map/ppermute | solution.py:59
  65.4 9.0 %collective-permute-start.5 = (f32[5,8,1,128]{3,2,1,0:T(1,128)S(1)}, f32[5,8,1,128]{3,2,1,0:T(1,128)S(1)}, u32[]{:S(2)}, u32[]{:S(2)}) collective-permute-start(f32[5,8,1,128]{3,2,1,0:T(1,128)S(1)} %get-tuple-element.73), channel_id=1, source_target_pairs={{16,0},{32,16},{48,32},{64,48},{80,64},{96,80},{112,96},{128,112},... | collective-permute-start | bytes 61448 | tf_op jit(solution)/shard_map/ppermute | solution.py:62
  74.7 33.2 %collective-permute-start.6 = (f32[5,8,10,1]{3,2,1,0:T(8,128)S(1)}, f32[5,8,10,1]{3,2,1,0:T(8,128)S(1)}, u32[]{:S(2)}, u32[]{:S(2)}) collective-permute-start(f32[5,8,10,1]{3,2,1,0:T(8,128)S(1)} %get-tuple-element.66), channel_id=1, source_target_pairs={{0,1},{1,2},{2,3},{3,4},{4,5},{5,6},{6,7},{7,8},{8,9},{9,10},{10,1... | collective-permute-start | bytes 4808 | tf_op jit(solution)/shard_map/ppermute | solution.py:59
  82.1 25.8 %collective-permute-start.7 = (f32[5,8,10,1]{3,2,1,0:T(8,128)S(1)}, f32[5,8,10,1]{3,2,1,0:T(8,128)S(1)}, u32[]{:S(2)}, u32[]{:S(2)}) collective-permute-start(f32[5,8,10,1]{3,2,1,0:T(8,128)S(1)} %get-tuple-element.67), channel_id=1, source_target_pairs={{1,0},{2,1},{3,2},{4,3},{5,4},{6,5},{7,6},{8,7},{9,8},{10,9},{11,1... | collective-permute-start | bytes 4808 | tf_op jit(solution)/shard_map/ppermute | solution.py:62
  110.2 12.5 %collective-permute-start.8 = (f32[5,8,1,128]{3,2,1,0:T(1,128)S(1)}, f32[5,8,1,128]{3,2,1,0:T(1,128)S(1)}, u32[]{:S(2)}, u32[]{:S(2)}) collective-permute-start(f32[5,8,1,128]{3,2,1,0:T(1,128)S(1)} %get-tuple-element.70), channel_id=1, source_target_pairs={{0,16},{16,32},{32,48},{48,64},{64,80},{80,96},{96,112},{112,128},... | collective-permute-start | bytes 61448 | tf_op jit(solution)/shard_map/ppermute | solution.py:59
  112.1 12.1 %collective-permute-start.9 = (f32[5,8,1,128]{3,2,1,0:T(1,128)S(1)}, f32[5,8,1,128]{3,2,1,0:T(1,128)S(1)}, u32[]{:S(2)}, u32[]{:S(2)}) collective-permute-start(f32[5,8,1,128]{3,2,1,0:T(1,128)S(1)} %get-tuple-element.71), channel_id=1, source_target_pairs={{16,0},{32,16},{48,32},{64,48},{80,64},{96,80},{112,96},{128,112},... | collective-permute-start | bytes 61448 | tf_op jit(solution)/shard_map/ppermute | solution.py:62
  124.4 31.3 %collective-permute-start.10 = (f32[5,8,10,1]{3,2,1,0:T(8,128)S(1)}, f32[5,8,10,1]{3,2,1,0:T(8,128)S(1)}, u32[]{:S(2)}, u32[]{:S(2)}) collective-permute-start(f32[5,8,10,1]{3,2,1,0:T(8,128)S(1)} %get-tuple-element.64), channel_id=1, source_target_pairs={{0,1},{1,2},{2,3},{3,4},{4,5},{5,6},{6,7},{7,8},{8,9},{9,10},{10,1... | collective-permute-start | bytes 4808 | tf_op jit(solution)/shard_map/ppermute | solution.py:59
  132.2 27.7 %collective-permute-start.11 = (f32[5,8,10,1]{3,2,1,0:T(8,128)S(1)}, f32[5,8,10,1]{3,2,1,0:T(8,128)S(1)}, u32[]{:S(2)}, u32[]{:S(2)}) collective-permute-start(f32[5,8,10,1]{3,2,1,0:T(8,128)S(1)} %get-tuple-element.65), channel_id=1, source_target_pairs={{1,0},{2,1},{3,2},{4,3},{5,4},{6,5},{7,6},{8,7},{9,8},{10,9},{11,1... | collective-permute-start | bytes 4808 | tf_op jit(solution)/shard_map/ppermute | solution.py:62
  161.9 0.9 copy-start.2
  162.2 1.5 copy-start.3
  162.5 2.1 copy-start.4
  165.1 13.6 %collective-permute-start.12 = (f32[19,8,1,128]{3,2,1,0:T(1,128)S(1)}, f32[19,8,1,128]{3,2,1,0:T(1,128)S(1)}, u32[]{:S(2)}, u32[]{:S(2)}) collective-permute-start(f32[19,8,1,128]{3,2,1,0:T(1,128)S(1)} %get-tuple-element.63), channel_id=1, source_target_pairs={{0,16},{16,32},{32,48},{48,64},{64,80},{80,96},{96,112},{112,128},... | collective-permute-start | bytes 233480 | tf_op jit(solution)/shard_map/ppermute | solution.py:59
  167.1 13.0 %collective-permute-start.13 = (f32[19,8,1,128]{3,2,1,0:T(1,128)S(1)}, f32[19,8,1,128]{3,2,1,0:T(1,128)S(1)}, u32[]{:S(2)}, u32[]{:S(2)}) collective-permute-start(f32[19,8,1,128]{3,2,1,0:T(1,128)S(1)} %get-tuple-element.62), channel_id=1, source_target_pairs={{16,0},{32,16},{48,32},{64,48},{80,64},{96,80},{112,96},{128,112},... | collective-permute-start | bytes 233480 | tf_op jit(solution)/shard_map/ppermute | solution.py:62
  183.8 12.8 %collective-permute-start.14 = (f32[19,8,10,1]{0,1,3,2:T(8,128)S(1)}, f32[19,8,10,1]{0,1,3,2:T(8,128)S(1)}, u32[]{:S(2)}, u32[]{:S(2)}) collective-permute-start(f32[19,8,10,1]{0,1,3,2:T(8,128)S(1)} %copy.52), channel_id=1, source_target_pairs={{0,1},{1,2},{2,3},{3,4},{4,5},{5,6},{6,7},{7,8},{8,9},{9,10},{10,1... | collective-permute-start | bytes 18248 | tf_op jit(solution)/shard_map/ppermute | solution.py:59
  187.1 10.9 %collective-permute-start.15 = (f32[19,8,10,1]{0,1,3,2:T(8,128)S(1)}, f32[19,8,10,1]{0,1,3,2:T(8,128)S(1)}, u32[]{:S(2)}, u32[]{:S(2)}) collective-permute-start(f32[19,8,10,1]{0,1,3,2:T(8,128)S(1)} %copy.54), channel_id=1, source_target_pairs={{1,0},{2,1},{3,2},{4,3},{5,4},{6,5},{7,6},{8,7},{9,8},{10,9},{11,1... | collective-permute-start | bytes 18248 | tf_op jit(solution)/shard_map/ppermute | solution.py:62
where the time goes:
time: 211 us; the launch traced here: 210 us
  starting transfers between devices  96.9 us (46%)
  waiting for transfers between devices  79.2 us (38%)
  other arithmetic  17.6 us (8%)
  local copies, waits for them, and re-layouts  11.4 us (5%)
  matrix products  3.66 us (2%)
    ppermute x8, starting transfers between devices, padded_2(): lax.ppermute(lax.slice_in_dim(block, 0, width, axis=dim), axis, backward)  60.4 us
    ppermute x8, waiting for transfers between devices, padded_2(): lax.ppermute(lax.slice_in_dim(block, block.shape[dim] - width, None, axis...  50.1 us
    ppermute x8, starting transfers between devices, padded_2(): lax.ppermute(lax.slice_in_dim(block, block.shape[dim] - width, None, axis...  36.5 us
    ppermute x8, waiting for transfers between devices, padded_2(): lax.ppermute(lax.slice_in_dim(block, 0, width, axis=dim), axis, backward)  29.1 us
    unnamed x29, other arithmetic  13.1 us
  transfers between devices with their start and end apart: 16, of which 8 were waited for; matrix products, arithmetic and copies ran while one was open for 3% of the time, Pallas kernels for 0%

commit v1 on v0

v1 whole, which is shorter than its diff:
```python
import functools
import math

import jax
import jax.numpy as jnp
import numpy as np
from jax import lax
from jax.experimental import pallas as pl
from jax.experimental.pallas import tpu as pltpu
from jax.sharding import PartitionSpec as P

lattice = np.array(
    [
        [0, 0, 0],
        [1, 0, 0],
        [-1, 0, 0],
        [0, 1, 0],
        [0, -1, 0],
        [0, 0, 1],
        [0, 0, -1],
        [1, 1, 0],
        [-1, -1, 0],
        [1, -1, 0],
        [-1, 1, 0],
        [1, 0, 1],
        [-1, 0, -1],
        [1, 0, -1],
        [-1, 0, 1],
        [0, 1, 1],
        [0, -1, -1],
        [0, 1, -1],
        [0, -1, 1],
    ]
)
tau_rate = 1.25
a_zero = 0.1
gamma_bulk = 3.0
stiffness = 0.4
pitch_wave = math.pi / 8.0
mobility_dt = 0.3

x_up = [i for i in range(19) if lattice[i][0] == 1]
x_down = [i + 1 for i in x_up]
y_up = [i for i in range(19) if lattice[i][1] == 1]
y_down = [i for i in range(19) if lattice[i][1] == -1]

VEL, DEN, POP, FACE = 20, 29, 30, 35
SLOTS = 16
FIELDS = 28
f32 = jnp.float32


def lanes():
    return lax.broadcasted_iota(jnp.int32, (8, 128), 1)


def slots():
    return lax.rem(lanes(), SLOTS)


def roll_y(value, shift):
    shift = shift % 128
    return value if shift == 0 else pltpu.roll(value, shift, 1)


def roll_z(value, shift):
    shift = shift % 8
    return value if shift == 0 else pltpu.roll(value, shift, 0)


def is_even(axis):
    return lax.rem(lax.axis_index(axis), 2) == 0


def stencil(center, x_ahead, x_behind):
    y_ahead, y_behind = roll_y(center, -1), roll_y(center, 1)
    z_ahead, z_behind = roll_z(center, -1), roll_z(center, 1)
    around = (x_ahead + x_behind) + (y_ahead + y_behind) + (z_ahead + z_behind)
    return around, (x_ahead - x_behind, y_ahead - y_behind, z_ahead - z_behind)


def molecular_field(q, around, dx, dy, dz):
    q0, q1, q2, q3, q4 = q
    qzz = -(q0 + q3)
    s0, s1, s2, s3, s4 = q0 * q0, q1 * q1, q2 * q2, q3 * q3, q4 * q4
    square = s0 + s3 + qzz * qzz + 2.0 * (s1 + s2 + s4)
    third = square * (1.0 / 3.0)
    bulk = a_zero * gamma_bulk
    product = (
        s0 + s1 + s2 - third,
        q2 * q4 - q1 * qzz,
        q1 * q4 - q2 * q3,
        s1 + s3 + s4 - third,
        q1 * q2 - q4 * q0,
    )
    chiral = (
        2.0 * (dy[2] - dz[1]),
        (dy[4] - dx[2]) + (dz[0] - dz[3]),
        (dx[1] - dz[4]) - (2.0 * dy[0] + dy[3]),
        2.0 * (dz[1] - dx[4]),
        (dz[2] - dy[1]) + (dx[0] + 2.0 * dx[3]),
    )
    linear = a_zero * (gamma_bulk / 3.0 - 1.0) - stiffness * (4.0 * pitch_wave**2 + 6.0)
    factor = linear - bulk * square
    return [
        bulk * product[k]
        + factor * q[k]
        + stiffness * around[k]
        - (stiffness * pitch_wave) * chiral[k]
        for k in range(5)
    ]


def gather_stencil(load):
    q, around, dx, dy, dz = [], [], [], [], []
    for k in range(5):
        center, ahead, behind = load(k)
        total, (a, b, c) = stencil(center, ahead, behind)
        q.append(center)
        around.append(total)
        dx.append(a)
        dy.append(b)
        dz.append(c)
    return q, around, dx, dy, dz


def updated(q, field, dx, dy, dz, velocity):
    hx, hy, hz = (0.5 * v for v in velocity)
    return [
        q[k] + mobility_dt * field[k] - (hx * dx[k] + hy * dy[k] + hz * dz[k]) for k in range(5)
    ]


def force_of(field, dx, dy, dz):
    first = field[0] + 0.5 * field[3]
    second = field[3] + 0.5 * field[0]
    return [
        first * d[0] + second * d[3] + field[1] * d[1] + field[2] * d[2] + field[4] * d[4]
        for d in (dx, dy, dz)
    ]


def collide(which, load, density, velocity, force):
    half = 0.5 / density
    u = [velocity[a] + force[a] * half for a in range(3)]
    speed = u[0] * u[0] + u[1] * u[1] + u[2] * u[2]
    along = u[0] * force[0] + u[1] * force[1] + u[2] * force[2]
    keep = 1.0 - 0.5 * tau_rate
    base = (tau_rate * density) * (1.0 - 1.5 * speed) - (3.0 * keep) * along
    odd = [(3.0 * tau_rate) * density * u[a] + (3.0 * keep) * force[a] for a in range(3)]
    even = [(4.5 * tau_rate) * density * u[a] + (9.0 * keep) * force[a] for a in range(3)]

    def dot(c, vector):
        total = None
        for a in range(3):
            if c[a]:
                term = vector[a]
                if total is None:
                    total = term if c[a] > 0 else -term
                else:
                    total = total + term if c[a] > 0 else total - term
        return total

    rest = 1.0 - tau_rate
    done = set()
    for i in which:
        if i in done:
            continue
        if i == 0:
            yield 0, rest * load(0) + (1.0 / 3.0) * base
            continue
        low = i if i % 2 else i - 1
        c = [int(v) for v in lattice[low]]
        weight = 1.0 / 18.0 if low < 7 else 1.0 / 36.0
        first = weight * (base + dot(c, u) * dot(c, even))
        second = weight * dot(c, odd)
        for j, sign in ((low, 1), (low + 1, -1)):
            if j in which:
                done.add(j)
                yield j, rest * load(j) + (first + second if sign > 0 else first - second)


def moments_kernel(pop_ref, order_ref, base_ref, first_ref, second_ref):
    def row(x, carry):
        p = [pop_ref[i, pl.ds(x, 8, stride=8), :] for i in range(19)]
        density = p[0]
        for i in range(1, 19):
            density = density + p[i]
        inverse = 1.0 / density
        for a in range(3):
            plus = [p[i] for i in range(19) if lattice[i][a] == 1]
            minus = [p[i] for i in range(19) if lattice[i][a] == -1]
            momentum = functools.reduce(lambda s, t: s + t, plus) - functools.reduce(
                lambda s, t: s + t, minus
            )
            base_ref[5 + a, x] = momentum * inverse
        base_ref[8, x] = density
        for k in range(5):
            base_ref[k, x] = order_ref[k, pl.ds(x, 8, stride=8), :]
        return carry

    lax.fori_loop(0, 8, row, 0)
    even = is_even("row")
    for out, high in ((first_ref, even), (second_ref, jnp.logical_not(even))):

        @pl.when(high)
        def _():
            for k in range(5):
                out[4 * k : 4 * k + 4] = base_ref[k, 4:8]
            for a in range(3):
                out[VEL + 3 * a : VEL + 3 * a + 3] = base_ref[5 + a, 5:8]
            out[DEN] = base_ref[8, 7]
            for j, i in enumerate(x_up):
                out[POP + j] = pop_ref[i, pl.ds(7, 8, stride=8), :]

        @pl.when(jnp.logical_not(high))
        def _():
            for k in range(5):
                out[4 * k : 4 * k + 4] = base_ref[k, 0:4]
            for a in range(3):
                out[VEL + 3 * a : VEL + 3 * a + 3] = base_ref[5 + a, 0:3]
            out[DEN] = base_ref[8, 0]
            for j, i in enumerate(x_down):
                out[POP + j] = pop_ref[i, pl.ds(0, 8, stride=8), :]


def placed(value, row, into):
    q = row % 8
    lane = lanes()
    mask = jnp.logical_and(lane >= SLOTS * q, lane < SLOTS * q + SLOTS)
    return jnp.where(mask, roll_y(value, 8 + SLOTS * q), into)


def own_edges_kernel(base_ref, pop_ref, edge_ref):
    def pack(load, fill, field):
        low = high = jnp.full((8, 128), fill, f32)
        for x in range(4):
            low = placed(load(x), x + 4, low)
            high = placed(load(x + 4), x + 8, high)
        edge_ref[field, 0] = low
        edge_ref[field, 1] = high

    def base_field(f, carry):
        pack(lambda x: base_ref[f, x], 0.0, f)
        return carry

    def pop_field(i, carry):
        pack(lambda x: pop_ref[i, pl.ds(x, 8, stride=8), :], 0.0, 9 + i)
        return carry

    lax.fori_loop(0, 8, base_field, 0)
    pack(lambda x: base_ref[8, x], 1.0, 8)
    lax.fori_loop(0, 19, pop_field, 0)


def column_message_kernel(own_ref, recv_a, recv_b, edge_ref, first_ref, second_ref):
    even = is_even("row")
    slot = slots()

    def halo(j):
        a, b = recv_a[j], recv_b[j]
        return jnp.where(even, b, a), jnp.where(even, a, b)

    def widen(field, rows):
        low, high = own_ref[field, 0], own_ref[field, 1]
        for j_low, j_high, row_low, row_high in rows:
            if j_low == j_high:
                below, above = halo(j_low)
                low, high = placed(below, row_low, low), placed(above, row_high, high)
        edge_ref[field, 0] = low
        edge_ref[field, 1] = high

    for k in range(5):
        widen(k, [(4 * k + r, 4 * k + r, r, 12 + r) for r in range(4)])
    for a in range(3):
        widen(5 + a, [(VEL + 3 * a + r, VEL + 3 * a + r, 1 + r, 12 + r) for r in range(3)])
    widen(8, [(DEN, DEN, 3, 12)])
    for i in range(19):
        low, high = own_ref[9 + i, 0], own_ref[9 + i, 1]
        if i in x_up:
            low = placed(halo(POP + x_up.index(i))[0], 3, low)
        if i in x_down:
            high = placed(halo(POP + x_down.index(i))[1], 12, high)
        edge_ref[9 + i, 0] = low
        edge_ref[9 + i, 1] = high

    col_even = is_even("col")
    for h in range(2):
        for g, parts in enumerate(((0, 1, 2, 3), (4, 5, 6, 7))):
            to_left = to_right = jnp.zeros((8, 128), f32)
            for u, f in enumerate(parts):
                value = edge_ref[f, h]
                mask = jnp.logical_and(slot >= 4 * u, slot < 4 * u + 4)
                to_left = jnp.where(mask, roll_y(value, 4 * u - 8), to_left)
                to_right = jnp.where(mask, roll_y(value, 4 * u - 4), to_right)
            first_ref[2 * g + h] = jnp.where(col_even, to_right, to_left)
            second_ref[2 * g + h] = jnp.where(col_even, to_left, to_right)
        to_left = to_right = jnp.zeros((8, 128), f32)
        for s in range(6):
            left_field = 8 if s == 0 else 9 + y_down[s - 1]
            right_field = 8 if s == 0 else 9 + y_up[s - 1]
            to_left = jnp.where(slot == s, roll_y(edge_ref[left_field, h], s - 8), to_left)
            to_right = jnp.where(slot == s, roll_y(edge_ref[right_field, h], s - 7), to_right)
        first_ref[4 + h] = jnp.where(col_even, to_right, to_left)
        second_ref[4 + h] = jnp.where(col_even, to_left, to_right)


def main_kernel(
    base_ref, recv_a, recv_b, pop_ref, moved_ref, order_ref, q_zero, q_one, q_two, vel, den
):
    even = is_even("row")

    def halo(j):
        a, b = recv_a[j], recv_b[j]
        return jnp.where(even, b, a), jnp.where(even, a, b)

    for k in range(5):
        q_zero[k, 4:12] = base_ref[k]
        for r in range(4):
            q_zero[k, r], q_zero[k, 12 + r] = halo(4 * k + r)
    for a in range(3):
        vel[a, 3:11] = base_ref[5 + a]
        for r in range(3):
            vel[a, r], vel[a, 11 + r] = halo(VEL + 3 * a + r)
    den[0], den[9] = halo(DEN)

    def relax(source, target):
        def row(r, carry):
            q, around, dx, dy, dz = gather_stencil(
                lambda k: (source[k, r], source[k, r + 1], source[k, r - 1])
            )
            field = molecular_field(q, around, dx, dy, dz)
            new = updated(q, field, dx, dy, dz, [vel[a, r - 1] for a in range(3)])
            for k in range(5):
                target[k, r] = new[k]
            return carry

        return row

    lax.fori_loop(1, 15, relax(q_zero, q_one), 0)
    lax.fori_loop(2, 14, relax(q_one, q_two), 0)

    def last(x):
        q, around, dx, dy, dz = gather_stencil(
            lambda k: (q_two[k, x + 4], q_two[k, x + 5], q_two[k, x + 3])
        )
        field = molecular_field(q, around, dx, dy, dz)
        velocity = [vel[a, x + 3] for a in range(3)]
        return q, field, dx, dy, dz, velocity, force_of(field, dx, dy, dz)

    def stream(i, value, row):
        a, b, c = (int(v) for v in lattice[i])
        moved_ref[i, row + a] = roll_y(roll_z(value, c), b)

    def own_row(x, carry):
        q, field, dx, dy, dz, velocity, force = last(x)
        new = updated(q, field, dx, dy, dz, velocity)
        for k in range(5):
            order_ref[k, x] = new[k]
        for i, value in collide(
            range(19),
            lambda i: pop_ref[i, pl.ds(x, 8, stride=8), :],
            base_ref[8, x],
            velocity,
            force,
        ):
            stream(i, value, x + 1)
        return carry

    lax.fori_loop(0, 8, own_row, 0)
    for x, which, side in ((-1, x_up, 0), (8, x_down, 1)):
        _, _, _, _, _, velocity, force = last(x)
        for i, value in collide(
            which,
            lambda i, which=which, side=side: halo(POP + which.index(i))[side],
            den[9 * side],
            velocity,
            force,
        ):
            stream(i, value, x + 1)


def edge_kernel(
    edge_ref, recv_a, recv_b, moved_ref, order_ref, out_pop, out_order, strip, q_one, q_two, done
):
    even = is_even("col")
    slot, lane = slots(), lanes()

    def columns(j):
        a, b = recv_a[j], recv_b[j]
        return jnp.where(even, b, a), jnp.where(even, a, b)

    for h in range(2):
        for f in range(8):
            from_left, from_right = columns(2 * (f // 4) + h)
            u = f % 4
            own = edge_ref[f, h]
            strip[f, h] = jnp.where(slot < 4, roll_y(from_left, -4 * u), roll_y(own, -4))
            strip[f, 2 + h] = jnp.where(slot < 8, own, roll_y(from_right, 8 - 4 * u))
        from_left, from_right = columns(4 + h)
        for f in range(8, FIELDS):
            own = edge_ref[f, h]
            left, right = roll_y(own, -4), own
            if f == 8 or f - 9 in y_up:
                s = 0 if f == 8 else 1 + y_up.index(f - 9)
                left = jnp.where(slot == 3, roll_y(from_left, 3 - s), left)
            if f == 8 or f - 9 in y_down:
                s = 0 if f == 8 else 1 + y_down.index(f - 9)
                right = jnp.where(slot == 8, roll_y(from_right, 8 - s), right)
            strip[f, h] = left
            strip[f, 2 + h] = right

    def neighbours(source, unit):
        other = jnp.bitwise_xor(unit, 1)

        def load(k):
            me, that = source[k, unit], source[k, other]
            ahead = jnp.where(lane >= 112, roll_y(that, -16), roll_y(me, -16))
            behind = jnp.where(lane < 16, roll_y(that, 16), roll_y(me, 16))
            return me, ahead, behind

        return load

    def relax(source, target):
        def step(unit, carry):
            q, around, dx, dy, dz = gather_stencil(neighbours(source, unit))
            field = molecular_field(q, around, dx, dy, dz)
            new = updated(q, field, dx, dy, dz, [strip[5 + a, unit] for a in range(3)])
            for k in range(5):
                target[k, unit] = new[k]
            return carry

        return step

    lax.fori_loop(0, 4, relax(strip, q_one), 0)
    lax.fori_loop(0, 4, relax(q_one, q_two), 0)

    def last(unit, carry):
        q, around, dx, dy, dz = gather_stencil(neighbours(q_two, unit))
        field = molecular_field(q, around, dx, dy, dz)
        velocity = [strip[5 + a, unit] for a in range(3)]
        new = updated(q, field, dx, dy, dz, velocity)
        force = force_of(field, dx, dy, dz)
        for k in range(5):
            done[19 + k, unit] = new[k]
        for i, value in collide(
            range(19), lambda i: strip[9 + i, unit], strip[8, unit], velocity, force
        ):
            _, b, c = (int(v) for v in lattice[i])
            done[i, unit] = roll_y(roll_z(value, c), b)
        return carry

    lax.fori_loop(0, 4, last, 0)

    edge_lane = jnp.logical_or(lane < 4, lane >= 124)

    def merged(field, shift, x, value):
        row = x + 4 - shift
        h, q = row // 8, row % 8
        pair = halves[field][h]
        return jnp.where(edge_lane, roll_y(pair, -(SLOTS * q + 8)), value)

    halves = {}
    for f in range(24):
        halves[f] = [
            jnp.where(slot < 8, done[f, 2 + h], roll_y(done[f, h], 4)) for h in range(2)
        ]
        shift = int(lattice[f][0]) if f < 19 else 0
        for x in range(8):
            if f < 19:
                out_pop[f, pl.ds(x, 8, stride=8), :] = merged(f, shift, x, moved_ref[f, x + 1])
            else:
                out_order[f - 19, pl.ds(x, 8, stride=8), :] = merged(
                    f, shift, x, order_ref[f - 19, x]
                )


def call(kernel, out_shapes, scratch, flops, *args):
    whole = pl.BlockSpec(memory_space=pltpu.VMEM)
    return pl.pallas_call(
        kernel,
        out_shape=[jax.ShapeDtypeStruct(s, f32) for s in out_shapes],
        in_specs=[whole] * len(args),
        out_specs=[whole] * len(out_shapes),
        scratch_shapes=[pltpu.VMEM(s, f32) for s in scratch],
        cost_estimate=pl.CostEstimate(
            flops=flops,
            bytes_accessed=4 * sum(math.prod(s) for s in out_shapes) + sum(4 * a.size for a in args),
            transcendentals=0,
        ),
        compiler_params=pltpu.CompilerParams(vmem_limit_bytes=12 * 1024 * 1024),
    )(*args)


def swap(size, first):
    return [
        (i, (i + 1) % size if i % 2 == first else (i - 1) % size) for i in range(size)
    ]


def body(rows, cols, populations, order_tensor):
    pops = populations.reshape(19, 64, 128)
    order = order_tensor.reshape(5, 64, 128)
    face = (FACE, 8, 128)
    base, first, second = call(
        moments_kernel, [(9, 8, 8, 128), face, face], [], 2_000_000, pops, order
    )
    recv_a = lax.ppermute(first, "row", swap(rows, 0))
    recv_b = lax.ppermute(second, "row", swap(rows, 1))
    own_edges = call(
        own_edges_kernel, [(FIELDS, 2, 8, 128)], [], 2_000_000, base, pops
    )[0]
    side = (6, 8, 128)
    edges, left, right = call(
        column_message_kernel,
        [(FIELDS, 2, 8, 128), side, side],
        [],
        1_000_000,
        own_edges,
        recv_a,
        recv_b,
    )
    col_a = lax.ppermute(left, "col", swap(cols, 0))
    col_b = lax.ppermute(right, "col", swap(cols, 1))
    moved, relaxed = call(
        main_kernel,
        [(19, 10, 8, 128), (5, 8, 8, 128)],
        [(5, 16, 8, 128)] * 3 + [(3, 14, 8, 128), (10, 8, 128)],
        20_000_000,
        base,
        recv_a,
        recv_b,
        pops,
    )
    new_pops, new_order = call(
        edge_kernel,
        [(19, 64, 128), (5, 64, 128)],
        [(FIELDS, 4, 8, 128), (5, 4, 8, 128), (5, 4, 8, 128), (24, 4, 8, 128)],
        8_000_000,
        edges,
        col_a,
        col_b,
        moved,
        relaxed,
    )
    return new_pops.reshape(populations.shape), new_order.reshape(order_tensor.shape)


def solution(mesh):
    spec = P(None, None, "row", "col")
    return jax.shard_map(
        functools.partial(body, mesh.shape["row"], mesh.shape["col"]),
        mesh=mesh,
        in_specs=(spec, spec),
        out_specs=(spec, spec),
        check_vma=False,
    )
```

time: 211 us -> 47.5 us (0.23)
  the two profiles are of different devices: /device:TPU:6 before, /device:TPU:32 now
where the time goes in v1:
time: 47.5 us; the launch traced here: 47.2 us
  starting transfers between devices  32.2 us (68%)
  Pallas kernels  10.4 us (22%)
  waiting for transfers between devices  2.01 us (4%)
  local copies, waits for them, and re-layouts  1.99 us (4%)
  between operations  0.7 us (1%)
    ppermute x1, starting transfers between devices, body(): col_b = lax.ppermute(right, 'col', swap(cols, 1))  11.4 us
    ppermute x1, starting transfers between devices, body(): col_a = lax.ppermute(left, 'col', swap(cols, 0))  10.9 us
    pallas_call x5, Pallas kernels, call(): pl.pallas_call(kernel, out_shape=[jax.ShapeDtypeStruct(s, f32) for s in o...  10.4 us
    ppermute x1, starting transfers between devices, body(): recv_b = lax.ppermute(second, 'row', swap(rows, 1))  7.89 us
    ppermute x1, waiting for transfers between devices, body(): recv_b = lax.ppermute(second, 'row', swap(rows, 1))  2 us
    unnamed x6, local copies, waits for them, and re-layouts  1.99 us
    ppermute x1, starting transfers between devices, body(): recv_a = lax.ppermute(first, 'row', swap(rows, 0))  1.92 us
  transfers between devices with their start and end apart: 4, of which 1 were waited for; matrix products, arithmetic and copies ran while one was open for 0% of the time, Pallas kernels for 13%

profile of v1, /device:TPU:32, one launch (start us, length us, event | category | flops | bytes accessed | tf_op | source)
XLA Modules:
  0.0 47.2 jit_solution(8760290798391464348)
XLA Ops:
  0.6 0.0 copy-start
  0.6 1.1 %copy-done = f32[19,8,8,128]{3,2,1,0:T(8,128)S(1)} copy-done((f32[19,8,8,128]{3,2,1,0:T(8,128)S(1)}, f32[19,8,8,128]{3,2,1,0:T(8,128)}, u32[]{:S(2)}) %copy-start) | copy-done | bytes 622616
  1.7 0.0 copy-start.2
  1.7 0.9 %copy-done.2 = f32[5,8,8,128]{3,2,1,0:T(8,128)S(1)} copy-done((f32[5,8,8,128]{3,2,1,0:T(8,128)S(1)}, f32[5,8,8,128]{3,2,1,0:T(8,128)}, u32[]{:S(2)}) %copy-start.2) | copy-done | bytes 163864
  2.6 0.3 shard_map.41
  2.9 1.9 %collective-permute-start = (f32[35,8,128]{2,1,0:T(8,128)S(1)}, f32[35,8,128]{2,1,0:T(8,128)S(1)}, u32[]{:S(2)}, u32[]{:S(2)}) collective-permute-start(f32[35,8,128]{2,1,0:T(8,128)S(1)} %get-tuple-element.13), channel_id=1, source_target_pairs={{0,16},{16,0},{32,48},{48,32},{64,80},{80,64},{96,112},{112,96},{1... | collective-permute-start | bytes 430088 | tf_op jit(solution)/shard_map/ppermute | solution.py:508
  4.9 7.9 %collective-permute-start.1 = (f32[35,8,128]{2,1,0:T(8,128)S(1)}, f32[35,8,128]{2,1,0:T(8,128)S(1)}, u32[]{:S(2)}, u32[]{:S(2)}) collective-permute-start(f32[35,8,128]{2,1,0:T(8,128)S(1)} %get-tuple-element.14), channel_id=1, source_target_pairs={{0,1008},{16,32},{32,16},{48,64},{64,48},{80,96},{96,80},{112,128}... | collective-permute-start | bytes 430088 | tf_op jit(solution)/shard_map/ppermute | solution.py:509
  12.8 0.0 copy-start.1
  12.8 2.1 %shard_map.42.own_ref = f32[28,2,8,128]{3,2,1,0:T(8,128)S(1)} custom-call(f32[9,8,8,128]{3,2,1,0:T(8,128)S(1)} %get-tuple-element.12.base_ref, f32[19,64,128]{2,1,0:T(8,128)S(1)} %bitcast.5), custom_call_target="tpu_custom_call" | custom-call | flops 2000000 | bytes 1146880 | tf_op jit(solution)/shard_map/pallas_call | solution.py:480
  14.9 0.0 collective-permute-done.recv_a
  14.9 2.0 %collective-permute-done.1.recv_b = f32[35,8,128]{2,1,0:T(8,128)S(1)} collective-permute-done((f32[35,8,128]{2,1,0:T(8,128)S(1)}, f32[35,8,128]{2,1,0:T(8,128)S(1)}, u32[]{:S(2)}, u32[]{:S(2)}) %collective-permute-start.1) | collective-permute-done | bytes 143392 | tf_op jit(solution)/shard_map/ppermute | solution.py:509
  16.9 0.2 shard_map.43
  17.1 10.9 %collective-permute-start.2 = (f32[6,8,128]{2,1,0:T(8,128)S(1)}, f32[6,8,128]{2,1,0:T(8,128)S(1)}, u32[]{:S(2)}, u32[]{:S(2)}) collective-permute-start(f32[6,8,128]{2,1,0:T(8,128)S(1)} %get-tuple-element.16), channel_id=1, source_target_pairs={{0,1},{1,0},{2,3},{3,2},{4,5},{5,4},{6,7},{7,6},{8,9},{9,8},{10,11... | collective-permute-start | bytes 73736 | tf_op jit(solution)/shard_map/ppermute | solution.py:523
  28.1 11.4 %collective-permute-start.3 = (f32[6,8,128]{2,1,0:T(8,128)S(1)}, f32[6,8,128]{2,1,0:T(8,128)S(1)}, u32[]{:S(2)}, u32[]{:S(2)}) collective-permute-start(f32[6,8,128]{2,1,0:T(8,128)S(1)} %get-tuple-element.17), channel_id=1, source_target_pairs={{0,15},{1,2},{2,1},{3,4},{4,3},{5,6},{6,5},{7,8},{8,7},{9,10},{10,... | collective-permute-start | bytes 73736 | tf_op jit(solution)/shard_map/ppermute | solution.py:524
  39.5 0.0 copy-done.1
  39.5 3.9 %shard_map.44 = (f32[19,10,8,128]{3,2,1,0:T(8,128)S(1)}, f32[5,8,8,128]{3,2,1,0:T(8,128)S(1)}) custom-call(f32[9,8,8,128]{3,2,1,0:T(8,128)S(1)} %get-tuple-element.12.base_ref, f32[35,8,128]{2,1,0:T(8,128)S(1)} %collective-permute-done.recv_a, f32[35,8,128]{2,1,0:T(8,128)S(1)} %collective-permute-done.1.recv_b, f32[19,64,128]{2,1,0:T(8,128)S(1)} %bitcast.6), custom_call_target="tpu_custom_call" | custom-call | flops 20000000 | bytes 2146304 | tf_op jit(solution)/shard_map/pallas_call | solution.py:480
  43.4 0.0 collective-permute-done.2.recv_a
  43.4 0.0 collective-permute-done.3.recv_b
  43.4 3.8 %shard_map.45 = (f32[19,64,128]{2,1,0:T(8,128)}, f32[5,64,128]{2,1,0:T(8,128)}) custom-call(f32[28,2,8,128]{3,2,1,0:T(8,128)S(1)} %get-tuple-element.15.edge_ref, f32[6,8,128]{2,1,0:T(8,128)S(1)} %collective-permute-done.2.recv_a, f32[6,8,128]{2,1,0:T(8,128)S(1)} %collective-permute-done.3.recv_b, f32[19,10,8,128]{3,2,1,0:T(8,128)S(1)} %get-tuple-element.18.moved_ref, ...), custom_call_target="tpu_custom_call" | custom-call | flops 8000000 | bytes 2007040 | tf_op jit(solution)/shard_map/pallas_call | solution.py:480
Async XLA Ops:
  0.6 1.1 %copy-start = (f32[19,8,8,128]{3,2,1,0:T(8,128)S(1)}, f32[19,8,8,128]{3,2,1,0:T(8,128)}, u32[]{:S(2)}) copy-start(f32[19,8,8,128]{3,2,1,0:T(8,128)} %param.2) | copy-start | bytes 1867780
  1.7 0.9 %copy-start.2 = (f32[5,8,8,128]{3,2,1,0:T(8,128)S(1)}, f32[5,8,8,128]{3,2,1,0:T(8,128)}, u32[]{:S(2)}) copy-start(f32[5,8,8,128]{3,2,1,0:T(8,128)} %param.3) | copy-start | bytes 491524
  2.9 11.9 %collective-permute-start = (f32[35,8,128]{2,1,0:T(8,128)S(1)}, f32[35,8,128]{2,1,0:T(8,128)S(1)}, u32[]{:S(2)}, u32[]{:S(2)}) collective-permute-start(f32[35,8,128]{2,1,0:T(8,128)S(1)} %get-tuple-element.13), channel_id=1, source_target_pairs={{0,16},{16,0},{32,48},{48,32},{64,80},{80,64},{96,112},{112,96},{1... | collective-permute-start | bytes 430088 | tf_op jit(solution)/shard_map/ppermute | solution.py:508
  4.9 12.0 %collective-permute-start.1 = (f32[35,8,128]{2,1,0:T(8,128)S(1)}, f32[35,8,128]{2,1,0:T(8,128)S(1)}, u32[]{:S(2)}, u32[]{:S(2)}) collective-permute-start(f32[35,8,128]{2,1,0:T(8,128)S(1)} %get-tuple-element.14), channel_id=1, source_target_pairs={{0,1008},{16,32},{32,16},{48,64},{64,48},{80,96},{96,80},{112,128}... | collective-permute-start | bytes 430088 | tf_op jit(solution)/shard_map/ppermute | solution.py:509
  12.8 26.7 %copy-start.1 = (f32[19,8,8,128]{3,2,1,0:T(8,128)S(1)}, f32[19,8,8,128]{3,2,1,0:T(8,128)}, u32[]{:S(2)}) copy-start(f32[19,8,8,128]{3,2,1,0:T(8,128)} %param.2) | copy-start | bytes 1867780
  17.1 26.3 %collective-permute-start.2 = (f32[6,8,128]{2,1,0:T(8,128)S(1)}, f32[6,8,128]{2,1,0:T(8,128)S(1)}, u32[]{:S(2)}, u32[]{:S(2)}) collective-permute-start(f32[6,8,128]{2,1,0:T(8,128)S(1)} %get-tuple-element.16), channel_id=1, source_target_pairs={{0,1},{1,0},{2,3},{3,2},{4,5},{5,4},{6,7},{7,6},{8,9},{9,8},{10,11... | collective-permute-start | bytes 73736 | tf_op jit(solution)/shard_map/ppermute | solution.py:523
  28.1 15.4 %collective-permute-start.3 = (f32[6,8,128]{2,1,0:T(8,128)S(1)}, f32[6,8,128]{2,1,0:T(8,128)S(1)}, u32[]{:S(2)}, u32[]{:S(2)}) collective-permute-start(f32[6,8,128]{2,1,0:T(8,128)S(1)} %get-tuple-element.17), channel_id=1, source_target_pairs={{0,15},{1,2},{2,1},{3,4},{4,3},{5,6},{6,5},{7,8},{8,7},{9,10},{10,... | collective-permute-start | bytes 73736 | tf_op jit(solution)/shard_map/ppermute | solution.py:524

commit v2 on v1

--- a/solution.py
+++ b/solution.py
@@ -46,7 +46,10 @@
 
 VEL, DEN, POP, FACE = 20, 29, 30, 35
 SLOTS = 16
-FIELDS = 28
+near = sorted(y_up + y_down)
+far = [i for i in range(19) if i not in near]
+NEAR, FAR = 9 + len(near), len(far)
+MOVE_UNROLL, RELAX_UNROLL, EDGE_UNROLL = 4, 7, 2
 f32 = jnp.float32
 
 
@@ -180,7 +183,18 @@
                 yield j, rest * load(j) + (first + second if sign > 0 else first - second)
 
 
-def moments_kernel(pop_ref, order_ref, base_ref, first_ref, second_ref):
+def moments_kernel(
+    pop_hbm, order_hbm, base_ref, first_ref, second_ref, pop_ref, order_ref, sems
+):
+    copies = [
+        pltpu.make_async_copy(order_hbm, order_ref, sems.at[0]),
+        pltpu.make_async_copy(pop_hbm, pop_ref, sems.at[1]),
+    ]
+    for copy in copies:
+        copy.start()
+    for copy in copies:
+        copy.wait()
+
     def row(x, carry):
         p = [pop_ref[i, pl.ds(x, 8, stride=8), :] for i in range(19)]
         density = p[0]
@@ -240,17 +254,10 @@
         edge_ref[field, 0] = low
         edge_ref[field, 1] = high
 
-    def base_field(f, carry):
-        pack(lambda x: base_ref[f, x], 0.0, f)
-        return carry
-
-    def pop_field(i, carry):
-        pack(lambda x: pop_ref[i, pl.ds(x, 8, stride=8), :], 0.0, 9 + i)
-        return carry
-
-    lax.fori_loop(0, 8, base_field, 0)
-    pack(lambda x: base_ref[8, x], 1.0, 8)
-    lax.fori_loop(0, 19, pop_field, 0)
+    for f in range(9):
+        pack(lambda x, f=f: base_ref[f, x], 1.0 if f == 8 else 0.0, f)
+    for n, i in enumerate(near):
+        pack(lambda x, i=i: pop_ref[i, pl.ds(x, 8, stride=8), :], 0.0, 9 + n)
 
 
 def column_message_kernel(own_ref, recv_a, recv_b, edge_ref, first_ref, second_ref):
@@ -263,26 +270,25 @@
 
     def widen(field, rows):
         low, high = own_ref[field, 0], own_ref[field, 1]
-        for j_low, j_high, row_low, row_high in rows:
-            if j_low == j_high:
-                below, above = halo(j_low)
-                low, high = placed(below, row_low, low), placed(above, row_high, high)
+        for j, row_low, row_high in rows:
+            below, above = halo(j)
+            low, high = placed(below, row_low, low), placed(above, row_high, high)
         edge_ref[field, 0] = low
         edge_ref[field, 1] = high
 
     for k in range(5):
-        widen(k, [(4 * k + r, 4 * k + r, r, 12 + r) for r in range(4)])
+        widen(k, [(4 * k + r, r, 12 + r) for r in range(4)])
     for a in range(3):
-        widen(5 + a, [(VEL + 3 * a + r, VEL + 3 * a + r, 1 + r, 12 + r) for r in range(3)])
-    widen(8, [(DEN, DEN, 3, 12)])
-    for i in range(19):
-        low, high = own_ref[9 + i, 0], own_ref[9 + i, 1]
+        widen(5 + a, [(VEL + 3 * a + r, 1 + r, 12 + r) for r in range(3)])
+    widen(8, [(DEN, 3, 12)])
+    for n, i in enumerate(near):
+        low, high = own_ref[9 + n, 0], own_ref[9 + n, 1]
         if i in x_up:
             low = placed(halo(POP + x_up.index(i))[0], 3, low)
         if i in x_down:
             high = placed(halo(POP + x_down.index(i))[1], 12, high)
-        edge_ref[9 + i, 0] = low
-        edge_ref[9 + i, 1] = high
+        edge_ref[9 + n, 0] = low
+        edge_ref[9 + n, 1] = high
 
     col_even = is_even("col")
     for h in range(2):
@@ -297,8 +303,8 @@
             second_ref[2 * g + h] = jnp.where(col_even, to_left, to_right)
         to_left = to_right = jnp.zeros((8, 128), f32)
         for s in range(6):
-            left_field = 8 if s == 0 else 9 + y_down[s - 1]
-            right_field = 8 if s == 0 else 9 + y_up[s - 1]
+            left_field = 8 if s == 0 else 9 + near.index(y_down[s - 1])
+            right_field = 8 if s == 0 else 9 + near.index(y_up[s - 1])
             to_left = jnp.where(slot == s, roll_y(edge_ref[left_field, h], s - 8), to_left)
             to_right = jnp.where(slot == s, roll_y(edge_ref[right_field, h], s - 7), to_right)
         first_ref[4 + h] = jnp.where(col_even, to_right, to_left)
@@ -306,7 +312,18 @@
 
 
 def main_kernel(
-    base_ref, recv_a, recv_b, pop_ref, moved_ref, order_ref, q_zero, q_one, q_two, vel, den
+    base_ref,
+    recv_a,
+    recv_b,
+    pop_ref,
+    moved_ref,
+    order_ref,
+    far_ref,
+    q_zero,
+    q_one,
+    q_two,
+    vel,
+    den,
 ):
     even = is_even("row")
 
@@ -337,8 +354,8 @@
 
         return row
 
-    lax.fori_loop(1, 15, relax(q_zero, q_one), 0)
-    lax.fori_loop(2, 14, relax(q_one, q_two), 0)
+    lax.fori_loop(1, 15, relax(q_zero, q_one), 0, unroll=RELAX_UNROLL)
+    lax.fori_loop(2, 14, relax(q_one, q_two), 0, unroll=6)
 
     def last(x):
         q, around, dx, dy, dz = gather_stencil(
@@ -367,7 +384,20 @@
             stream(i, value, x + 1)
         return carry
 
-    lax.fori_loop(0, 8, own_row, 0)
+    lax.fori_loop(0, 8, own_row, 0, unroll=MOVE_UNROLL)
+
+    for n, i in enumerate(far):
+        low = high = jnp.zeros((8, 128), f32)
+        for x in range(4):
+            low = placed(pop_ref[i, pl.ds(x, 8, stride=8), :], x + 4, low)
+            high = placed(pop_ref[i, pl.ds(x + 4, 8, stride=8), :], x + 8, high)
+        if i in x_up:
+            low = placed(halo(POP + x_up.index(i))[0], 3, low)
+        if i in x_down:
+            high = placed(halo(POP + x_down.index(i))[1], 12, high)
+        far_ref[n, 0] = low
+        far_ref[n, 1] = high
+
     for x, which, side in ((-1, x_up, 0), (8, x_down, 1)):
         _, _, _, _, _, velocity, force = last(x)
         for i, value in collide(
@@ -381,7 +411,18 @@
 
 
 def edge_kernel(
-    edge_ref, recv_a, recv_b, moved_ref, order_ref, out_pop, out_order, strip, q_one, q_two, done
+    edge_ref,
+    far_ref,
+    recv_a,
+    recv_b,
+    moved_ref,
+    order_ref,
+    out_pop,
+    out_order,
+    strip,
+    q_one,
+    q_two,
+    done,
 ):
     even = is_even("col")
     slot, lane = slots(), lanes()
@@ -398,20 +439,26 @@
             strip[f, h] = jnp.where(slot < 4, roll_y(from_left, -4 * u), roll_y(own, -4))
             strip[f, 2 + h] = jnp.where(slot < 8, own, roll_y(from_right, 8 - 4 * u))
         from_left, from_right = columns(4 + h)
-        for f in range(8, FIELDS):
-            own = edge_ref[f, h]
+        for f in range(8, 28):
+            i = f - 9
+            if f == 8:
+                own = edge_ref[8, h]
+            elif i in near:
+                own = edge_ref[9 + near.index(i), h]
+            else:
+                own = far_ref[far.index(i), h]
             left, right = roll_y(own, -4), own
-            if f == 8 or f - 9 in y_up:
-                s = 0 if f == 8 else 1 + y_up.index(f - 9)
+            if f == 8 or i in y_up:
+                s = 0 if f == 8 else 1 + y_up.index(i)
                 left = jnp.where(slot == 3, roll_y(from_left, 3 - s), left)
-            if f == 8 or f - 9 in y_down:
-                s = 0 if f == 8 else 1 + y_down.index(f - 9)
+            if f == 8 or i in y_down:
+                s = 0 if f == 8 else 1 + y_down.index(i)
                 right = jnp.where(slot == 8, roll_y(from_right, 8 - s), right)
             strip[f, h] = left
             strip[f, 2 + h] = right
 
     def neighbours(source, unit):
-        other = jnp.bitwise_xor(unit, 1)
+        other = unit ^ 1
 
         def load(k):
             me, that = source[k, unit], source[k, other]
@@ -432,8 +479,8 @@
 
         return step
 
-    lax.fori_loop(0, 4, relax(strip, q_one), 0)
-    lax.fori_loop(0, 4, relax(q_one, q_two), 0)
+    lax.fori_loop(0, 4, relax(strip, q_one), 0, unroll=EDGE_UNROLL)
+    lax.fori_loop(0, 4, relax(q_one, q_two), 0, unroll=EDGE_UNROLL)
 
     def last(unit, carry):
         q, around, dx, dy, dz = gather_stencil(neighbours(q_two, unit))
@@ -450,7 +497,7 @@
             done[i, unit] = roll_y(roll_z(value, c), b)
         return carry
 
-    lax.fori_loop(0, 4, last, 0)
+    lax.fori_loop(0, 4, last, 0, unroll=EDGE_UNROLL)
 
     edge_lane = jnp.logical_or(lane < 4, lane >= 124)
 
@@ -475,14 +522,15 @@
                 )
 
 
-def call(kernel, out_shapes, scratch, flops, *args):
+def call(kernel, out_shapes, scratch, flops, *args, from_hbm=False):
     whole = pl.BlockSpec(memory_space=pltpu.VMEM)
+    source = pl.BlockSpec(memory_space=pltpu.HBM) if from_hbm else whole
     return pl.pallas_call(
         kernel,
         out_shape=[jax.ShapeDtypeStruct(s, f32) for s in out_shapes],
-        in_specs=[whole] * len(args),
+        in_specs=[source] * len(args),
         out_specs=[whole] * len(out_shapes),
-        scratch_shapes=[pltpu.VMEM(s, f32) for s in scratch],
+        scratch_shapes=[pltpu.VMEM(s, f32) if isinstance(s, tuple) else s for s in scratch],
         cost_estimate=pl.CostEstimate(
             flops=flops,
             bytes_accessed=4 * sum(math.prod(s) for s in out_shapes) + sum(4 * a.size for a in args),
@@ -499,21 +547,22 @@
 
 
 def body(rows, cols, populations, order_tensor):
-    pops = populations.reshape(19, 64, 128)
-    order = order_tensor.reshape(5, 64, 128)
-    face = (FACE, 8, 128)
-    base, first, second = call(
-        moments_kernel, [(9, 8, 8, 128), face, face], [], 2_000_000, pops, order
+    face, side = (FACE, 8, 128), (6, 8, 128)
+    base, first, second, pops = call(
+        moments_kernel,
+        [(9, 8, 8, 128), face, face, (19, 64, 128)],
+        [(5, 64, 128), pltpu.SemaphoreType.DMA((2,))],
+        2_000_000,
+        pltpu.with_memory_space_constraint(populations.reshape(19, 64, 128), pltpu.HBM),
+        pltpu.with_memory_space_constraint(order_tensor.reshape(5, 64, 128), pltpu.HBM),
+        from_hbm=True,
     )
+    recv_b = lax.ppermute(second, "row", swap(rows, 1))
     recv_a = lax.ppermute(first, "row", swap(rows, 0))
-    recv_b = lax.ppermute(second, "row", swap(rows, 1))
-    own_edges = call(
-        own_edges_kernel, [(FIELDS, 2, 8, 128)], [], 2_000_000, base, pops
-    )[0]
-    side = (6, 8, 128)
+    own_edges = call(own_edges_kernel, [(NEAR, 2, 8, 128)], [], 2_000_000, base, pops)[0]
     edges, left, right = call(
         column_message_kernel,
-        [(FIELDS, 2, 8, 128), side, side],
+        [(NEAR, 2, 8, 128), side, side],
         [],
         1_000_000,
         own_edges,
@@ -522,9 +571,9 @@
     )
     col_a = lax.ppermute(left, "col", swap(cols, 0))
     col_b = lax.ppermute(right, "col", swap(cols, 1))
-    moved, relaxed = call(
+    moved, relaxed, far_edges = call(
         main_kernel,
-        [(19, 10, 8, 128), (5, 8, 8, 128)],
+        [(19, 10, 8, 128), (5, 8, 8, 128), (FAR, 2, 8, 128)],
         [(5, 16, 8, 128)] * 3 + [(3, 14, 8, 128), (10, 8, 128)],
         20_000_000,
         base,
@@ -535,9 +584,10 @@
     new_pops, new_order = call(
         edge_kernel,
         [(19, 64, 128), (5, 64, 128)],
-        [(FIELDS, 4, 8, 128), (5, 4, 8, 128), (5, 4, 8, 128), (24, 4, 8, 128)],
+        [(28, 4, 8, 128), (5, 4, 8, 128), (5, 4, 8, 128), (24, 4, 8, 128)],
         8_000_000,
         edges,
+        far_edges,
         col_a,
         col_b,
         moved,

time: 47.5 us -> 44.3 us (0.933)
  the two profiles are of different devices: /device:TPU:32 before, /device:TPU:4 now
where the time goes in v2:
time: 44.3 us; the launch traced here: 44 us
  starting transfers between devices  31.3 us (71%)
  Pallas kernels  6.69 us (15%)
  waiting for transfers between devices  5.32 us (12%)
  between operations  0.69 us (2%)
    ppermute x1, starting transfers between devices, body(): col_a = lax.ppermute(left, 'col', swap(cols, 0))  10.9 us
    ppermute x1, starting transfers between devices, body(): recv_b = lax.ppermute(second, 'row', swap(rows, 1))  10.9 us
    ppermute x1, starting transfers between devices, body(): col_b = lax.ppermute(right, 'col', swap(cols, 1))  7.58 us
    pallas_call x5, Pallas kernels, call(): pl.pallas_call(kernel, out_shape=[jax.ShapeDtypeStruct(s, f32) for s in o...  6.69 us
    ppermute x1, waiting for transfers between devices, body(): recv_b = lax.ppermute(second, 'row', swap(rows, 1))  3.87 us
    ppermute x1, starting transfers between devices, body(): recv_a = lax.ppermute(first, 'row', swap(rows, 0))  1.92 us
    ppermute x1, waiting for transfers between devices, body(): col_b = lax.ppermute(right, 'col', swap(cols, 1))  1.45 us
  transfers between devices with their start and end apart: 4, of which 2 were waited for; matrix products, arithmetic and copies ran while one was open for 0% of the time, Pallas kernels for 4%

profile of v2, /device:TPU:4, one launch (start us, length us, event | category | flops | bytes accessed | tf_op | source)
XLA Modules:
  0.0 44.0 jit_solution(11754791194728884343)
XLA Ops:
  0.6 1.5 %shard_map.41 = (f32[9,8,8,128]{3,2,1,0:T(8,128)S(1)}, f32[35,8,128]{2,1,0:T(8,128)S(1)}, f32[35,8,128]{2,1,0:T(8,128)S(1)}, f32[19,64,128]{2,1,0:T(8,128)S(1)}) custom-call(f32[19,64,128]{2,1,0:T(8,128)} %bitcast.4, f32[5,64,128]{2,1,0:T(8,128)} %bitcast.5), custom_call_target="tpu_custom_call" | custom-call | flops 2000000 | bytes 1990656 | tf_op jit(solution)/shard_map/pallas_call | solution.py:528
  2.1 1.9 %collective-permute-start = (f32[35,8,128]{2,1,0:T(8,128)S(1)}, f32[35,8,128]{2,1,0:T(8,128)S(1)}, u32[]{:S(2)}, u32[]{:S(2)}) collective-permute-start(f32[35,8,128]{2,1,0:T(8,128)S(1)} %get-tuple-element.16), channel_id=1, source_target_pairs={{0,16},{16,0},{32,48},{48,32},{64,80},{80,64},{96,112},{112,96},{1... | collective-permute-start | bytes 430088 | tf_op jit(solution)/shard_map/ppermute | solution.py:561
  4.1 10.9 %collective-permute-start.1 = (f32[35,8,128]{2,1,0:T(8,128)S(1)}, f32[35,8,128]{2,1,0:T(8,128)S(1)}, u32[]{:S(2)}, u32[]{:S(2)}) collective-permute-start(f32[35,8,128]{2,1,0:T(8,128)S(1)} %get-tuple-element.17), channel_id=1, source_target_pairs={{0,1008},{16,32},{32,16},{48,64},{64,48},{80,96},{96,80},{112,128}... | collective-permute-start | bytes 430088 | tf_op jit(solution)/shard_map/ppermute | solution.py:560
  15.0 0.2 shard_map.42.own_ref
  15.2 0.0 collective-permute-done.recv_a
  15.2 3.9 %collective-permute-done.1.recv_b = f32[35,8,128]{2,1,0:T(8,128)S(1)} collective-permute-done((f32[35,8,128]{2,1,0:T(8,128)S(1)}, f32[35,8,128]{2,1,0:T(8,128)S(1)}, u32[]{:S(2)}, u32[]{:S(2)}) %collective-permute-start.1) | collective-permute-done | bytes 143392 | tf_op jit(solution)/shard_map/ppermute | solution.py:560
  19.1 0.2 shard_map.43
  19.3 10.9 %collective-permute-start.2 = (f32[6,8,128]{2,1,0:T(8,128)S(1)}, f32[6,8,128]{2,1,0:T(8,128)S(1)}, u32[]{:S(2)}, u32[]{:S(2)}) collective-permute-start(f32[6,8,128]{2,1,0:T(8,128)S(1)} %get-tuple-element.20), channel_id=1, source_target_pairs={{0,1},{1,0},{2,3},{3,2},{4,5},{5,4},{6,7},{7,6},{8,9},{9,8},{10,11... | collective-permute-start | bytes 73736 | tf_op jit(solution)/shard_map/ppermute | solution.py:572
  30.3 7.6 %collective-permute-start.3 = (f32[6,8,128]{2,1,0:T(8,128)S(1)}, f32[6,8,128]{2,1,0:T(8,128)S(1)}, u32[]{:S(2)}, u32[]{:S(2)}) collective-permute-start(f32[6,8,128]{2,1,0:T(8,128)S(1)} %get-tuple-element.21), channel_id=1, source_target_pairs={{0,15},{1,2},{2,1},{3,4},{4,3},{5,6},{6,5},{7,8},{8,7},{9,10},{10,... | collective-permute-start | bytes 73736 | tf_op jit(solution)/shard_map/ppermute | solution.py:573
  37.8 1.5 %shard_map.44 = (f32[19,10,8,128]{3,2,1,0:T(8,128)S(1)}, f32[5,8,8,128]{3,2,1,0:T(8,128)S(1)}, f32[9,2,8,128]{3,2,1,0:T(8,128)S(1)}) custom-call(f32[9,8,8,128]{3,2,1,0:T(8,128)S(1)} %get-tuple-element.14.base_ref, f32[35,8,128]{2,1,0:T(8,128)S(1)} %collective-permute-done.recv_a, f32[35,8,128]{2,1,0:T(8,128)S(1)} %collective-permute-done.1.recv_b, ...), custom_call_target="tpu_custom_call" | custom-call | flops 20000000 | bytes 2220032 | tf_op jit(solution)/shard_map/pallas_call | solution.py:528
  39.3 0.0 collective-permute-done.2.recv_a
  39.3 1.4 %collective-permute-done.3.recv_b = f32[6,8,128]{2,1,0:T(8,128)S(1)} collective-permute-done((f32[6,8,128]{2,1,0:T(8,128)S(1)}, f32[6,8,128]{2,1,0:T(8,128)S(1)}, u32[]{:S(2)}, u32[]{:S(2)}) %collective-permute-start.3) | collective-permute-done | bytes 24608 | tf_op jit(solution)/shard_map/ppermute | solution.py:573
  40.8 3.2 %shard_map.45 = (f32[19,64,128]{2,1,0:T(8,128)}, f32[5,64,128]{2,1,0:T(8,128)}) custom-call(f32[19,2,8,128]{3,2,1,0:T(8,128)S(1)} %get-tuple-element.18.edge_ref, f32[9,2,8,128]{3,2,1,0:T(8,128)S(1)} %get-tuple-element.19.far_ref, f32[6,8,128]{2,1,0:T(8,128)S(1)} %collective-permute-done.2.recv_a, f32[6,8,128]{2,1,0:T(8,128)S(1)} %collective-permute-done.3.recv_b, ...), custom_call_target="tpu_custom_call" | custom-call | flops 8000000 | bytes 2007040 | tf_op jit(solution)/shard_map/pallas_call | solution.py:528
Async XLA Ops:
  2.1 13.1 %collective-permute-start = (f32[35,8,128]{2,1,0:T(8,128)S(1)}, f32[35,8,128]{2,1,0:T(8,128)S(1)}, u32[]{:S(2)}, u32[]{:S(2)}) collective-permute-start(f32[35,8,128]{2,1,0:T(8,128)S(1)} %get-tuple-element.16), channel_id=1, source_target_pairs={{0,16},{16,0},{32,48},{48,32},{64,80},{80,64},{96,112},{112,96},{1... | collective-permute-start | bytes 430088 | tf_op jit(solution)/shard_map/ppermute | solution.py:561
  4.1 15.0 %collective-permute-start.1 = (f32[35,8,128]{2,1,0:T(8,128)S(1)}, f32[35,8,128]{2,1,0:T(8,128)S(1)}, u32[]{:S(2)}, u32[]{:S(2)}) collective-permute-start(f32[35,8,128]{2,1,0:T(8,128)S(1)} %get-tuple-element.17), channel_id=1, source_target_pairs={{0,1008},{16,32},{32,16},{48,64},{64,48},{80,96},{96,80},{112,128}... | collective-permute-start | bytes 430088 | tf_op jit(solution)/shard_map/ppermute | solution.py:560
  19.3 20.0 %collective-permute-start.2 = (f32[6,8,128]{2,1,0:T(8,128)S(1)}, f32[6,8,128]{2,1,0:T(8,128)S(1)}, u32[]{:S(2)}, u32[]{:S(2)}) collective-permute-start(f32[6,8,128]{2,1,0:T(8,128)S(1)} %get-tuple-element.20), channel_id=1, source_target_pairs={{0,1},{1,0},{2,3},{3,2},{4,5},{5,4},{6,7},{7,6},{8,9},{9,8},{10,11... | collective-permute-start | bytes 73736 | tf_op jit(solution)/shard_map/ppermute | solution.py:572
  30.3 10.5 %collective-permute-start.3 = (f32[6,8,128]{2,1,0:T(8,128)S(1)}, f32[6,8,128]{2,1,0:T(8,128)S(1)}, u32[]{:S(2)}, u32[]{:S(2)}) collective-permute-start(f32[6,8,128]{2,1,0:T(8,128)S(1)} %get-tuple-element.21), channel_id=1, source_target_pairs={{0,15},{1,2},{2,1},{3,4},{4,3},{5,6},{6,5},{7,8},{8,7},{9,10},{10,... | collective-permute-start | bytes 73736 | tf_op jit(solution)/shard_map/ppermute | solution.py:573

commit v3 on v2

--- a/solution.py
+++ b/solution.py
@@ -49,7 +49,7 @@
 near = sorted(y_up + y_down)
 far = [i for i in range(19) if i not in near]
 NEAR, FAR = 9 + len(near), len(far)
-MOVE_UNROLL, RELAX_UNROLL, EDGE_UNROLL = 4, 7, 2
+CHUNKS = (0, 7, 13)
 f32 = jnp.float32
 
 
@@ -260,7 +260,9 @@
         pack(lambda x, i=i: pop_ref[i, pl.ds(x, 8, stride=8), :], 0.0, 9 + n)
 
 
-def column_message_kernel(own_ref, recv_a, recv_b, edge_ref, first_ref, second_ref):
+def column_message_kernel(
+    own_ref, recv_b, recv_a, edge_ref, first_ref, second_ref, third_ref
+):
     even = is_even("row")
     slot = slots()
 
@@ -299,7 +301,7 @@
                 mask = jnp.logical_and(slot >= 4 * u, slot < 4 * u + 4)
                 to_left = jnp.where(mask, roll_y(value, 4 * u - 8), to_left)
                 to_right = jnp.where(mask, roll_y(value, 4 * u - 4), to_right)
-            first_ref[2 * g + h] = jnp.where(col_even, to_right, to_left)
+            first_ref[2 * g + h] = third_ref[2 * g + h] = jnp.where(col_even, to_right, to_left)
             second_ref[2 * g + h] = jnp.where(col_even, to_left, to_right)
         to_left = to_right = jnp.zeros((8, 128), f32)
         for s in range(6):
@@ -307,14 +309,14 @@
             right_field = 8 if s == 0 else 9 + near.index(y_up[s - 1])
             to_left = jnp.where(slot == s, roll_y(edge_ref[left_field, h], s - 8), to_left)
             to_right = jnp.where(slot == s, roll_y(edge_ref[right_field, h], s - 7), to_right)
-        first_ref[4 + h] = jnp.where(col_even, to_right, to_left)
+        first_ref[4 + h] = third_ref[4 + h] = jnp.where(col_even, to_right, to_left)
         second_ref[4 + h] = jnp.where(col_even, to_left, to_right)
 
 
 def main_kernel(
     base_ref,
+    recv_b,
     recv_a,
-    recv_b,
     pop_ref,
     moved_ref,
     order_ref,
@@ -354,7 +356,7 @@
 
         return row
 
-    lax.fori_loop(1, 15, relax(q_zero, q_one), 0, unroll=RELAX_UNROLL)
+    lax.fori_loop(1, 15, relax(q_zero, q_one), 0, unroll=7)
     lax.fori_loop(2, 14, relax(q_one, q_two), 0, unroll=6)
 
     def last(x):
@@ -384,7 +386,7 @@
             stream(i, value, x + 1)
         return carry
 
-    lax.fori_loop(0, 8, own_row, 0, unroll=MOVE_UNROLL)
+    lax.fori_loop(0, 8, own_row, 0, unroll=4)
 
     for n, i in enumerate(far):
         low = high = jnp.zeros((8, 128), f32)
@@ -413,22 +415,26 @@
 def edge_kernel(
     edge_ref,
     far_ref,
-    recv_a,
+    recv_first,
     recv_b,
+    recv_last,
     moved_ref,
     order_ref,
-    out_pop,
-    out_order,
+    new_pop,
+    new_order,
     strip,
     q_one,
     q_two,
-    done,
+    pop_out,
+    order_out,
+    sems,
 ):
     even = is_even("col")
+    late = lax.rem(lax.axis_index("col"), 4) >= 2
     slot, lane = slots(), lanes()
 
     def columns(j):
-        a, b = recv_a[j], recv_b[j]
+        a, b = jnp.where(late, recv_last[j], recv_first[j]), recv_b[j]
         return jnp.where(even, b, a), jnp.where(even, a, b)
 
     for h in range(2):
@@ -436,7 +442,7 @@
             from_left, from_right = columns(2 * (f // 4) + h)
             u = f % 4
             own = edge_ref[f, h]
-            strip[f, h] = jnp.where(slot < 4, roll_y(from_left, -4 * u), roll_y(own, -4))
+            strip[f, h] = jnp.where(slot < 8, roll_y(from_left, 4 - 4 * u), own)
             strip[f, 2 + h] = jnp.where(slot < 8, own, roll_y(from_right, 8 - 4 * u))
         from_left, from_right = columns(4 + h)
         for f in range(8, 28):
@@ -447,10 +453,10 @@
                 own = edge_ref[9 + near.index(i), h]
             else:
                 own = far_ref[far.index(i), h]
-            left, right = roll_y(own, -4), own
+            left = right = own
             if f == 8 or i in y_up:
                 s = 0 if f == 8 else 1 + y_up.index(i)
-                left = jnp.where(slot == 3, roll_y(from_left, 3 - s), left)
+                left = jnp.where(slot == 7, roll_y(from_left, 7 - s), left)
             if f == 8 or i in y_down:
                 s = 0 if f == 8 else 1 + y_down.index(i)
                 right = jnp.where(slot == 8, roll_y(from_right, 8 - s), right)
@@ -472,64 +478,71 @@
         def step(unit, carry):
             q, around, dx, dy, dz = gather_stencil(neighbours(source, unit))
             field = molecular_field(q, around, dx, dy, dz)
-            new = updated(q, field, dx, dy, dz, [strip[5 + a, unit] for a in range(3)])
+            return updated(q, field, dx, dy, dz, [strip[5 + a, unit] for a in range(3)])
+
+        results = [step(unit, 0) for unit in range(4)]
+        for unit in range(4):
             for k in range(5):
-                target[k, unit] = new[k]
-            return carry
-
-        return step
-
-    lax.fori_loop(0, 4, relax(strip, q_one), 0, unroll=EDGE_UNROLL)
-    lax.fori_loop(0, 4, relax(q_one, q_two), 0, unroll=EDGE_UNROLL)
-
-    def last(unit, carry):
+                target[k, unit] = results[unit][k]
+
+    relax(strip, q_one)
+    relax(q_one, q_two)
+
+    edge_lane = jnp.logical_or(lane < 4, lane >= 124)
+
+    def merge(field, units, load, shift_x, shift_y, target):
+        halves = [jnp.where(slot < 8 - shift_y, units[2 + h], units[h]) for h in range(2)]
+        rows = []
+        for x in range(8):
+            row = x + 4 - shift_x
+            pair = roll_y(halves[row // 8], shift_y - (SLOTS * (row % 8) + 8))
+            rows.append(jnp.where(edge_lane, pair, load(x)))
+        for x in range(8):
+            target[field, pl.ds(x, 8, stride=8), :] = rows[x]
+
+    copies = [pltpu.make_async_copy(order_out, new_order, sems.at[0])]
+    bounds = CHUNKS + (19,)
+    for n, first in enumerate(CHUNKS):
+        rows = pl.ds(first, bounds[n + 1] - first)
+        copies.append(pltpu.make_async_copy(pop_out.at[rows], new_pop.at[rows], sems.at[n + 1]))
+
+    relaxed, moving = [], []
+    for unit in range(4):
         q, around, dx, dy, dz = gather_stencil(neighbours(q_two, unit))
         field = molecular_field(q, around, dx, dy, dz)
         velocity = [strip[5 + a, unit] for a in range(3)]
-        new = updated(q, field, dx, dy, dz, velocity)
+        relaxed.append(updated(q, field, dx, dy, dz, velocity))
         force = force_of(field, dx, dy, dz)
-        for k in range(5):
-            done[19 + k, unit] = new[k]
-        for i, value in collide(
-            range(19), lambda i: strip[9 + i, unit], strip[8, unit], velocity, force
-        ):
-            _, b, c = (int(v) for v in lattice[i])
-            done[i, unit] = roll_y(roll_z(value, c), b)
-        return carry
-
-    lax.fori_loop(0, 4, last, 0, unroll=EDGE_UNROLL)
-
-    edge_lane = jnp.logical_or(lane < 4, lane >= 124)
-
-    def merged(field, shift, x, value):
-        row = x + 4 - shift
-        h, q = row // 8, row % 8
-        pair = halves[field][h]
-        return jnp.where(edge_lane, roll_y(pair, -(SLOTS * q + 8)), value)
-
-    halves = {}
-    for f in range(24):
-        halves[f] = [
-            jnp.where(slot < 8, done[f, 2 + h], roll_y(done[f, h], 4)) for h in range(2)
-        ]
-        shift = int(lattice[f][0]) if f < 19 else 0
-        for x in range(8):
-            if f < 19:
-                out_pop[f, pl.ds(x, 8, stride=8), :] = merged(f, shift, x, moved_ref[f, x + 1])
-            else:
-                out_order[f - 19, pl.ds(x, 8, stride=8), :] = merged(
-                    f, shift, x, order_ref[f - 19, x]
-                )
-
-
-def call(kernel, out_shapes, scratch, flops, *args, from_hbm=False):
-    whole = pl.BlockSpec(memory_space=pltpu.VMEM)
-    source = pl.BlockSpec(memory_space=pltpu.HBM) if from_hbm else whole
+        moving.append(
+            collide(
+                range(19),
+                lambda i, unit=unit: strip[9 + i, unit],
+                strip[8, unit],
+                velocity,
+                force,
+            )
+        )
+    for k in range(5):
+        merge(k, [new[k] for new in relaxed], lambda x, k=k: order_ref[k, x], 0, 0, order_out)
+    copies[0].start()
+    for items in zip(*moving):
+        i = items[0][0]
+        a, b, c = (int(v) for v in lattice[i])
+        units = [roll_z(value, c) for _, value in items]
+        merge(i, units, lambda x, i=i: moved_ref[i, x + 1], a, b, pop_out)
+        if i + 1 in bounds:
+            copies[bounds.index(i + 1)].start()
+    for copy in copies:
+        copy.wait()
+
+
+def call(kernel, out_shapes, scratch, flops, *args, from_hbm=False, to_hbm=False):
+    whole, outside = (pl.BlockSpec(memory_space=m) for m in (pltpu.VMEM, pltpu.HBM))
     return pl.pallas_call(
         kernel,
         out_shape=[jax.ShapeDtypeStruct(s, f32) for s in out_shapes],
-        in_specs=[source] * len(args),
-        out_specs=[whole] * len(out_shapes),
+        in_specs=[outside if from_hbm else whole] * len(args),
+        out_specs=[outside if to_hbm else whole] * len(out_shapes),
         scratch_shapes=[pltpu.VMEM(s, f32) if isinstance(s, tuple) else s for s in scratch],
         cost_estimate=pl.CostEstimate(
             flops=flops,
@@ -544,6 +557,10 @@
     return [
         (i, (i + 1) % size if i % 2 == first else (i - 1) % size) for i in range(size)
     ]
+
+
+def part(size, late):
+    return [(i, i ^ 1) for i in range(size) if (i % 4 >= 2) == late]
 
 
 def body(rows, cols, populations, order_tensor):
@@ -560,38 +577,48 @@
     recv_b = lax.ppermute(second, "row", swap(rows, 1))
     recv_a = lax.ppermute(first, "row", swap(rows, 0))
     own_edges = call(own_edges_kernel, [(NEAR, 2, 8, 128)], [], 2_000_000, base, pops)[0]
-    edges, left, right = call(
+    edges, first, second, third = call(
         column_message_kernel,
-        [(NEAR, 2, 8, 128), side, side],
+        [(NEAR, 2, 8, 128), side, side, side],
         [],
         1_000_000,
         own_edges,
+        recv_b,
         recv_a,
-        recv_b,
     )
-    col_a = lax.ppermute(left, "col", swap(cols, 0))
-    col_b = lax.ppermute(right, "col", swap(cols, 1))
+    col_first = lax.ppermute(first, "col", part(cols, False))
+    col_b = lax.ppermute(second, "col", swap(cols, 1))
+    col_last = lax.ppermute(third, "col", part(cols, True))
     moved, relaxed, far_edges = call(
         main_kernel,
         [(19, 10, 8, 128), (5, 8, 8, 128), (FAR, 2, 8, 128)],
         [(5, 16, 8, 128)] * 3 + [(3, 14, 8, 128), (10, 8, 128)],
         20_000_000,
         base,
+        recv_b,
         recv_a,
-        recv_b,
         pops,
     )
     new_pops, new_order = call(
         edge_kernel,
         [(19, 64, 128), (5, 64, 128)],
-        [(28, 4, 8, 128), (5, 4, 8, 128), (5, 4, 8, 128), (24, 4, 8, 128)],
+        [
+            (28, 4, 8, 128),
+            (5, 4, 8, 128),
+            (5, 4, 8, 128),
+            (19, 64, 128),
+            (5, 64, 128),
+            pltpu.SemaphoreType.DMA((len(CHUNKS) + 1,)),
+        ],
         8_000_000,
         edges,
         far_edges,
-        col_a,
+        col_first,
         col_b,
+        col_last,
         moved,
         relaxed,
+        to_hbm=True,
     )
     return new_pops.reshape(populations.shape), new_order.reshape(order_tensor.shape)
 

time: 44.3 us -> 40.1 us (0.905)
  the two profiles are of different devices: /device:TPU:4 before, /device:TPU:1 now
where the time goes in v3:
time: 40.1 us; the launch traced here: 39.8 us
  starting transfers between devices  32.4 us (81%)
  Pallas kernels  4.98 us (12%)
  waiting for transfers between devices  1.73 us (4%)
  between operations  0.7 us (2%)
    ppermute x1, starting transfers between devices, body(): recv_a = lax.ppermute(first, 'row', swap(rows, 0))  12.6 us
    ppermute x1, starting transfers between devices, body(): col_b = lax.ppermute(second, 'col', swap(cols, 1))  7.44 us
    ppermute x1, starting transfers between devices, body(): col_first = lax.ppermute(first, 'col', part(cols, False))  6.31 us
    ppermute x1, starting transfers between devices, body(): recv_b = lax.ppermute(second, 'row', swap(rows, 1))  5.39 us
    pallas_call x5, Pallas kernels, call(): pl.pallas_call(kernel, out_shape=[jax.ShapeDtypeStruct(s, f32) for s in o...  4.98 us
    ppermute x1, waiting for transfers between devices, body(): col_b = lax.ppermute(second, 'col', swap(cols, 1))  0.98 us
  transfers between devices with their start and end apart: 5, of which 2 were waited for; matrix products, arithmetic and copies ran while one was open for 0% of the time, Pallas kernels for 4%

profile of v3, /device:TPU:1, one launch (start us, length us, event | category | flops | bytes accessed | tf_op | source)
XLA Modules:
  0.0 39.8 jit_solution(4590490378250733369)
XLA Ops:
  0.6 1.5 %shard_map.41 = (f32[9,8,8,128]{3,2,1,0:T(8,128)S(1)}, f32[35,8,128]{2,1,0:T(8,128)S(1)}, f32[35,8,128]{2,1,0:T(8,128)S(1)}, f32[19,64,128]{2,1,0:T(8,128)S(1)}) custom-call(f32[19,64,128]{2,1,0:T(8,128)} %bitcast.4, f32[5,64,128]{2,1,0:T(8,128)} %bitcast.5), custom_call_target="tpu_custom_call" | custom-call | flops 2000000 | bytes 1990656 | tf_op jit(solution)/shard_map/pallas_call | solution.py:541
  2.1 5.4 %collective-permute-start = (f32[35,8,128]{2,1,0:T(8,128)S(1)}, f32[35,8,128]{2,1,0:T(8,128)S(1)}, u32[]{:S(2)}, u32[]{:S(2)}) collective-permute-start(f32[35,8,128]{2,1,0:T(8,128)S(1)} %get-tuple-element.17), channel_id=1, source_target_pairs={{0,1008},{16,32},{32,16},{48,64},{64,48},{80,96},{96,80},{112,128}... | collective-permute-start | bytes 430088 | tf_op jit(solution)/shard_map/ppermute | solution.py:577
  7.5 12.6 %collective-permute-start.1 = (f32[35,8,128]{2,1,0:T(8,128)S(1)}, f32[35,8,128]{2,1,0:T(8,128)S(1)}, u32[]{:S(2)}, u32[]{:S(2)}) collective-permute-start(f32[35,8,128]{2,1,0:T(8,128)S(1)} %get-tuple-element.18), channel_id=1, source_target_pairs={{0,16},{16,0},{32,48},{48,32},{64,80},{80,64},{96,112},{112,96},{1... | collective-permute-start | bytes 430088 | tf_op jit(solution)/shard_map/ppermute | solution.py:578
  20.1 0.2 shard_map.42.own_ref
  20.4 0.0 collective-permute-done.recv_b
  20.4 0.7 %collective-permute-done.1.recv_a = f32[35,8,128]{2,1,0:T(8,128)S(1)} collective-permute-done((f32[35,8,128]{2,1,0:T(8,128)S(1)}, f32[35,8,128]{2,1,0:T(8,128)S(1)}, u32[]{:S(2)}, u32[]{:S(2)}) %collective-permute-start.1) | collective-permute-done | bytes 143392 | tf_op jit(solution)/shard_map/ppermute | solution.py:578
  21.1 0.2 shard_map.43
  21.4 6.3 %collective-permute-start.2 = (f32[6,8,128]{2,1,0:T(8,128)S(1)}, f32[6,8,128]{2,1,0:T(8,128)S(1)}, u32[]{:S(2)}, u32[]{:S(2)}) collective-permute-start(f32[6,8,128]{2,1,0:T(8,128)S(1)} %get-tuple-element.21), channel_id=1, source_target_pairs={{0,1},{1,0},{4,5},{5,4},{8,9},{9,8},{12,13},{13,12},{16,17},{17,16... | collective-permute-start | bytes 73736 | tf_op jit(solution)/shard_map/ppermute | solution.py:589
  27.7 7.4 %collective-permute-start.3 = (f32[6,8,128]{2,1,0:T(8,128)S(1)}, f32[6,8,128]{2,1,0:T(8,128)S(1)}, u32[]{:S(2)}, u32[]{:S(2)}) collective-permute-start(f32[6,8,128]{2,1,0:T(8,128)S(1)} %get-tuple-element.22), channel_id=1, source_target_pairs={{0,15},{1,2},{2,1},{3,4},{4,3},{5,6},{6,5},{7,8},{8,7},{9,10},{10,... | collective-permute-start | bytes 73736 | tf_op jit(solution)/shard_map/ppermute | solution.py:590
  35.1 0.7 %collective-permute-start.4 = (f32[6,8,128]{2,1,0:T(8,128)S(1)}, f32[6,8,128]{2,1,0:T(8,128)S(1)}, u32[]{:S(2)}, u32[]{:S(2)}) collective-permute-start(f32[6,8,128]{2,1,0:T(8,128)S(1)} %get-tuple-element.23), channel_id=1, source_target_pairs={{2,3},{3,2},{6,7},{7,6},{10,11},{11,10},{14,15},{15,14},{18,19},{1... | collective-permute-start | bytes 73736 | tf_op jit(solution)/shard_map/ppermute | solution.py:591
  35.8 1.5 %shard_map.44 = (f32[19,10,8,128]{3,2,1,0:T(8,128)S(1)}, f32[5,8,8,128]{3,2,1,0:T(8,128)S(1)}, f32[9,2,8,128]{3,2,1,0:T(8,128)S(1)}) custom-call(f32[9,8,8,128]{3,2,1,0:T(8,128)S(1)} %get-tuple-element.15.base_ref, f32[35,8,128]{2,1,0:T(8,128)S(1)} %collective-permute-done.recv_b, f32[35,8,128]{2,1,0:T(8,128)S(1)} %collective-permute-done.1.recv_a, ...), custom_call_target="tpu_custom_call" | custom-call | flops 20000000 | bytes 2220032 | tf_op jit(solution)/shard_map/pallas_call | solution.py:541
  37.3 0.0 collective-permute-done.2.recv_first
  37.3 1.0 %collective-permute-done.3.recv_b = f32[6,8,128]{2,1,0:T(8,128)S(1)} collective-permute-done((f32[6,8,128]{2,1,0:T(8,128)S(1)}, f32[6,8,128]{2,1,0:T(8,128)S(1)}, u32[]{:S(2)}, u32[]{:S(2)}) %collective-permute-start.3) | collective-permute-done | bytes 24608 | tf_op jit(solution)/shard_map/ppermute | solution.py:590
  38.3 0.0 collective-permute-done.4.recv_last
  38.3 1.5 %shard_map.45 = (f32[19,64,128]{2,1,0:T(8,128)}, f32[5,64,128]{2,1,0:T(8,128)}) custom-call(f32[19,2,8,128]{3,2,1,0:T(8,128)S(1)} %get-tuple-element.19.edge_ref, f32[9,2,8,128]{3,2,1,0:T(8,128)S(1)} %get-tuple-element.20.far_ref, f32[6,8,128]{2,1,0:T(8,128)S(1)} %collective-permute-done.2.recv_first, f32[6,8,128]{2,1,0:T(8,128)S(1)} %collective-permute-done.3.recv_b, ...), custom_call_target="tpu_custom_call" | custom-call | flops 8000000 | bytes 2031616 | tf_op jit(solution)/shard_map/pallas_call | solution.py:541
Async XLA Ops:
  2.1 18.2 %collective-permute-start = (f32[35,8,128]{2,1,0:T(8,128)S(1)}, f32[35,8,128]{2,1,0:T(8,128)S(1)}, u32[]{:S(2)}, u32[]{:S(2)}) collective-permute-start(f32[35,8,128]{2,1,0:T(8,128)S(1)} %get-tuple-element.17), channel_id=1, source_target_pairs={{0,1008},{16,32},{32,16},{48,64},{64,48},{80,96},{96,80},{112,128}... | collective-permute-start | bytes 430088 | tf_op jit(solution)/shard_map/ppermute | solution.py:577
  7.5 13.6 %collective-permute-start.1 = (f32[35,8,128]{2,1,0:T(8,128)S(1)}, f32[35,8,128]{2,1,0:T(8,128)S(1)}, u32[]{:S(2)}, u32[]{:S(2)}) collective-permute-start(f32[35,8,128]{2,1,0:T(8,128)S(1)} %get-tuple-element.18), channel_id=1, source_target_pairs={{0,16},{16,0},{32,48},{48,32},{64,80},{80,64},{96,112},{112,96},{1... | collective-permute-start | bytes 430088 | tf_op jit(solution)/shard_map/ppermute | solution.py:578
  21.4 15.9 %collective-permute-start.2 = (f32[6,8,128]{2,1,0:T(8,128)S(1)}, f32[6,8,128]{2,1,0:T(8,128)S(1)}, u32[]{:S(2)}, u32[]{:S(2)}) collective-permute-start(f32[6,8,128]{2,1,0:T(8,128)S(1)} %get-tuple-element.21), channel_id=1, source_target_pairs={{0,1},{1,0},{4,5},{5,4},{8,9},{9,8},{12,13},{13,12},{16,17},{17,16... | collective-permute-start | bytes 73736 | tf_op jit(solution)/shard_map/ppermute | solution.py:589
  27.7 10.6 %collective-permute-start.3 = (f32[6,8,128]{2,1,0:T(8,128)S(1)}, f32[6,8,128]{2,1,0:T(8,128)S(1)}, u32[]{:S(2)}, u32[]{:S(2)}) collective-permute-start(f32[6,8,128]{2,1,0:T(8,128)S(1)} %get-tuple-element.22), channel_id=1, source_target_pairs={{0,15},{1,2},{2,1},{3,4},{4,3},{5,6},{6,5},{7,8},{8,7},{9,10},{10,... | collective-permute-start | bytes 73736 | tf_op jit(solution)/shard_map/ppermute | solution.py:590
  35.1 3.1 %collective-permute-start.4 = (f32[6,8,128]{2,1,0:T(8,128)S(1)}, f32[6,8,128]{2,1,0:T(8,128)S(1)}, u32[]{:S(2)}, u32[]{:S(2)}) collective-permute-start(f32[6,8,128]{2,1,0:T(8,128)S(1)} %get-tuple-element.23), channel_id=1, source_target_pairs={{2,3},{3,2},{6,7},{7,6},{10,11},{11,10},{14,15},{15,14},{18,19},{1... | collective-permute-start | bytes 73736 | tf_op jit(solution)/shard_map/ppermute | solution.py:591

commit v4 on v3

--- a/solution.py
+++ b/solution.py
@@ -261,7 +261,7 @@
 
 
 def column_message_kernel(
-    own_ref, recv_b, recv_a, edge_ref, first_ref, second_ref, third_ref
+    own_ref, recv_b, recv_a, edge_ref, first_ref, second_ref, third_ref, fourth_ref
 ):
     even = is_even("row")
     slot = slots()
@@ -302,7 +302,7 @@
                 to_left = jnp.where(mask, roll_y(value, 4 * u - 8), to_left)
                 to_right = jnp.where(mask, roll_y(value, 4 * u - 4), to_right)
             first_ref[2 * g + h] = third_ref[2 * g + h] = jnp.where(col_even, to_right, to_left)
-            second_ref[2 * g + h] = jnp.where(col_even, to_left, to_right)
+            second_ref[2 * g + h] = fourth_ref[2 * g + h] = jnp.where(col_even, to_left, to_right)
         to_left = to_right = jnp.zeros((8, 128), f32)
         for s in range(6):
             left_field = 8 if s == 0 else 9 + near.index(y_down[s - 1])
@@ -310,10 +310,37 @@
             to_left = jnp.where(slot == s, roll_y(edge_ref[left_field, h], s - 8), to_left)
             to_right = jnp.where(slot == s, roll_y(edge_ref[right_field, h], s - 7), to_right)
         first_ref[4 + h] = third_ref[4 + h] = jnp.where(col_even, to_right, to_left)
-        second_ref[4 + h] = jnp.where(col_even, to_left, to_right)
-
-
-def main_kernel(
+        second_ref[4 + h] = fourth_ref[4 + h] = jnp.where(col_even, to_left, to_right)
+
+
+def is_late():
+    return lax.rem(lax.axis_index("col"), 4) >= 2
+
+
+def early_main_kernel(base_ref, recv_b, recv_a, pop_ref, third_ref, fourth_ref, *rest):
+    outputs, scratch = rest[:3], rest[5:]
+    rest[3][...] = third_ref[...]
+    rest[4][...] = fourth_ref[...]
+
+    @pl.when(jnp.logical_not(is_late()))
+    def _():
+        main_block(base_ref, recv_b, recv_a, pop_ref, *outputs, *scratch)
+
+
+def late_main_kernel(base_ref, recv_b, recv_a, pop_ref, *rest):
+    done, outputs, scratch = rest[:3], rest[3:6], rest[6:]
+
+    @pl.when(is_late())
+    def _():
+        main_block(base_ref, recv_b, recv_a, pop_ref, *outputs, *scratch)
+
+    @pl.when(jnp.logical_not(is_late()))
+    def _():
+        for source, target in zip(done, outputs):
+            target[...] = source[...]
+
+
+def main_block(
     base_ref,
     recv_b,
     recv_a,
@@ -415,8 +442,9 @@
 def edge_kernel(
     edge_ref,
     far_ref,
+    recv_down,
     recv_first,
-    recv_b,
+    recv_up,
     recv_last,
     moved_ref,
     order_ref,
@@ -430,11 +458,12 @@
     sems,
 ):
     even = is_even("col")
-    late = lax.rem(lax.axis_index("col"), 4) >= 2
+    late = is_late()
     slot, lane = slots(), lanes()
 
     def columns(j):
-        a, b = jnp.where(late, recv_last[j], recv_first[j]), recv_b[j]
+        a = jnp.where(late, recv_last[j], recv_first[j])
+        b = jnp.where(late, recv_up[j], recv_down[j])
         return jnp.where(even, b, a), jnp.where(even, a, b)
 
     for h in range(2):
@@ -559,6 +588,11 @@
     ]
 
 
+def crossing(size):
+    down = [(i, (i + 1) % size if i % 2 else i - 1) for i in range(size) if i % 4 >= 2]
+    return down, [(target, source) for source, target in down]
+
+
 def part(size, late):
     return [(i, i ^ 1) for i in range(size) if (i % 4 >= 2) == late]
 
@@ -577,27 +611,44 @@
     recv_b = lax.ppermute(second, "row", swap(rows, 1))
     recv_a = lax.ppermute(first, "row", swap(rows, 0))
     own_edges = call(own_edges_kernel, [(NEAR, 2, 8, 128)], [], 2_000_000, base, pops)[0]
-    edges, first, second, third = call(
+    edges, first, second, third, fourth = call(
         column_message_kernel,
-        [(NEAR, 2, 8, 128), side, side, side],
+        [(NEAR, 2, 8, 128), side, side, side, side],
         [],
         1_000_000,
         own_edges,
         recv_b,
         recv_a,
     )
-    col_first = lax.ppermute(first, "col", part(cols, False))
-    col_b = lax.ppermute(second, "col", swap(cols, 1))
-    col_last = lax.ppermute(third, "col", part(cols, True))
-    moved, relaxed, far_edges = call(
-        main_kernel,
-        [(19, 10, 8, 128), (5, 8, 8, 128), (FAR, 2, 8, 128)],
-        [(5, 16, 8, 128)] * 3 + [(3, 14, 8, 128), (10, 8, 128)],
+    down, up = crossing(cols)
+    recv_down = lax.ppermute(second, "col", down)
+    recv_first = lax.ppermute(first, "col", part(cols, False))
+    blocks = [(19, 10, 8, 128), (5, 8, 8, 128), (FAR, 2, 8, 128)]
+    scratch = [(5, 16, 8, 128)] * 3 + [(3, 14, 8, 128), (10, 8, 128)]
+    *half_done, third_again, fourth_again = call(
+        early_main_kernel,
+        [*blocks, side, side],
+        scratch,
         20_000_000,
         base,
         recv_b,
         recv_a,
         pops,
+        third,
+        fourth,
+    )
+    recv_up = lax.ppermute(fourth_again, "col", up)
+    recv_last = lax.ppermute(third_again, "col", part(cols, True))
+    moved, relaxed, far_edges = call(
+        late_main_kernel,
+        blocks,
+        scratch,
+        20_000_000,
+        base,
+        recv_b,
+        recv_a,
+        pops,
+        *half_done,
     )
     new_pops, new_order = call(
         edge_kernel,
@@ -613,9 +664,10 @@
         8_000_000,
         edges,
         far_edges,
-        col_first,
-        col_b,
-        col_last,
+        recv_down,
+        recv_first,
+        recv_up,
+        recv_last,
         moved,
         relaxed,
         to_hbm=True,

time: 40.1 us -> 39.2 us (0.978)
  waiting for transfers between devices: 1.73 us -> 0.9 us
    ppermute x3 -> x4, waiting for transfers between devices: 0.99 us -> 0.15 us  [the longest x1 0.14 us: body(): recv_up = lax.ppermute(fourth_again, 'col', up)]
    ppermute x3 -> x4, starting transfers between devices: 14.4 us -> 14.2 us  [the longest x1 6.31 us: body(): recv_first = lax.ppermute(first, 'col', part(cols, False))]
    pallas_call x5 -> x6, Pallas kernels: 4.98 us -> 5.08 us  [call(): pl.pallas_call(kernel, out_shape=[jax.ShapeDtypeStruct(s, f32) for s in o...]
  transfers between devices with their start and end apart: 5 -> 6, of which waited for: 2 -> 2; matrix products, arithmetic and copies ran while one was open for 0% -> 0% of each run, Pallas kernels for 4% -> 5%
where the time goes in v4:
time: 39.2 us; the launch traced here: 38.9 us
  starting transfers between devices  32.2 us (82%)
  Pallas kernels  5.08 us (13%)
  waiting for transfers between devices  0.9 us (2%)
  between operations  0.73 us (2%)
    ppermute x1, starting transfers between devices, body(): recv_a = lax.ppermute(first, 'row', swap(rows, 0))  12.6 us
    ppermute x1, starting transfers between devices, body(): recv_first = lax.ppermute(first, 'col', part(cols, False))  6.31 us
    ppermute x1, starting transfers between devices, body(): recv_up = lax.ppermute(fourth_again, 'col', up)  5.96 us
    ppermute x1, starting transfers between devices, body(): recv_b = lax.ppermute(second, 'row', swap(rows, 1))  5.39 us
    pallas_call x6, Pallas kernels, call(): pl.pallas_call(kernel, out_shape=[jax.ShapeDtypeStruct(s, f32) for s in o...  5.08 us
    ppermute x1, starting transfers between devices, body(): recv_down = lax.ppermute(second, 'col', down)  1.29 us
  transfers between devices with their start and end apart: 6, of which 2 were waited for; matrix products, arithmetic and copies ran while one was open for 0% of the time, Pallas kernels for 5%

profile of v4, /device:TPU:1, one launch (start us, length us, event | category | flops | bytes accessed | tf_op | source)
XLA Modules:
  0.0 38.9 jit_solution(2535629532898995945)
XLA Ops:
  0.6 1.5 %shard_map.41 = (f32[9,8,8,128]{3,2,1,0:T(8,128)S(1)}, f32[35,8,128]{2,1,0:T(8,128)S(1)}, f32[35,8,128]{2,1,0:T(8,128)S(1)}, f32[19,64,128]{2,1,0:T(8,128)S(1)}) custom-call(f32[19,64,128]{2,1,0:T(8,128)} %bitcast.4, f32[5,64,128]{2,1,0:T(8,128)} %bitcast.5), custom_call_target="tpu_custom_call" | custom-call | flops 2000000 | bytes 1990656 | tf_op jit(solution)/shard_map/pallas_call | solution.py:570
  2.1 5.4 %collective-permute-start = (f32[35,8,128]{2,1,0:T(8,128)S(1)}, f32[35,8,128]{2,1,0:T(8,128)S(1)}, u32[]{:S(2)}, u32[]{:S(2)}) collective-permute-start(f32[35,8,128]{2,1,0:T(8,128)S(1)} %get-tuple-element.23), channel_id=1, source_target_pairs={{0,1008},{16,32},{32,16},{48,64},{64,48},{80,96},{96,80},{112,128}... | collective-permute-start | bytes 430088 | tf_op jit(solution)/shard_map/ppermute | solution.py:611
  7.5 12.6 %collective-permute-start.1 = (f32[35,8,128]{2,1,0:T(8,128)S(1)}, f32[35,8,128]{2,1,0:T(8,128)S(1)}, u32[]{:S(2)}, u32[]{:S(2)}) collective-permute-start(f32[35,8,128]{2,1,0:T(8,128)S(1)} %get-tuple-element.24), channel_id=1, source_target_pairs={{0,16},{16,0},{32,48},{48,32},{64,80},{80,64},{96,112},{112,96},{1... | collective-permute-start | bytes 430088 | tf_op jit(solution)/shard_map/ppermute | solution.py:612
  20.1 0.2 shard_map.42.own_ref
  20.4 0.0 collective-permute-done.recv_b
  20.4 0.7 %collective-permute-done.1.recv_a = f32[35,8,128]{2,1,0:T(8,128)S(1)} collective-permute-done((f32[35,8,128]{2,1,0:T(8,128)S(1)}, f32[35,8,128]{2,1,0:T(8,128)S(1)}, u32[]{:S(2)}, u32[]{:S(2)}) %collective-permute-start.1) | collective-permute-done | bytes 143392 | tf_op jit(solution)/shard_map/ppermute | solution.py:612
  21.1 0.2 shard_map.43
  21.4 1.3 %collective-permute-start.2 = (f32[6,8,128]{2,1,0:T(8,128)S(1)}, f32[6,8,128]{2,1,0:T(8,128)S(1)}, u32[]{:S(2)}, u32[]{:S(2)}) collective-permute-start(f32[6,8,128]{2,1,0:T(8,128)S(1)} %get-tuple-element.32), channel_id=1, source_target_pairs={{2,1},{3,4},{6,5},{7,8},{10,9},{11,12},{14,13},{15,0},{18,17},{19,... | collective-permute-start | bytes 73736 | tf_op jit(solution)/shard_map/ppermute | solution.py:624
  22.7 6.3 %collective-permute-start.3 = (f32[6,8,128]{2,1,0:T(8,128)S(1)}, f32[6,8,128]{2,1,0:T(8,128)S(1)}, u32[]{:S(2)}, u32[]{:S(2)}) collective-permute-start(f32[6,8,128]{2,1,0:T(8,128)S(1)} %get-tuple-element.33), channel_id=1, source_target_pairs={{0,1},{1,0},{4,5},{5,4},{8,9},{9,8},{12,13},{13,12},{16,17},{17,16... | collective-permute-start | bytes 73736 | tf_op jit(solution)/shard_map/ppermute | solution.py:625
  29.0 1.5 %shard_map.44 = (f32[19,10,8,128]{3,2,1,0:T(8,128)S(1)}, f32[5,8,8,128]{3,2,1,0:T(8,128)S(1)}, f32[9,2,8,128]{3,2,1,0:T(8,128)S(1)}, f32[6,8,128]{2,1,0:T(8,128)S(1)}, f32[6,8,128]{2,1,0:T(8,128)S(1)}) custom-call(f32[9,8,8,128]{3,2,1,0:T(8,128)S(1)} %get-tuple-element.21.base_ref, f32[35,8,128]{2,1,0:T(8,128)S(1)} %collective-permute-done.recv_b, ...), custom_call_target="tpu_custom_call" | custom-call | flops 20000000 | bytes 2318336 | tf_op jit(solution)/shard_map/pallas_call | solution.py:570
  30.5 6.0 %collective-permute-start.4 = (f32[6,8,128]{2,1,0:T(8,128)S(1)}, f32[6,8,128]{2,1,0:T(8,128)S(1)}, u32[]{:S(2)}, u32[]{:S(2)}) collective-permute-start(f32[6,8,128]{2,1,0:T(8,128)S(1)} %get-tuple-element.34), channel_id=1, source_target_pairs={{1,2},{4,3},{5,6},{8,7},{9,10},{12,11},{13,14},{0,15},{17,18},{20,... | collective-permute-start | bytes 73736 | tf_op jit(solution)/shard_map/ppermute | solution.py:640
  36.4 0.7 %collective-permute-start.5 = (f32[6,8,128]{2,1,0:T(8,128)S(1)}, f32[6,8,128]{2,1,0:T(8,128)S(1)}, u32[]{:S(2)}, u32[]{:S(2)}) collective-permute-start(f32[6,8,128]{2,1,0:T(8,128)S(1)} %get-tuple-element.35), channel_id=1, source_target_pairs={{2,3},{3,2},{6,7},{7,6},{10,11},{11,10},{14,15},{15,14},{18,19},{1... | collective-permute-start | bytes 73736 | tf_op jit(solution)/shard_map/ppermute | solution.py:641
  37.1 0.1 shard_map.45
  37.2 0.0 collective-permute-done.2.recv_down
  37.2 0.0 collective-permute-done.3.recv_first
  37.2 0.1 collective-permute-done.4.recv_up
  37.4 0.0 collective-permute-done.5.recv_last
  37.4 1.5 %shard_map.46 = (f32[19,64,128]{2,1,0:T(8,128)}, f32[5,64,128]{2,1,0:T(8,128)}) custom-call(f32[19,2,8,128]{3,2,1,0:T(8,128)S(1)} %get-tuple-element.25.edge_ref, f32[9,2,8,128]{3,2,1,0:T(8,128)S(1)} %get-tuple-element.31.far_ref, f32[6,8,128]{2,1,0:T(8,128)S(1)} %collective-permute-done.2.recv_down, f32[6,8,128]{2,1,0:T(8,128)S(1)} %collective-permute-done.3.recv_first, ...), custom_call_target="tpu_custom_call" | custom-call | flops 8000000 | bytes 2056192 | tf_op jit(solution)/shard_map/pallas_call | solution.py:570
Async XLA Ops:
  2.1 18.2 %collective-permute-start = (f32[35,8,128]{2,1,0:T(8,128)S(1)}, f32[35,8,128]{2,1,0:T(8,128)S(1)}, u32[]{:S(2)}, u32[]{:S(2)}) collective-permute-start(f32[35,8,128]{2,1,0:T(8,128)S(1)} %get-tuple-element.23), channel_id=1, source_target_pairs={{0,1008},{16,32},{32,16},{48,64},{64,48},{80,96},{96,80},{112,128}... | collective-permute-start | bytes 430088 | tf_op jit(solution)/shard_map/ppermute | solution.py:611
  7.5 13.6 %collective-permute-start.1 = (f32[35,8,128]{2,1,0:T(8,128)S(1)}, f32[35,8,128]{2,1,0:T(8,128)S(1)}, u32[]{:S(2)}, u32[]{:S(2)}) collective-permute-start(f32[35,8,128]{2,1,0:T(8,128)S(1)} %get-tuple-element.24), channel_id=1, source_target_pairs={{0,16},{16,0},{32,48},{48,32},{64,80},{80,64},{96,112},{112,96},{1... | collective-permute-start | bytes 430088 | tf_op jit(solution)/shard_map/ppermute | solution.py:612
  21.4 15.8 %collective-permute-start.2 = (f32[6,8,128]{2,1,0:T(8,128)S(1)}, f32[6,8,128]{2,1,0:T(8,128)S(1)}, u32[]{:S(2)}, u32[]{:S(2)}) collective-permute-start(f32[6,8,128]{2,1,0:T(8,128)S(1)} %get-tuple-element.32), channel_id=1, source_target_pairs={{2,1},{3,4},{6,5},{7,8},{10,9},{11,12},{14,13},{15,0},{18,17},{19,... | collective-permute-start | bytes 73736 | tf_op jit(solution)/shard_map/ppermute | solution.py:624
  22.7 14.6 %collective-permute-start.3 = (f32[6,8,128]{2,1,0:T(8,128)S(1)}, f32[6,8,128]{2,1,0:T(8,128)S(1)}, u32[]{:S(2)}, u32[]{:S(2)}) collective-permute-start(f32[6,8,128]{2,1,0:T(8,128)S(1)} %get-tuple-element.33), channel_id=1, source_target_pairs={{0,1},{1,0},{4,5},{5,4},{8,9},{9,8},{12,13},{13,12},{16,17},{17,16... | collective-permute-start | bytes 73736 | tf_op jit(solution)/shard_map/ppermute | solution.py:625
  30.5 6.9 %collective-permute-start.4 = (f32[6,8,128]{2,1,0:T(8,128)S(1)}, f32[6,8,128]{2,1,0:T(8,128)S(1)}, u32[]{:S(2)}, u32[]{:S(2)}) collective-permute-start(f32[6,8,128]{2,1,0:T(8,128)S(1)} %get-tuple-element.34), channel_id=1, source_target_pairs={{1,2},{4,3},{5,6},{8,7},{9,10},{12,11},{13,14},{0,15},{17,18},{20,... | collective-permute-start | bytes 73736 | tf_op jit(solution)/shard_map/ppermute | solution.py:640
  36.4 0.9 %collective-permute-start.5 = (f32[6,8,128]{2,1,0:T(8,128)S(1)}, f32[6,8,128]{2,1,0:T(8,128)S(1)}, u32[]{:S(2)}, u32[]{:S(2)}) collective-permute-start(f32[6,8,128]{2,1,0:T(8,128)S(1)} %get-tuple-element.35), channel_id=1, source_target_pairs={{2,3},{3,2},{6,7},{7,6},{10,11},{11,10},{14,15},{15,14},{18,19},{1... | collective-permute-start | bytes 73736 | tf_op jit(solution)/shard_map/ppermute | solution.py:641

commit v5 on v4

--- a/solution.py
+++ b/solution.py
@@ -44,7 +44,9 @@
 y_up = [i for i in range(19) if lattice[i][1] == 1]
 y_down = [i for i in range(19) if lattice[i][1] == -1]
 
-VEL, DEN, POP, FACE = 20, 29, 30, 35
+VEL, DEN, POP, FACE, PADDED = 20, 29, 30, 35, 42
+CROSS_COST = 4_000_000_000
+STRIPS = 6
 SLOTS = 16
 near = sorted(y_up + y_down)
 far = [i for i in range(19) if i not in near]
@@ -183,8 +185,22 @@
                 yield j, rest * load(j) + (first + second if sign > 0 else first - second)
 
 
+def placed(value, row, into):
+    q = row % 8
+    lane = lanes()
+    mask = jnp.logical_and(lane >= SLOTS * q, lane < SLOTS * q + SLOTS)
+    return jnp.where(mask, roll_y(value, 8 + SLOTS * q), into)
+
+
 def moments_kernel(
-    pop_hbm, order_hbm, base_ref, first_ref, second_ref, pop_ref, order_ref, sems
+    pop_hbm,
+    order_hbm,
+    base_ref,
+    edge_ref,
+    strip_ref,
+    pop_ref,
+    order_ref,
+    sems,
 ):
     copies = [
         pltpu.make_async_copy(order_hbm, order_ref, sems.at[0]),
@@ -195,8 +211,11 @@
     for copy in copies:
         copy.wait()
 
-    def row(x, carry):
-        p = [pop_ref[i, pl.ds(x, 8, stride=8), :] for i in range(19)]
+    def pop(i, x):
+        return pop_ref[i, pl.ds(x, 8, stride=8), :]
+
+    for x in range(8):
+        p = [pop(i, x) for i in range(19)]
         density = p[0]
         for i in range(1, 19):
             density = density + p[i]
@@ -211,41 +230,7 @@
         base_ref[8, x] = density
         for k in range(5):
             base_ref[k, x] = order_ref[k, pl.ds(x, 8, stride=8), :]
-        return carry
-
-    lax.fori_loop(0, 8, row, 0)
-    even = is_even("row")
-    for out, high in ((first_ref, even), (second_ref, jnp.logical_not(even))):
-
-        @pl.when(high)
-        def _():
-            for k in range(5):
-                out[4 * k : 4 * k + 4] = base_ref[k, 4:8]
-            for a in range(3):
-                out[VEL + 3 * a : VEL + 3 * a + 3] = base_ref[5 + a, 5:8]
-            out[DEN] = base_ref[8, 7]
-            for j, i in enumerate(x_up):
-                out[POP + j] = pop_ref[i, pl.ds(7, 8, stride=8), :]
-
-        @pl.when(jnp.logical_not(high))
-        def _():
-            for k in range(5):
-                out[4 * k : 4 * k + 4] = base_ref[k, 0:4]
-            for a in range(3):
-                out[VEL + 3 * a : VEL + 3 * a + 3] = base_ref[5 + a, 0:3]
-            out[DEN] = base_ref[8, 0]
-            for j, i in enumerate(x_down):
-                out[POP + j] = pop_ref[i, pl.ds(0, 8, stride=8), :]
-
-
-def placed(value, row, into):
-    q = row % 8
-    lane = lanes()
-    mask = jnp.logical_and(lane >= SLOTS * q, lane < SLOTS * q + SLOTS)
-    return jnp.where(mask, roll_y(value, 8 + SLOTS * q), into)
-
-
-def own_edges_kernel(base_ref, pop_ref, edge_ref):
+
     def pack(load, fill, field):
         low = high = jnp.full((8, 128), fill, f32)
         for x in range(4):
@@ -257,40 +242,86 @@
     for f in range(9):
         pack(lambda x, f=f: base_ref[f, x], 1.0 if f == 8 else 0.0, f)
     for n, i in enumerate(near):
-        pack(lambda x, i=i: pop_ref[i, pl.ds(x, 8, stride=8), :], 0.0, 9 + n)
+        pack(lambda x, i=i: pop(i, x), 0.0, 9 + n)
+
+    even = is_even("row")
+    for side, chosen in ((0, even), (1, jnp.logical_not(even))):
+
+        @pl.when(chosen)
+        def _():
+            pack_strips(edge_ref, side, strip_ref)
+
+
+def rows_kernel(base_ref, edge_ref, pop_ref, first_ref, second_ref):
+    even = is_even("row")
+    second_ref[FACE:] = jnp.zeros((PADDED - FACE, 8, 128), f32)
+    for rows, high in ((first_ref, even), (second_ref, jnp.logical_not(even))):
+        for side, chosen in ((1, high), (0, jnp.logical_not(high))):
+
+            @pl.when(chosen)
+            def _():
+                if rows is first_ref:
+                    pack_strips(edge_ref, side, rows.at[FACE:])
+                for k in range(5):
+                    rows[4 * k : 4 * k + 4] = base_ref[k, 4 * side : 4 * side + 4]
+                for a in range(3):
+                    rows[VEL + 3 * a : VEL + 3 * a + 3] = base_ref[5 + a, 5 * side : 5 * side + 3]
+                rows[DEN] = base_ref[8, 7 * side]
+                for j, i in enumerate(x_up if side else x_down):
+                    rows[POP + j] = pop_ref[i, pl.ds(7 * side, 8, stride=8), :]
+
+
+def pack_strips(edge_ref, side, target):
+    fields = list(range(9)) + corner_fields(side)
+    mine = lanes() < 64 if side else lanes() >= 64
+    for n in range(0, len(fields), 2):
+        value = edge_ref[fields[n], side]
+        if n + 1 < len(fields):
+            value = jnp.where(mine, value, roll_y(edge_ref[fields[n + 1], side], 64))
+        target[n // 2] = value
+
+
+def corner_fields(side):
+    return [9 + near.index(i) for i in (x_up if side else x_down) if i in near]
+
+
+def widen(edge_ref, strips, below, out_ref):
+    left_half = lanes() < 64
+    fields = list(range(9)) + corner_fields(1 if below else 0)
+    half = 0 if below else 1
+    for n, f in enumerate(fields):
+        value = roll_y(strips[n // 2], 64 * (n % 2))
+        keep = left_half if below else jnp.logical_not(left_half)
+        out_ref[f, half] = jnp.where(keep, value, edge_ref[f, half])
+
+
+def cross_chip_kernel(own_ref, strip_ref, edge_ref):
+    even = is_even("row")
+    edge_ref[...] = own_ref[...]
+
+    @pl.when(even)
+    def _():
+        widen(own_ref, strip_ref, True, edge_ref)
+
+    @pl.when(jnp.logical_not(even))
+    def _():
+        widen(own_ref, strip_ref, False, edge_ref)
 
 
 def column_message_kernel(
-    own_ref, recv_b, recv_a, edge_ref, first_ref, second_ref, third_ref, fourth_ref
+    half_ref, first_row_ref, edge_ref, first_ref, second_ref, third_ref, fourth_ref
 ):
     even = is_even("row")
     slot = slots()
-
-    def halo(j):
-        a, b = recv_a[j], recv_b[j]
-        return jnp.where(even, b, a), jnp.where(even, a, b)
-
-    def widen(field, rows):
-        low, high = own_ref[field, 0], own_ref[field, 1]
-        for j, row_low, row_high in rows:
-            below, above = halo(j)
-            low, high = placed(below, row_low, low), placed(above, row_high, high)
-        edge_ref[field, 0] = low
-        edge_ref[field, 1] = high
-
-    for k in range(5):
-        widen(k, [(4 * k + r, r, 12 + r) for r in range(4)])
-    for a in range(3):
-        widen(5 + a, [(VEL + 3 * a + r, 1 + r, 12 + r) for r in range(3)])
-    widen(8, [(DEN, 3, 12)])
-    for n, i in enumerate(near):
-        low, high = own_ref[9 + n, 0], own_ref[9 + n, 1]
-        if i in x_up:
-            low = placed(halo(POP + x_up.index(i))[0], 3, low)
-        if i in x_down:
-            high = placed(halo(POP + x_down.index(i))[1], 12, high)
-        edge_ref[9 + n, 0] = low
-        edge_ref[9 + n, 1] = high
+    edge_ref[...] = half_ref[...]
+
+    @pl.when(even)
+    def _():
+        widen(half_ref, first_row_ref.at[FACE:], False, edge_ref)
+
+    @pl.when(jnp.logical_not(even))
+    def _():
+        widen(half_ref, first_row_ref.at[FACE:], True, edge_ref)
 
     col_even = is_even("col")
     for h in range(2):
@@ -598,26 +629,31 @@
 
 
 def body(rows, cols, populations, order_tensor):
-    face, side = (FACE, 8, 128), (6, 8, 128)
-    base, first, second, pops = call(
+    side = (6, 8, 128)
+    base, own_edges, strips, pops = call(
         moments_kernel,
-        [(9, 8, 8, 128), face, face, (19, 64, 128)],
+        [(9, 8, 8, 128), (NEAR, 2, 8, 128), (STRIPS, 8, 128), (19, 64, 128)],
         [(5, 64, 128), pltpu.SemaphoreType.DMA((2,))],
         2_000_000,
         pltpu.with_memory_space_constraint(populations.reshape(19, 64, 128), pltpu.HBM),
         pltpu.with_memory_space_constraint(order_tensor.reshape(5, 64, 128), pltpu.HBM),
         from_hbm=True,
     )
-    recv_b = lax.ppermute(second, "row", swap(rows, 1))
-    recv_a = lax.ppermute(first, "row", swap(rows, 0))
-    own_edges = call(own_edges_kernel, [(NEAR, 2, 8, 128)], [], 2_000_000, base, pops)[0]
+    recv_strip = lax.ppermute(strips, "row", swap(rows, 1))
+    first_rows, second_rows = call(
+        rows_kernel, [(FACE + STRIPS, 8, 128), (PADDED, 8, 128)], [], 1_000_000, base, own_edges, pops
+    )
+    recv_a = lax.ppermute(first_rows, "row", swap(rows, 0))
+    recv_b = lax.ppermute(second_rows, "row", swap(rows, 1))
+    half_edges = call(
+        cross_chip_kernel, [(NEAR, 2, 8, 128)], [], CROSS_COST, own_edges, recv_strip
+    )[0]
     edges, first, second, third, fourth = call(
         column_message_kernel,
         [(NEAR, 2, 8, 128), side, side, side, side],
         [],
         1_000_000,
-        own_edges,
-        recv_b,
+        half_edges,
         recv_a,
     )
     down, up = crossing(cols)

time: 39.2 us -> 44.2 us (1.13)
  starting transfers between devices: 32.2 us -> 37.5 us
  waiting for transfers between devices: 0.9 us -> 0.16 us
    ppermute x1, starting transfers between devices: 5.96 us -> 9.38 us  [body(): recv_up = lax.ppermute(fourth_again, 'col', up)]
    ppermute x2 -> x3, starting transfers between devices: 18 us -> 19.9 us  [the longest x1 12.6 us: body(): recv_a = lax.ppermute(first_rows, 'row', swap(rows, 0))]
    ppermute x2 -> x3, waiting for transfers between devices: 0.74 us -> 0.01 us  [the longest x1 0.01 us: body(): recv_strip = lax.ppermute(strips, 'row', swap(rows, 1))]
    pallas_call x6 -> x7, Pallas kernels: 5.08 us -> 5.1 us  [call(): pl.pallas_call(kernel, out_shape=[jax.ShapeDtypeStruct(s, f32) for s in o...]
  transfers between devices with their start and end apart: 6 -> 7, of which waited for: 2 -> 1; matrix products, arithmetic and copies ran while one was open for 0% -> 0% of each run, Pallas kernels for 5% -> 5%
where the time goes in v5:
time: 44.2 us; the launch traced here: 43.6 us
  starting transfers between devices  37.5 us (85%)
  Pallas kernels  5.1 us (12%)
  between operations  0.75 us (2%)
    ppermute x1, starting transfers between devices, body(): recv_a = lax.ppermute(first_rows, 'row', swap(rows, 0))  12.6 us
    ppermute x1, starting transfers between devices, body(): recv_up = lax.ppermute(fourth_again, 'col', up)  9.38 us
    ppermute x1, starting transfers between devices, body(): recv_first = lax.ppermute(first, 'col', part(cols, False))  6.34 us
    ppermute x1, starting transfers between devices, body(): recv_strip = lax.ppermute(strips, 'row', swap(rows, 1))  5.36 us
    pallas_call x7, Pallas kernels, call(): pl.pallas_call(kernel, out_shape=[jax.ShapeDtypeStruct(s, f32) for s in o...  5.1 us
    ppermute x1, starting transfers between devices, body(): recv_b = lax.ppermute(second_rows, 'row', swap(rows, 1))  1.92 us
    ppermute x1, starting transfers between devices, body(): recv_down = lax.ppermute(second, 'col', down)  1.29 us
  transfers between devices with their start and end apart: 7, of which 1 were waited for; matrix products, arithmetic and copies ran while one was open for 0% of the time, Pallas kernels for 5%

profile of v5, /device:TPU:1, one launch (start us, length us, event | category | flops | bytes accessed | tf_op | source)
XLA Modules:
  0.0 43.6 jit_solution(13784770374149462616)
XLA Ops:
  0.6 1.6 %shard_map.41 = (f32[9,8,8,128]{3,2,1,0:T(8,128)S(1)}, f32[19,2,8,128]{3,2,1,0:T(8,128)S(1)}, f32[6,8,128]{2,1,0:T(8,128)S(1)}, f32[19,64,128]{2,1,0:T(8,128)S(1)}) custom-call(f32[19,64,128]{2,1,0:T(8,128)} %bitcast.4, f32[5,64,128]{2,1,0:T(8,128)} %bitcast.5), custom_call_target="tpu_custom_call" | custom-call | flops 2000000 | bytes 1884160 | tf_op jit(solution)/shard_map/pallas_call | solution.py:601
  2.2 5.4 %collective-permute-start = (f32[6,8,128]{2,1,0:T(8,128)S(1)}, f32[6,8,128]{2,1,0:T(8,128)S(1)}, u32[]{:S(2)}, u32[]{:S(2)}) collective-permute-start(f32[6,8,128]{2,1,0:T(8,128)S(1)} %get-tuple-element.24), channel_id=1, source_target_pairs={{0,1008},{16,32},{32,16},{48,64},{64,48},{80,96},{96,80},{112,128}... | collective-permute-start | bytes 73736 | tf_op jit(solution)/shard_map/ppermute | solution.py:642
  7.6 0.1 shard_map.43
  7.7 12.6 %collective-permute-start.1 = (f32[41,8,128]{2,1,0:T(8,128)S(1)}, f32[41,8,128]{2,1,0:T(8,128)S(1)}, u32[]{:S(2)}, u32[]{:S(2)}) collective-permute-start(f32[41,8,128]{2,1,0:T(8,128)S(1)} %get-tuple-element.27), channel_id=1, source_target_pairs={{0,16},{16,0},{32,48},{48,32},{64,80},{80,64},{96,112},{112,96},{1... | collective-permute-start | bytes 503816 | tf_op jit(solution)/shard_map/ppermute | solution.py:646
  20.3 1.9 %collective-permute-start.2 = (f32[42,8,128]{2,1,0:T(8,128)S(1)}, f32[42,8,128]{2,1,0:T(8,128)S(1)}, u32[]{:S(2)}, u32[]{:S(2)}) collective-permute-start(f32[42,8,128]{2,1,0:T(8,128)S(1)} %get-tuple-element.29), channel_id=1, source_target_pairs={{0,1008},{16,32},{32,16},{48,64},{64,48},{80,96},{96,80},{112,128}... | collective-permute-start | bytes 516104 | tf_op jit(solution)/shard_map/ppermute | solution.py:647
  22.2 0.0 collective-permute-done.strip_ref
  22.2 0.1 shard_map.42.half_ref
  22.3 0.0 collective-permute-done.1.first_row_ref.recv_a
  22.3 0.2 shard_map.44
  22.5 1.3 %collective-permute-start.3 = (f32[6,8,128]{2,1,0:T(8,128)S(1)}, f32[6,8,128]{2,1,0:T(8,128)S(1)}, u32[]{:S(2)}, u32[]{:S(2)}) collective-permute-start(f32[6,8,128]{2,1,0:T(8,128)S(1)} %get-tuple-element.36), channel_id=1, source_target_pairs={{2,1},{3,4},{6,5},{7,8},{10,9},{11,12},{14,13},{15,0},{18,17},{19,... | collective-permute-start | bytes 73736 | tf_op jit(solution)/shard_map/ppermute | solution.py:660
  23.8 6.3 %collective-permute-start.4 = (f32[6,8,128]{2,1,0:T(8,128)S(1)}, f32[6,8,128]{2,1,0:T(8,128)S(1)}, u32[]{:S(2)}, u32[]{:S(2)}) collective-permute-start(f32[6,8,128]{2,1,0:T(8,128)S(1)} %get-tuple-element.37), channel_id=1, source_target_pairs={{0,1},{1,0},{4,5},{5,4},{8,9},{9,8},{12,13},{13,12},{16,17},{17,16... | collective-permute-start | bytes 73736 | tf_op jit(solution)/shard_map/ppermute | solution.py:661
  30.2 0.0 collective-permute-done.2.recv_b
  30.2 1.5 %shard_map.45 = (f32[19,10,8,128]{3,2,1,0:T(8,128)S(1)}, f32[5,8,8,128]{3,2,1,0:T(8,128)S(1)}, f32[9,2,8,128]{3,2,1,0:T(8,128)S(1)}, f32[6,8,128]{2,1,0:T(8,128)S(1)}, f32[6,8,128]{2,1,0:T(8,128)S(1)}) custom-call(f32[9,8,8,128]{3,2,1,0:T(8,128)S(1)} %get-tuple-element.25.base_ref, f32[42,8,128]{2,1,0:T(8,128)S(1)} %collective-permute-done.2.recv_b, ...), custom_call_target="tpu_custom_call" | custom-call | flops 20000000 | bytes 2371584 | tf_op jit(solution)/shard_map/pallas_call | solution.py:601
  31.7 9.4 %collective-permute-start.5 = (f32[6,8,128]{2,1,0:T(8,128)S(1)}, f32[6,8,128]{2,1,0:T(8,128)S(1)}, u32[]{:S(2)}, u32[]{:S(2)}) collective-permute-start(f32[6,8,128]{2,1,0:T(8,128)S(1)} %get-tuple-element.38), channel_id=1, source_target_pairs={{1,2},{4,3},{5,6},{8,7},{9,10},{12,11},{13,14},{0,15},{17,18},{20,... | collective-permute-start | bytes 73736 | tf_op jit(solution)/shard_map/ppermute | solution.py:676
  41.1 0.7 %collective-permute-start.6 = (f32[6,8,128]{2,1,0:T(8,128)S(1)}, f32[6,8,128]{2,1,0:T(8,128)S(1)}, u32[]{:S(2)}, u32[]{:S(2)}) collective-permute-start(f32[6,8,128]{2,1,0:T(8,128)S(1)} %get-tuple-element.39), channel_id=1, source_target_pairs={{2,3},{3,2},{6,7},{7,6},{10,11},{11,10},{14,15},{15,14},{18,19},{1... | collective-permute-start | bytes 73736 | tf_op jit(solution)/shard_map/ppermute | solution.py:677
  41.8 0.1 shard_map.46
  41.9 0.0 collective-permute-done.3.recv_down
  41.9 0.0 collective-permute-done.4.recv_first
  41.9 0.1 collective-permute-done.5.recv_up
  42.0 0.0 collective-permute-done.6.recv_last
  42.0 1.5 %shard_map.47 = (f32[19,64,128]{2,1,0:T(8,128)}, f32[5,64,128]{2,1,0:T(8,128)}) custom-call(f32[19,2,8,128]{3,2,1,0:T(8,128)S(1)} %get-tuple-element.28.edge_ref, f32[9,2,8,128]{3,2,1,0:T(8,128)S(1)} %get-tuple-element.35.far_ref, f32[6,8,128]{2,1,0:T(8,128)S(1)} %collective-permute-done.3.recv_down, f32[6,8,128]{2,1,0:T(8,128)S(1)} %collective-permute-done.4.recv_first, ...), custom_call_target="tpu_custom_call" | custom-call | flops 8000000 | bytes 2056192 | tf_op jit(solution)/shard_map/pallas_call | solution.py:601
Async XLA Ops:
  2.2 20.0 %collective-permute-start = (f32[6,8,128]{2,1,0:T(8,128)S(1)}, f32[6,8,128]{2,1,0:T(8,128)S(1)}, u32[]{:S(2)}, u32[]{:S(2)}) collective-permute-start(f32[6,8,128]{2,1,0:T(8,128)S(1)} %get-tuple-element.24), channel_id=1, source_target_pairs={{0,1008},{16,32},{32,16},{48,64},{64,48},{80,96},{96,80},{112,128}... | collective-permute-start | bytes 73736 | tf_op jit(solution)/shard_map/ppermute | solution.py:642
  7.7 14.6 %collective-permute-start.1 = (f32[41,8,128]{2,1,0:T(8,128)S(1)}, f32[41,8,128]{2,1,0:T(8,128)S(1)}, u32[]{:S(2)}, u32[]{:S(2)}) collective-permute-start(f32[41,8,128]{2,1,0:T(8,128)S(1)} %get-tuple-element.27), channel_id=1, source_target_pairs={{0,16},{16,0},{32,48},{48,32},{64,80},{80,64},{96,112},{112,96},{1... | collective-permute-start | bytes 503816 | tf_op jit(solution)/shard_map/ppermute | solution.py:646
  20.3 9.9 %collective-permute-start.2 = (f32[42,8,128]{2,1,0:T(8,128)S(1)}, f32[42,8,128]{2,1,0:T(8,128)S(1)}, u32[]{:S(2)}, u32[]{:S(2)}) collective-permute-start(f32[42,8,128]{2,1,0:T(8,128)S(1)} %get-tuple-element.29), channel_id=1, source_target_pairs={{0,1008},{16,32},{32,16},{48,64},{64,48},{80,96},{96,80},{112,128}... | collective-permute-start | bytes 516104 | tf_op jit(solution)/shard_map/ppermute | solution.py:647
  22.5 19.3 %collective-permute-start.3 = (f32[6,8,128]{2,1,0:T(8,128)S(1)}, f32[6,8,128]{2,1,0:T(8,128)S(1)}, u32[]{:S(2)}, u32[]{:S(2)}) collective-permute-start(f32[6,8,128]{2,1,0:T(8,128)S(1)} %get-tuple-element.36), channel_id=1, source_target_pairs={{2,1},{3,4},{6,5},{7,8},{10,9},{11,12},{14,13},{15,0},{18,17},{19,... | collective-permute-start | bytes 73736 | tf_op jit(solution)/shard_map/ppermute | solution.py:660
  23.8 18.0 %collective-permute-start.4 = (f32[6,8,128]{2,1,0:T(8,128)S(1)}, f32[6,8,128]{2,1,0:T(8,128)S(1)}, u32[]{:S(2)}, u32[]{:S(2)}) collective-permute-start(f32[6,8,128]{2,1,0:T(8,128)S(1)} %get-tuple-element.37), channel_id=1, source_target_pairs={{0,1},{1,0},{4,5},{5,4},{8,9},{9,8},{12,13},{13,12},{16,17},{17,16... | collective-permute-start | bytes 73736 | tf_op jit(solution)/shard_map/ppermute | solution.py:661
  31.7 10.3 %collective-permute-start.5 = (f32[6,8,128]{2,1,0:T(8,128)S(1)}, f32[6,8,128]{2,1,0:T(8,128)S(1)}, u32[]{:S(2)}, u32[]{:S(2)}) collective-permute-start(f32[6,8,128]{2,1,0:T(8,128)S(1)} %get-tuple-element.38), channel_id=1, source_target_pairs={{1,2},{4,3},{5,6},{8,7},{9,10},{12,11},{13,14},{0,15},{17,18},{20,... | collective-permute-start | bytes 73736 | tf_op jit(solution)/shard_map/ppermute | solution.py:676
  41.1 0.9 %collective-permute-start.6 = (f32[6,8,128]{2,1,0:T(8,128)S(1)}, f32[6,8,128]{2,1,0:T(8,128)S(1)}, u32[]{:S(2)}, u32[]{:S(2)}) collective-permute-start(f32[6,8,128]{2,1,0:T(8,128)S(1)} %get-tuple-element.39), channel_id=1, source_target_pairs={{2,3},{3,2},{6,7},{7,6},{10,11},{11,10},{14,15},{15,14},{18,19},{1... | collective-permute-start | bytes 73736 | tf_op jit(solution)/shard_map/ppermute | solution.py:677

commit v6 on v4

--- a/solution.py
+++ b/solution.py
@@ -213,7 +213,7 @@
             base_ref[k, x] = order_ref[k, pl.ds(x, 8, stride=8), :]
         return carry
 
-    lax.fori_loop(0, 8, row, 0)
+    lax.fori_loop(0, 8, row, 0, unroll=8)
     even = is_even("row")
     for out, high in ((first_ref, even), (second_ref, jnp.logical_not(even))):
 
@@ -317,7 +317,7 @@
     return lax.rem(lax.axis_index("col"), 4) >= 2
 
 
-def early_main_kernel(base_ref, recv_b, recv_a, pop_ref, third_ref, fourth_ref, *rest):
+def early_main_kernel(base_ref, recv_b, recv_a, pop_ref, third_ref, fourth_ref, _, *rest):
     outputs, scratch = rest[:3], rest[5:]
     rest[3][...] = third_ref[...]
     rest[4][...] = fourth_ref[...]
@@ -622,7 +622,10 @@
     )
     down, up = crossing(cols)
     recv_down = lax.ppermute(second, "col", down)
-    recv_first = lax.ppermute(first, "col", part(cols, False))
+    late = lax.rem(lax.axis_index("col"), 4) >= 2
+    recv_first = lax.cond(
+        late, lambda m: m, lambda m: lax.ppermute(m, "col", part(cols, False)), first
+    )
     blocks = [(19, 10, 8, 128), (5, 8, 8, 128), (FAR, 2, 8, 128)]
     scratch = [(5, 16, 8, 128)] * 3 + [(3, 14, 8, 128), (10, 8, 128)]
     *half_done, third_again, fourth_again = call(
@@ -636,9 +639,12 @@
         pops,
         third,
         fourth,
+        recv_first,
     )
     recv_up = lax.ppermute(fourth_again, "col", up)
-    recv_last = lax.ppermute(third_again, "col", part(cols, True))
+    recv_last = lax.cond(
+        late, lambda m: lax.ppermute(m, "col", part(cols, True)), lambda m: m, third_again
+    )
     moved, relaxed, far_edges = call(
         late_main_kernel,
         blocks,

time: 39.2 us -> 38.4 us (0.980)
  starting transfers between devices: 32.2 us -> 28.7 us
  waiting for transfers between devices: 0.9 us -> 3.72 us
    ppermute x1, starting transfers between devices: 5.96 us -> 3.14 us  [body(): recv_up = lax.ppermute(fourth_again, 'col', up)]
    ppermute x2 -> x1, waiting for transfers between devices: 0.01 us -> 2.18 us  [body(): lax.ppermute(m, 'col', part(cols, False))]
    ppermute x1, waiting for transfers between devices: 0.14 us -> 0.81 us  [body(): recv_up = lax.ppermute(fourth_again, 'col', up)]
    ppermute x2 -> x1, starting transfers between devices: 6.97 us -> 6.31 us  [body(): lax.ppermute(m, 'col', part(cols, False))]
  transfers between devices with their start and end apart: 6 -> 5, of which waited for: 2 -> 3; matrix products, arithmetic and copies ran while one was open for 0% -> 0% of each run, Pallas kernels for 5% -> 5%
where the time goes in v6:
time: 38.4 us; the launch traced here: 38.1 us
  starting transfers between devices  28.7 us (75%)
  Pallas kernels  4.91 us (13%)
  waiting for transfers between devices  3.72 us (10%)
  between operations  0.72 us (2%)
    ppermute x1, starting transfers between devices, body(): recv_a = lax.ppermute(first, 'row', swap(rows, 0))  12.6 us
    ppermute x1, starting transfers between devices, body(): lax.ppermute(m, 'col', part(cols, False))  6.31 us
    ppermute x1, starting transfers between devices, body(): recv_b = lax.ppermute(second, 'row', swap(rows, 1))  5.39 us
    pallas_call x6, Pallas kernels, call(): pl.pallas_call(kernel, out_shape=[jax.ShapeDtypeStruct(s, f32) for s in o...  4.91 us
    ppermute x1, starting transfers between devices, body(): recv_up = lax.ppermute(fourth_again, 'col', up)  3.14 us
    ppermute x1, waiting for transfers between devices, body(): lax.ppermute(m, 'col', part(cols, False))  2.18 us
    ppermute x1, starting transfers between devices, body(): recv_down = lax.ppermute(second, 'col', down)  1.29 us
    ppermute x1, waiting for transfers between devices, body(): recv_up = lax.ppermute(fourth_again, 'col', up)  0.81 us
  transfers between devices with their start and end apart: 5, of which 3 were waited for; matrix products, arithmetic and copies ran while one was open for 0% of the time, Pallas kernels for 5%

profile of v6, /device:TPU:1, one launch (start us, length us, event | category | flops | bytes accessed | tf_op | source)
XLA Modules:
  0.0 38.1 jit_solution(401417150830744218)
XLA Ops:
  0.6 1.3 %shard_map.41 = (f32[9,8,8,128]{3,2,1,0:T(8,128)S(1)}, f32[35,8,128]{2,1,0:T(8,128)S(1)}, f32[35,8,128]{2,1,0:T(8,128)S(1)}, f32[19,64,128]{2,1,0:T(8,128)S(1)}) custom-call(f32[19,64,128]{2,1,0:T(8,128)} %bitcast.4, f32[5,64,128]{2,1,0:T(8,128)} %bitcast.5), custom_call_target="tpu_custom_call" | custom-call | flops 2000000 | bytes 1990656 | tf_op jit(solution)/shard_map/pallas_call | solution.py:570
  2.0 5.4 %collective-permute-start.2 = (f32[35,8,128]{2,1,0:T(8,128)S(1)}, f32[35,8,128]{2,1,0:T(8,128)S(1)}, u32[]{:S(2)}, u32[]{:S(2)}) collective-permute-start(f32[35,8,128]{2,1,0:T(8,128)S(1)} %get-tuple-element.33), channel_id=1, source_target_pairs={{0,1008},{16,32},{32,16},{48,64},{64,48},{80,96},{96,80},{112,128}... | collective-permute-start | bytes 430088 | tf_op jit(solution)/shard_map/ppermute | solution.py:611
  7.4 12.6 %collective-permute-start.3 = (f32[35,8,128]{2,1,0:T(8,128)S(1)}, f32[35,8,128]{2,1,0:T(8,128)S(1)}, u32[]{:S(2)}, u32[]{:S(2)}) collective-permute-start(f32[35,8,128]{2,1,0:T(8,128)S(1)} %get-tuple-element.34), channel_id=1, source_target_pairs={{0,16},{16,0},{32,48},{48,32},{64,80},{80,64},{96,112},{112,96},{1... | collective-permute-start | bytes 430088 | tf_op jit(solution)/shard_map/ppermute | solution.py:612
  20.0 0.2 shard_map.42.own_ref
  20.2 0.0 collective-permute-done.2.recv_b
  20.2 0.7 %collective-permute-done.3.recv_a = f32[35,8,128]{2,1,0:T(8,128)S(1)} collective-permute-done((f32[35,8,128]{2,1,0:T(8,128)S(1)}, f32[35,8,128]{2,1,0:T(8,128)S(1)}, u32[]{:S(2)}, u32[]{:S(2)}) %collective-permute-start.3) | collective-permute-done | bytes 143392 | tf_op jit(solution)/shard_map/ppermute | solution.py:612
  21.0 0.2 shard_map.43
  21.2 1.3 %collective-permute-start.4 = (f32[6,8,128]{2,1,0:T(8,128)S(1)}, f32[6,8,128]{2,1,0:T(8,128)S(1)}, u32[]{:S(2)}, u32[]{:S(2)}) collective-permute-start(f32[6,8,128]{2,1,0:T(8,128)S(1)} %get-tuple-element.43), channel_id=1, source_target_pairs={{2,1},{3,4},{6,5},{7,8},{10,9},{11,12},{14,13},{15,0},{18,17},{19,... | collective-permute-start | bytes 73736 | tf_op jit(solution)/shard_map/ppermute | solution.py:624
  22.5 8.5 %conditional.2 = (f32[6,8,128]{2,1,0:T(8,128)S(1)}) conditional(s32[]{:T(128)} %convert_element_type.4, f32[6,8,128]{2,1,0:T(8,128)S(1)} %get-tuple-element.38, f32[6,8,128]{2,1,0:T(8,128)S(1)} %get-tuple-element.38), branch_computations={%region_0.0_spmd, %region_1.0_spmd} | conditional | bytes 98352 | solution.py:626
  22.5 6.3 %collective-permute-start = (f32[6,8,128]{2,1,0:T(8,128)S(1)}, f32[6,8,128]{2,1,0:T(8,128)S(1)}, u32[]{:S(2)}, u32[]{:S(2)}) collective-permute-start(f32[6,8,128]{2,1,0:T(8,128)S(1)} %param), channel_id=1, source_target_pairs={{0,1},{1,0},{4,5},{5,4},{8,9},{9,8},{12,13},{13,12},{16,17},{17,16... | collective-permute-start | bytes 73736 | tf_op jit(solution)/shard_map/cond/branch_0_fun/ppermute | solution.py:627
  28.8 2.2 %collective-permute-done = f32[6,8,128]{2,1,0:T(8,128)S(1)} collective-permute-done((f32[6,8,128]{2,1,0:T(8,128)S(1)}, f32[6,8,128]{2,1,0:T(8,128)S(1)}, u32[]{:S(2)}, u32[]{:S(2)}) %collective-permute-start) | collective-permute-done | bytes 24608 | tf_op jit(solution)/shard_map/cond/branch_0_fun/ppermute | solution.py:627
  31.0 1.5 %shard_map.44 = (f32[19,10,8,128]{3,2,1,0:T(8,128)S(1)}, f32[5,8,8,128]{3,2,1,0:T(8,128)S(1)}, f32[9,2,8,128]{3,2,1,0:T(8,128)S(1)}, f32[6,8,128]{2,1,0:T(8,128)S(1)}, f32[6,8,128]{2,1,0:T(8,128)S(1)}) custom-call(f32[9,8,8,128]{3,2,1,0:T(8,128)S(1)} %get-tuple-element.31.base_ref, f32[35,8,128]{2,1,0:T(8,128)S(1)} %collective-permute-done.2.recv_b, ...), custom_call_target="tpu_custom_call" | custom-call | flops 20000000 | bytes 2342912 | tf_op jit(solution)/shard_map/pallas_call | solution.py:570
  32.5 3.1 %collective-permute-start.5 = (f32[6,8,128]{2,1,0:T(8,128)S(1)}, f32[6,8,128]{2,1,0:T(8,128)S(1)}, u32[]{:S(2)}, u32[]{:S(2)}) collective-permute-start(f32[6,8,128]{2,1,0:T(8,128)S(1)} %get-tuple-element.44), channel_id=1, source_target_pairs={{1,2},{4,3},{5,6},{8,7},{9,10},{12,11},{13,14},{0,15},{17,18},{20,... | collective-permute-start | bytes 73736 | tf_op jit(solution)/shard_map/ppermute | solution.py:644
  35.7 0.1 shard_map.45
  35.8 0.0 collective-permute-done.4.recv_down
  35.8 0.8 %collective-permute-done.5.recv_up = f32[6,8,128]{2,1,0:T(8,128)S(1)} collective-permute-done((f32[6,8,128]{2,1,0:T(8,128)S(1)}, f32[6,8,128]{2,1,0:T(8,128)S(1)}, u32[]{:S(2)}, u32[]{:S(2)}) %collective-permute-start.5) | collective-permute-done | bytes 24608 | tf_op jit(solution)/shard_map/ppermute | solution.py:644
  36.6 1.5 %shard_map.46 = (f32[19,64,128]{2,1,0:T(8,128)}, f32[5,64,128]{2,1,0:T(8,128)}) custom-call(f32[19,2,8,128]{3,2,1,0:T(8,128)S(1)} %get-tuple-element.35.edge_ref, f32[9,2,8,128]{3,2,1,0:T(8,128)S(1)} %get-tuple-element.42.far_ref, f32[6,8,128]{2,1,0:T(8,128)S(1)} %collective-permute-done.4.recv_down, f32[6,8,128]{2,1,0:T(8,128)S(1)} %get-tuple-element.50._.recv_first, ...), custom_call_target="tpu_custom_call" | custom-call | flops 8000000 | bytes 2056192 | tf_op jit(solution)/shard_map/pallas_call | solution.py:570
  (1 shorter events, 0.0 us)
Async XLA Ops:
  2.0 18.2 %collective-permute-start.2 = (f32[35,8,128]{2,1,0:T(8,128)S(1)}, f32[35,8,128]{2,1,0:T(8,128)S(1)}, u32[]{:S(2)}, u32[]{:S(2)}) collective-permute-start(f32[35,8,128]{2,1,0:T(8,128)S(1)} %get-tuple-element.33), channel_id=1, source_target_pairs={{0,1008},{16,32},{32,16},{48,64},{64,48},{80,96},{96,80},{112,128}... | collective-permute-start | bytes 430088 | tf_op jit(solution)/shard_map/ppermute | solution.py:611
  7.4 13.6 %collective-permute-start.3 = (f32[35,8,128]{2,1,0:T(8,128)S(1)}, f32[35,8,128]{2,1,0:T(8,128)S(1)}, u32[]{:S(2)}, u32[]{:S(2)}) collective-permute-start(f32[35,8,128]{2,1,0:T(8,128)S(1)} %get-tuple-element.34), channel_id=1, source_target_pairs={{0,16},{16,0},{32,48},{48,32},{64,80},{80,64},{96,112},{112,96},{1... | collective-permute-start | bytes 430088 | tf_op jit(solution)/shard_map/ppermute | solution.py:612
  21.2 14.6 %collective-permute-start.4 = (f32[6,8,128]{2,1,0:T(8,128)S(1)}, f32[6,8,128]{2,1,0:T(8,128)S(1)}, u32[]{:S(2)}, u32[]{:S(2)}) collective-permute-start(f32[6,8,128]{2,1,0:T(8,128)S(1)} %get-tuple-element.43), channel_id=1, source_target_pairs={{2,1},{3,4},{6,5},{7,8},{10,9},{11,12},{14,13},{15,0},{18,17},{19,... | collective-permute-start | bytes 73736 | tf_op jit(solution)/shard_map/ppermute | solution.py:624
  22.5 8.5 %collective-permute-start = (f32[6,8,128]{2,1,0:T(8,128)S(1)}, f32[6,8,128]{2,1,0:T(8,128)S(1)}, u32[]{:S(2)}, u32[]{:S(2)}) collective-permute-start(f32[6,8,128]{2,1,0:T(8,128)S(1)} %param), channel_id=1, source_target_pairs={{0,1},{1,0},{4,5},{5,4},{8,9},{9,8},{12,13},{13,12},{16,17},{17,16... | collective-permute-start | bytes 73736 | tf_op jit(solution)/shard_map/cond/branch_0_fun/ppermute | solution.py:627
  32.5 4.1 %collective-permute-start.5 = (f32[6,8,128]{2,1,0:T(8,128)S(1)}, f32[6,8,128]{2,1,0:T(8,128)S(1)}, u32[]{:S(2)}, u32[]{:S(2)}) collective-permute-start(f32[6,8,128]{2,1,0:T(8,128)S(1)} %get-tuple-element.44), channel_id=1, source_target_pairs={{1,2},{4,3},{5,6},{8,7},{9,10},{12,11},{13,14},{0,15},{17,18},{20,... | collective-permute-start | bytes 73736 | tf_op jit(solution)/shard_map/ppermute | solution.py:644

commit v7 on v6

--- a/solution.py
+++ b/solution.py
@@ -439,13 +439,23 @@
             stream(i, value, x + 1)
 
 
-def edge_kernel(
+def early_edge_kernel(edge_ref, far_ref, recv_down, recv_first, moved_ref, order_ref, *rest):
+    @pl.when(jnp.logical_not(is_late()))
+    def _():
+        edge_block(edge_ref, far_ref, recv_down, recv_first, moved_ref, order_ref, *rest)
+
+
+def late_edge_kernel(edge_ref, far_ref, recv_up, recv_last, moved_ref, order_ref, *rest):
+    @pl.when(is_late())
+    def _():
+        edge_block(edge_ref, far_ref, recv_up, recv_last, moved_ref, order_ref, *rest[2:])
+
+
+def edge_block(
     edge_ref,
     far_ref,
-    recv_down,
-    recv_first,
-    recv_up,
-    recv_last,
+    recv_b,
+    recv_a,
     moved_ref,
     order_ref,
     new_pop,
@@ -458,12 +468,10 @@
     sems,
 ):
     even = is_even("col")
-    late = is_late()
     slot, lane = slots(), lanes()
 
     def columns(j):
-        a = jnp.where(late, recv_last[j], recv_first[j])
-        b = jnp.where(late, recv_up[j], recv_down[j])
+        a, b = recv_a[j], recv_b[j]
         return jnp.where(even, b, a), jnp.where(even, a, b)
 
     for h in range(2):
@@ -565,12 +573,12 @@
         copy.wait()
 
 
-def call(kernel, out_shapes, scratch, flops, *args, from_hbm=False, to_hbm=False):
+def call(kernel, out_shapes, scratch, flops, *args, hbm_args=(), to_hbm=False, aliases=None):
     whole, outside = (pl.BlockSpec(memory_space=m) for m in (pltpu.VMEM, pltpu.HBM))
     return pl.pallas_call(
         kernel,
         out_shape=[jax.ShapeDtypeStruct(s, f32) for s in out_shapes],
-        in_specs=[outside if from_hbm else whole] * len(args),
+        in_specs=[outside if n in hbm_args else whole for n in range(len(args))],
         out_specs=[outside if to_hbm else whole] * len(out_shapes),
         scratch_shapes=[pltpu.VMEM(s, f32) if isinstance(s, tuple) else s for s in scratch],
         cost_estimate=pl.CostEstimate(
@@ -578,6 +586,7 @@
             bytes_accessed=4 * sum(math.prod(s) for s in out_shapes) + sum(4 * a.size for a in args),
             transcendentals=0,
         ),
+        input_output_aliases=aliases or {},
         compiler_params=pltpu.CompilerParams(vmem_limit_bytes=12 * 1024 * 1024),
     )(*args)
 
@@ -606,7 +615,7 @@
         2_000_000,
         pltpu.with_memory_space_constraint(populations.reshape(19, 64, 128), pltpu.HBM),
         pltpu.with_memory_space_constraint(order_tensor.reshape(5, 64, 128), pltpu.HBM),
-        from_hbm=True,
+        hbm_args=(0, 1),
     )
     recv_b = lax.ppermute(second, "row", swap(rows, 1))
     recv_a = lax.ppermute(first, "row", swap(rows, 0))
@@ -656,27 +665,42 @@
         pops,
         *half_done,
     )
-    new_pops, new_order = call(
-        edge_kernel,
-        [(19, 64, 128), (5, 64, 128)],
-        [
-            (28, 4, 8, 128),
-            (5, 4, 8, 128),
-            (5, 4, 8, 128),
-            (19, 64, 128),
-            (5, 64, 128),
-            pltpu.SemaphoreType.DMA((len(CHUNKS) + 1,)),
-        ],
+    results = [(19, 64, 128), (5, 64, 128)]
+    scratch = [
+        (28, 4, 8, 128),
+        (5, 4, 8, 128),
+        (5, 4, 8, 128),
+        *results,
+        pltpu.SemaphoreType.DMA((len(CHUNKS) + 1,)),
+    ]
+    half_done = call(
+        early_edge_kernel,
+        results,
+        scratch,
         8_000_000,
         edges,
         far_edges,
         recv_down,
         recv_first,
+        moved,
+        relaxed,
+        to_hbm=True,
+    )
+    new_pops, new_order = call(
+        late_edge_kernel,
+        results,
+        scratch,
+        8_000_000,
+        edges,
+        far_edges,
         recv_up,
         recv_last,
         moved,
         relaxed,
+        *half_done,
+        hbm_args=(6, 7),
         to_hbm=True,
+        aliases={6: 0, 7: 1},
     )
     return new_pops.reshape(populations.shape), new_order.reshape(order_tensor.shape)
 

time: 38.4 us -> 37.6 us (0.979)
  waiting for transfers between devices: 3.72 us -> 2.92 us
    ppermute x1, waiting for transfers between devices: 0.81 us -> 0.01 us  [body(): recv_up = lax.ppermute(fourth_again, 'col', up)]
    pallas_call x6 -> x7, Pallas kernels: 4.91 us -> 4.99 us  [call(): pl.pallas_call(kernel, out_shape=[jax.ShapeDtypeStruct(s, f32) for s in o...]
  transfers between devices with their start and end apart: 5 -> 5, of which waited for: 3 -> 2; matrix products, arithmetic and copies ran while one was open for 0% -> 0% of each run, Pallas kernels for 5% -> 9%
where the time goes in v7:
time: 37.6 us; the launch traced here: 37.4 us
  starting transfers between devices  28.7 us (76%)
  Pallas kernels  4.99 us (13%)
  waiting for transfers between devices  2.92 us (8%)
  between operations  0.74 us (2%)
    ppermute x1, starting transfers between devices, body(): recv_a = lax.ppermute(first, 'row', swap(rows, 0))  12.6 us
    ppermute x1, starting transfers between devices, body(): lax.ppermute(m, 'col', part(cols, False))  6.31 us
    ppermute x1, starting transfers between devices, body(): recv_b = lax.ppermute(second, 'row', swap(rows, 1))  5.39 us
    pallas_call x7, Pallas kernels, call(): pl.pallas_call(kernel, out_shape=[jax.ShapeDtypeStruct(s, f32) for s in o...  4.99 us
    ppermute x1, starting transfers between devices, body(): recv_up = lax.ppermute(fourth_again, 'col', up)  3.14 us
    ppermute x1, waiting for transfers between devices, body(): lax.ppermute(m, 'col', part(cols, False))  2.18 us
    ppermute x1, starting transfers between devices, body(): recv_down = lax.ppermute(second, 'col', down)  1.29 us
  transfers between devices with their start and end apart: 5, of which 2 were waited for; matrix products, arithmetic and copies ran while one was open for 0% of the time, Pallas kernels for 9%

profile of v7, /device:TPU:1, one launch (start us, length us, event | category | flops | bytes accessed | tf_op | source)
XLA Modules:
  0.0 37.4 jit_solution(972088895471722571)
XLA Ops:
  0.6 1.3 %shard_map.41 = (f32[9,8,8,128]{3,2,1,0:T(8,128)S(1)}, f32[35,8,128]{2,1,0:T(8,128)S(1)}, f32[35,8,128]{2,1,0:T(8,128)S(1)}, f32[19,64,128]{2,1,0:T(8,128)S(1)}) custom-call(f32[19,64,128]{2,1,0:T(8,128)} %bitcast.4, f32[5,64,128]{2,1,0:T(8,128)} %bitcast.6), custom_call_target="tpu_custom_call" | custom-call | flops 2000000 | bytes 1990656 | tf_op jit(solution)/shard_map/pallas_call | solution.py:578
  2.0 5.4 %collective-permute-start.2 = (f32[35,8,128]{2,1,0:T(8,128)S(1)}, f32[35,8,128]{2,1,0:T(8,128)S(1)}, u32[]{:S(2)}, u32[]{:S(2)}) collective-permute-start(f32[35,8,128]{2,1,0:T(8,128)S(1)} %get-tuple-element.35), channel_id=1, source_target_pairs={{0,1008},{16,32},{32,16},{48,64},{64,48},{80,96},{96,80},{112,128}... | collective-permute-start | bytes 430088 | tf_op jit(solution)/shard_map/ppermute | solution.py:620
  7.4 12.6 %collective-permute-start.3 = (f32[35,8,128]{2,1,0:T(8,128)S(1)}, f32[35,8,128]{2,1,0:T(8,128)S(1)}, u32[]{:S(2)}, u32[]{:S(2)}) collective-permute-start(f32[35,8,128]{2,1,0:T(8,128)S(1)} %get-tuple-element.36), channel_id=1, source_target_pairs={{0,16},{16,0},{32,48},{48,32},{64,80},{80,64},{96,112},{112,96},{1... | collective-permute-start | bytes 430088 | tf_op jit(solution)/shard_map/ppermute | solution.py:621
  20.0 0.2 shard_map.42.own_ref
  20.2 0.0 collective-permute-done.2.recv_b
  20.2 0.7 %collective-permute-done.3.recv_a = f32[35,8,128]{2,1,0:T(8,128)S(1)} collective-permute-done((f32[35,8,128]{2,1,0:T(8,128)S(1)}, f32[35,8,128]{2,1,0:T(8,128)S(1)}, u32[]{:S(2)}, u32[]{:S(2)}) %collective-permute-start.3) | collective-permute-done | bytes 143392 | tf_op jit(solution)/shard_map/ppermute | solution.py:621
  21.0 0.2 shard_map.43
  21.2 1.3 %collective-permute-start.5 = (f32[6,8,128]{2,1,0:T(8,128)S(1)}, f32[6,8,128]{2,1,0:T(8,128)S(1)}, u32[]{:S(2)}, u32[]{:S(2)}) collective-permute-start(f32[6,8,128]{2,1,0:T(8,128)S(1)} %get-tuple-element.49), channel_id=1, source_target_pairs={{2,1},{3,4},{6,5},{7,8},{10,9},{11,12},{14,13},{15,0},{18,17},{19,... | collective-permute-start | bytes 73736 | tf_op jit(solution)/shard_map/ppermute | solution.py:633
  22.5 8.5 %conditional.2 = (f32[6,8,128]{2,1,0:T(8,128)S(1)}) conditional(s32[]{:T(128)} %convert_element_type.4, f32[6,8,128]{2,1,0:T(8,128)S(1)} %get-tuple-element.40, f32[6,8,128]{2,1,0:T(8,128)S(1)} %get-tuple-element.40), branch_computations={%region_0.0_spmd, %region_1.0_spmd} | conditional | bytes 98352 | solution.py:635
  22.5 6.3 %collective-permute-start = (f32[6,8,128]{2,1,0:T(8,128)S(1)}, f32[6,8,128]{2,1,0:T(8,128)S(1)}, u32[]{:S(2)}, u32[]{:S(2)}) collective-permute-start(f32[6,8,128]{2,1,0:T(8,128)S(1)} %param), channel_id=1, source_target_pairs={{0,1},{1,0},{4,5},{5,4},{8,9},{9,8},{12,13},{13,12},{16,17},{17,16... | collective-permute-start | bytes 73736 | tf_op jit(solution)/shard_map/cond/branch_0_fun/ppermute | solution.py:636
  28.8 2.2 %collective-permute-done = f32[6,8,128]{2,1,0:T(8,128)S(1)} collective-permute-done((f32[6,8,128]{2,1,0:T(8,128)S(1)}, f32[6,8,128]{2,1,0:T(8,128)S(1)}, u32[]{:S(2)}, u32[]{:S(2)}) %collective-permute-start) | collective-permute-done | bytes 24608 | tf_op jit(solution)/shard_map/cond/branch_0_fun/ppermute | solution.py:636
  31.0 1.5 %shard_map.44 = (f32[19,10,8,128]{3,2,1,0:T(8,128)S(1)}, f32[5,8,8,128]{3,2,1,0:T(8,128)S(1)}, f32[9,2,8,128]{3,2,1,0:T(8,128)S(1)}, f32[6,8,128]{2,1,0:T(8,128)S(1)}, f32[6,8,128]{2,1,0:T(8,128)S(1)}) custom-call(f32[9,8,8,128]{3,2,1,0:T(8,128)S(1)} %get-tuple-element.33.base_ref, f32[35,8,128]{2,1,0:T(8,128)S(1)} %collective-permute-done.2.recv_b, ...), custom_call_target="tpu_custom_call" | custom-call | flops 20000000 | bytes 2342912 | tf_op jit(solution)/shard_map/pallas_call | solution.py:578
  32.5 3.1 %collective-permute-start.4 = (f32[6,8,128]{2,1,0:T(8,128)S(1)}, f32[6,8,128]{2,1,0:T(8,128)S(1)}, u32[]{:S(2)}, u32[]{:S(2)}) collective-permute-start(f32[6,8,128]{2,1,0:T(8,128)S(1)} %get-tuple-element.45), channel_id=1, source_target_pairs={{1,2},{4,3},{5,6},{8,7},{9,10},{12,11},{13,14},{0,15},{17,18},{20,... | collective-permute-start | bytes 73736 | tf_op jit(solution)/shard_map/ppermute | solution.py:653
  35.7 0.1 shard_map.45
  35.8 0.0 collective-permute-done.5.recv_down
  35.8 1.5 %shard_map.46 = (f32[19,64,128]{2,1,0:T(8,128)}, f32[5,64,128]{2,1,0:T(8,128)}) custom-call(f32[19,2,8,128]{3,2,1,0:T(8,128)S(1)} %get-tuple-element.37.edge_ref, f32[9,2,8,128]{3,2,1,0:T(8,128)S(1)} %get-tuple-element.44.far_ref, f32[6,8,128]{2,1,0:T(8,128)S(1)} %collective-permute-done.5.recv_down, f32[6,8,128]{2,1,0:T(8,128)S(1)} %get-tuple-element.54._.recv_first, ...), custom_call_target="tpu_custom_call" | custom-call | flops 8000000 | bytes 2007040 | tf_op jit(solution)/shard_map/pallas_call | solution.py:578
  37.3 0.0 collective-permute-done.4.recv_up
  37.3 0.1 shard_map.47
  (1 shorter events, 0.0 us)
Async XLA Ops:
  2.0 18.2 %collective-permute-start.2 = (f32[35,8,128]{2,1,0:T(8,128)S(1)}, f32[35,8,128]{2,1,0:T(8,128)S(1)}, u32[]{:S(2)}, u32[]{:S(2)}) collective-permute-start(f32[35,8,128]{2,1,0:T(8,128)S(1)} %get-tuple-element.35), channel_id=1, source_target_pairs={{0,1008},{16,32},{32,16},{48,64},{64,48},{80,96},{96,80},{112,128}... | collective-permute-start | bytes 430088 | tf_op jit(solution)/shard_map/ppermute | solution.py:620
  7.4 13.6 %collective-permute-start.3 = (f32[35,8,128]{2,1,0:T(8,128)S(1)}, f32[35,8,128]{2,1,0:T(8,128)S(1)}, u32[]{:S(2)}, u32[]{:S(2)}) collective-permute-start(f32[35,8,128]{2,1,0:T(8,128)S(1)} %get-tuple-element.36), channel_id=1, source_target_pairs={{0,16},{16,0},{32,48},{48,32},{64,80},{80,64},{96,112},{112,96},{1... | collective-permute-start | bytes 430088 | tf_op jit(solution)/shard_map/ppermute | solution.py:621
  21.2 14.6 %collective-permute-start.5 = (f32[6,8,128]{2,1,0:T(8,128)S(1)}, f32[6,8,128]{2,1,0:T(8,128)S(1)}, u32[]{:S(2)}, u32[]{:S(2)}) collective-permute-start(f32[6,8,128]{2,1,0:T(8,128)S(1)} %get-tuple-element.49), channel_id=1, source_target_pairs={{2,1},{3,4},{6,5},{7,8},{10,9},{11,12},{14,13},{15,0},{18,17},{19,... | collective-permute-start | bytes 73736 | tf_op jit(solution)/shard_map/ppermute | solution.py:633
  22.5 8.5 %collective-permute-start = (f32[6,8,128]{2,1,0:T(8,128)S(1)}, f32[6,8,128]{2,1,0:T(8,128)S(1)}, u32[]{:S(2)}, u32[]{:S(2)}) collective-permute-start(f32[6,8,128]{2,1,0:T(8,128)S(1)} %param), channel_id=1, source_target_pairs={{0,1},{1,0},{4,5},{5,4},{8,9},{9,8},{12,13},{13,12},{16,17},{17,16... | collective-permute-start | bytes 73736 | tf_op jit(solution)/shard_map/cond/branch_0_fun/ppermute | solution.py:636
  32.5 4.8 %collective-permute-start.4 = (f32[6,8,128]{2,1,0:T(8,128)S(1)}, f32[6,8,128]{2,1,0:T(8,128)S(1)}, u32[]{:S(2)}, u32[]{:S(2)}) collective-permute-start(f32[6,8,128]{2,1,0:T(8,128)S(1)} %get-tuple-element.45), channel_id=1, source_target_pairs={{1,2},{4,3},{5,6},{8,7},{9,10},{12,11},{13,14},{0,15},{17,18},{20,... | collective-permute-start | bytes 73736 | tf_op jit(solution)/shard_map/ppermute | solution.py:653

commit v8 on v7

--- a/solution.py
+++ b/solution.py
@@ -45,6 +45,7 @@
 y_down = [i for i in range(19) if lattice[i][1] == -1]
 
 VEL, DEN, POP, FACE = 20, 29, 30, 35
+STRIPS = 6
 SLOTS = 16
 near = sorted(y_up + y_down)
 far = [i for i in range(19) if i not in near]
@@ -183,8 +184,19 @@
                 yield j, rest * load(j) + (first + second if sign > 0 else first - second)
 
 
+def placed(value, row, into):
+    q = row % 8
+    lane = lanes()
+    mask = jnp.logical_and(lane >= SLOTS * q, lane < SLOTS * q + SLOTS)
+    return jnp.where(mask, roll_y(value, 8 + SLOTS * q), into)
+
+
+def is_late():
+    return lax.rem(lax.axis_index("col"), 4) >= 2
+
+
 def moments_kernel(
-    pop_hbm, order_hbm, base_ref, first_ref, second_ref, pop_ref, order_ref, sems
+    pop_hbm, order_hbm, base_ref, edge_ref, first_ref, second_ref, first_strip, second_strip, pop_ref, order_ref, sems
 ):
     copies = [
         pltpu.make_async_copy(order_hbm, order_ref, sems.at[0]),
@@ -214,6 +226,19 @@
         return carry
 
     lax.fori_loop(0, 8, row, 0, unroll=8)
+    def pack(load, fill, field):
+        low = high = jnp.full((8, 128), fill, f32)
+        for x in range(4):
+            low = placed(load(x), x + 4, low)
+            high = placed(load(x + 4), x + 8, high)
+        edge_ref[field, 0] = low
+        edge_ref[field, 1] = high
+
+    for f in range(9):
+        pack(lambda x, f=f: base_ref[f, x], 1.0 if f == 8 else 0.0, f)
+    for n, i in enumerate(near):
+        pack(lambda x, i=i: pop_ref[i, pl.ds(x, 8, stride=8), :], 0.0, 9 + n)
+
     even = is_even("row")
     for out, high in ((first_ref, even), (second_ref, jnp.logical_not(even))):
 
@@ -237,31 +262,37 @@
             for j, i in enumerate(x_down):
                 out[POP + j] = pop_ref[i, pl.ds(0, 8, stride=8), :]
 
-
-def placed(value, row, into):
-    q = row % 8
-    lane = lanes()
-    mask = jnp.logical_and(lane >= SLOTS * q, lane < SLOTS * q + SLOTS)
-    return jnp.where(mask, roll_y(value, 8 + SLOTS * q), into)
-
-
-def own_edges_kernel(base_ref, pop_ref, edge_ref):
-    def pack(load, fill, field):
-        low = high = jnp.full((8, 128), fill, f32)
-        for x in range(4):
-            low = placed(load(x), x + 4, low)
-            high = placed(load(x + 4), x + 8, high)
-        edge_ref[field, 0] = low
-        edge_ref[field, 1] = high
-
-    for f in range(9):
-        pack(lambda x, f=f: base_ref[f, x], 1.0 if f == 8 else 0.0, f)
-    for n, i in enumerate(near):
-        pack(lambda x, i=i: pop_ref[i, pl.ds(x, 8, stride=8), :], 0.0, 9 + n)
+    left_half = lanes() < 64
+    for out, high in ((first_strip, even), (second_strip, jnp.logical_not(even))):
+        for side, chosen in ((1, high), (0, jnp.logical_not(high))):
+
+            @pl.when(chosen)
+            def _():
+                fields = list(range(9)) + corner_fields(side)
+                mine = left_half if side else jnp.logical_not(left_half)
+                for n in range(0, len(fields), 2):
+                    value = edge_ref[fields[n], side]
+                    if n + 1 < len(fields):
+                        other = roll_y(edge_ref[fields[n + 1], side], 64)
+                        value = jnp.where(mine, value, other)
+                    out[n // 2] = value
+
+
+def corner_fields(side):
+    return [9 + near.index(i) for i in (x_up if side else x_down) if i in near]
 
 
 def column_message_kernel(
-    own_ref, recv_b, recv_a, edge_ref, first_ref, second_ref, third_ref, fourth_ref
+    own_ref,
+    recv_b,
+    recv_a,
+    strip_b,
+    strip_a,
+    edge_ref,
+    first_ref,
+    second_ref,
+    third_ref,
+    fourth_ref,
 ):
     even = is_even("row")
     slot = slots()
@@ -270,27 +301,46 @@
         a, b = recv_a[j], recv_b[j]
         return jnp.where(even, b, a), jnp.where(even, a, b)
 
-    def widen(field, rows):
-        low, high = own_ref[field, 0], own_ref[field, 1]
-        for j, row_low, row_high in rows:
-            below, above = halo(j)
-            low, high = placed(below, row_low, low), placed(above, row_high, high)
-        edge_ref[field, 0] = low
-        edge_ref[field, 1] = high
-
-    for k in range(5):
-        widen(k, [(4 * k + r, r, 12 + r) for r in range(4)])
-    for a in range(3):
-        widen(5 + a, [(VEL + 3 * a + r, 1 + r, 12 + r) for r in range(3)])
-    widen(8, [(DEN, 3, 12)])
-    for n, i in enumerate(near):
-        low, high = own_ref[9 + n, 0], own_ref[9 + n, 1]
-        if i in x_up:
-            low = placed(halo(POP + x_up.index(i))[0], 3, low)
-        if i in x_down:
-            high = placed(halo(POP + x_down.index(i))[1], 12, high)
-        edge_ref[9 + n, 0] = low
-        edge_ref[9 + n, 1] = high
+    @pl.when(jnp.logical_not(is_late()))
+    def _():
+        def widen(field, rows):
+            low, high = own_ref[field, 0], own_ref[field, 1]
+            for j, row_low, row_high in rows:
+                below, above = halo(j)
+                low, high = placed(below, row_low, low), placed(above, row_high, high)
+            edge_ref[field, 0] = low
+            edge_ref[field, 1] = high
+
+        for k in range(5):
+            widen(k, [(4 * k + r, r, 12 + r) for r in range(4)])
+        for a in range(3):
+            widen(5 + a, [(VEL + 3 * a + r, 1 + r, 12 + r) for r in range(3)])
+        widen(8, [(DEN, 3, 12)])
+        for n, i in enumerate(near):
+            low, high = own_ref[9 + n, 0], own_ref[9 + n, 1]
+            if i in x_up:
+                low = placed(halo(POP + x_up.index(i))[0], 3, low)
+            if i in x_down:
+                high = placed(halo(POP + x_down.index(i))[1], 12, high)
+            edge_ref[9 + n, 0] = low
+            edge_ref[9 + n, 1] = high
+
+    @pl.when(is_late())
+    def _():
+        left_half = lanes() < 64
+        below = [jnp.where(even, strip_b[n], strip_a[n]) for n in range(STRIPS)]
+        above = [jnp.where(even, strip_a[n], strip_b[n]) for n in range(STRIPS)]
+        for f in range(NEAR):
+            for half, vectors, keep in (
+                (0, below, left_half),
+                (1, above, jnp.logical_not(left_half)),
+            ):
+                fields = list(range(9)) + corner_fields(1 - half)
+                value = own_ref[f, half]
+                if f in fields:
+                    n = fields.index(f)
+                    value = jnp.where(keep, roll_y(vectors[n // 2], 64 * (n % 2)), value)
+                edge_ref[f, half] = value
 
     col_even = is_even("col")
     for h in range(2):
@@ -311,10 +361,6 @@
             to_right = jnp.where(slot == s, roll_y(edge_ref[right_field, h], s - 7), to_right)
         first_ref[4 + h] = third_ref[4 + h] = jnp.where(col_even, to_right, to_left)
         second_ref[4 + h] = fourth_ref[4 + h] = jnp.where(col_even, to_left, to_right)
-
-
-def is_late():
-    return lax.rem(lax.axis_index("col"), 4) >= 2
 
 
 def early_main_kernel(base_ref, recv_b, recv_a, pop_ref, third_ref, fourth_ref, _, *rest):
@@ -607,19 +653,30 @@
 
 
 def body(rows, cols, populations, order_tensor):
-    face, side = (FACE, 8, 128), (6, 8, 128)
-    base, first, second, pops = call(
+    face, side, strip = (FACE, 8, 128), (6, 8, 128), (STRIPS, 8, 128)
+    base, own_edges, first_rows, second_rows, first_strip, second_strip, pops = call(
         moments_kernel,
-        [(9, 8, 8, 128), face, face, (19, 64, 128)],
+        [(9, 8, 8, 128), (NEAR, 2, 8, 128), face, face, strip, strip, (19, 64, 128)],
         [(5, 64, 128), pltpu.SemaphoreType.DMA((2,))],
         2_000_000,
         pltpu.with_memory_space_constraint(populations.reshape(19, 64, 128), pltpu.HBM),
         pltpu.with_memory_space_constraint(order_tensor.reshape(5, 64, 128), pltpu.HBM),
         hbm_args=(0, 1),
     )
-    recv_b = lax.ppermute(second, "row", swap(rows, 1))
-    recv_a = lax.ppermute(first, "row", swap(rows, 0))
-    own_edges = call(own_edges_kernel, [(NEAR, 2, 8, 128)], [], 2_000_000, base, pops)[0]
+    late = lax.rem(lax.axis_index("col"), 4) >= 2
+
+    def swap_rows(second, first):
+        return lax.ppermute(second, "row", swap(rows, 1)), lax.ppermute(first, "row", swap(rows, 0))
+
+    recv_b, recv_a, strip_b, strip_a = lax.cond(
+        late,
+        lambda b, a, sb, sa: (b, a, *swap_rows(sb, sa)),
+        lambda b, a, sb, sa: (*swap_rows(b, a), sb, sa),
+        second_rows,
+        first_rows,
+        second_strip,
+        first_strip,
+    )
     edges, first, second, third, fourth = call(
         column_message_kernel,
         [(NEAR, 2, 8, 128), side, side, side, side],
@@ -628,10 +685,11 @@
         own_edges,
         recv_b,
         recv_a,
+        strip_b,
+        strip_a,
     )
     down, up = crossing(cols)
     recv_down = lax.ppermute(second, "col", down)
-    late = lax.rem(lax.axis_index("col"), 4) >= 2
     recv_first = lax.cond(
         late, lambda m: m, lambda m: lax.ppermute(m, "col", part(cols, False)), first
     )
@@ -651,8 +709,13 @@
         recv_first,
     )
     recv_up = lax.ppermute(fourth_again, "col", up)
-    recv_last = lax.cond(
-        late, lambda m: lax.ppermute(m, "col", part(cols, True)), lambda m: m, third_again
+    recv_last, recv_b, recv_a = lax.cond(
+        late,
+        lambda m, b, a: (lax.ppermute(m, "col", part(cols, True)), *swap_rows(b, a)),
+        lambda m, b, a: (m, b, a),
+        third_again,
+        recv_b,
+        recv_a,
     )
     moved, relaxed, far_edges = call(
         late_main_kernel,

time: 37.6 us -> 38.1 us (1.013)
  waiting for transfers between devices: 2.92 us -> 3.36 us
  starting transfers between devices: 28.7 us -> 28.3 us
    ppermute x1, starting transfers between devices: 3.14 us -> 2.72 us  [body(): recv_up = lax.ppermute(fourth_again, 'col', up)]
    pallas_call x7 -> x6, Pallas kernels: 4.99 us -> 5.1 us  [call(): pl.pallas_call(kernel, out_shape=[jax.ShapeDtypeStruct(s, f32) for s in o...]
  transfers between devices with their start and end apart: 5 -> 5, of which waited for: 2 -> 2; matrix products, arithmetic and copies ran while one was open for 0% -> 0% of each run, Pallas kernels for 9% -> 8%
where the time goes in v8:
time: 38.1 us; the launch traced here: 37.6 us
  starting transfers between devices  28.3 us (74%)
  Pallas kernels  5.1 us (13%)
  waiting for transfers between devices  3.36 us (9%)
  between operations  0.71 us (2%)
    ppermute x1, starting transfers between devices, swap_rows(): lax.ppermute(first, 'row', swap(rows, 0))  12.6 us
    ppermute x1, starting transfers between devices, body(): lax.ppermute(m, 'col', part(cols, False))  6.33 us
    ppermute x1, starting transfers between devices, swap_rows(): lax.ppermute(second, 'row', swap(rows, 1))  5.37 us
    pallas_call x6, Pallas kernels, call(): pl.pallas_call(kernel, out_shape=[jax.ShapeDtypeStruct(s, f32) for s in o...  5.1 us
    ppermute x1, starting transfers between devices, body(): recv_up = lax.ppermute(fourth_again, 'col', up)  2.72 us
    ppermute x1, waiting for transfers between devices, body(): lax.ppermute(m, 'col', part(cols, False))  2.38 us
    ppermute x1, starting transfers between devices, body(): recv_down = lax.ppermute(second, 'col', down)  1.29 us
    ppermute x1, waiting for transfers between devices, swap_rows(): lax.ppermute(first, 'row', swap(rows, 0))  0.97 us
  transfers between devices with their start and end apart: 5, of which 2 were waited for; matrix products, arithmetic and copies ran while one was open for 0% of the time, Pallas kernels for 8%

profile of v8, /device:TPU:1, one launch (start us, length us, event | category | flops | bytes accessed | tf_op | source)
XLA Modules:
  0.0 37.6 jit_solution(14229377738274192784)
XLA Ops:
  0.6 1.7 %shard_map.41 = (f32[9,8,8,128]{3,2,1,0:T(8,128)S(1)}, f32[19,2,8,128]{3,2,1,0:T(8,128)S(1)}, f32[35,8,128]{2,1,0:T(8,128)S(1)}, f32[35,8,128]{2,1,0:T(8,128)S(1...) custom-call(f32[19,64,128]{2,1,0:T(8,128)} %bitcast.4, f32[5,64,128]{2,1,0:T(8,128)} %bitcast.6), custom_call_target="tpu_custom_call" | custom-call | flops 2000000 | bytes 2195456 | tf_op jit(solution)/shard_map/pallas_call | solution.py:624
  2.3 19.0 %conditional.3 = (f32[35,8,128]{2,1,0:T(8,128)S(1)}, f32[35,8,128]{2,1,0:T(8,128)S(1)}, f32[6,8,128]{2,1,0:T(8,128)S(1)}, f32[6,8,128]{2,1,0:T(8,128)S(1)}) conditional(s32[]{:T(128)} %convert_element_type.2, (f32[35,8,128]{2,1,0:T(8,128)S(1)}, f32[35,8,128]{2,1,0:T(8,128)S(1)}, f32[6,8,128]{2,1,0:T(8,128)S(1)}, ...), branch_computations={%region_0.0_spmd, %region_1.0_spmd} | conditional | bytes 1146992 | solution.py:671
  2.3 5.4 %collective-permute-start = (f32[35,8,128]{2,1,0:T(8,128)S(1)}, f32[35,8,128]{2,1,0:T(8,128)S(1)}, u32[]{:S(2)}, u32[]{:S(2)}) collective-permute-start(f32[35,8,128]{2,1,0:T(8,128)S(1)} %get-tuple-element.33), channel_id=1, source_target_pairs={{0,1008},{16,32},{32,16},{48,64},{64,48},{80,96},{96,80},{112,128}... | collective-permute-start | bytes 430088 | tf_op jit(solution)/shard_map/cond/branch_0_fun/ppermute | solution.py:669
  7.7 12.6 %collective-permute-start.1 = (f32[35,8,128]{2,1,0:T(8,128)S(1)}, f32[35,8,128]{2,1,0:T(8,128)S(1)}, u32[]{:S(2)}, u32[]{:S(2)}) collective-permute-start(f32[35,8,128]{2,1,0:T(8,128)S(1)} %get-tuple-element.34), channel_id=1, source_target_pairs={{0,16},{16,0},{32,48},{48,32},{64,80},{80,64},{96,112},{112,96},{1... | collective-permute-start | bytes 430088 | tf_op jit(solution)/shard_map/cond/branch_0_fun/ppermute | solution.py:669
  20.3 0.0 collective-permute-done
  20.3 1.0 %collective-permute-done.1 = f32[35,8,128]{2,1,0:T(8,128)S(1)} collective-permute-done((f32[35,8,128]{2,1,0:T(8,128)S(1)}, f32[35,8,128]{2,1,0:T(8,128)S(1)}, u32[]{:S(2)}, u32[]{:S(2)}) %collective-permute-start.1) | collective-permute-done | bytes 143392 | tf_op jit(solution)/shard_map/cond/branch_0_fun/ppermute | solution.py:669
  21.3 0.3 shard_map.42
  21.6 1.3 %collective-permute-start.9 = (f32[6,8,128]{2,1,0:T(8,128)S(1)}, f32[6,8,128]{2,1,0:T(8,128)S(1)}, u32[]{:S(2)}, u32[]{:S(2)}) collective-permute-start(f32[6,8,128]{2,1,0:T(8,128)S(1)} %get-tuple-element.103), channel_id=1, source_target_pairs={{2,1},{3,4},{6,5},{7,8},{10,9},{11,12},{14,13},{15,0},{18,17},{19,... | collective-permute-start | bytes 73736 | tf_op jit(solution)/shard_map/ppermute | solution.py:692
  22.9 8.7 %conditional.4 = (f32[6,8,128]{2,1,0:T(8,128)S(1)}) conditional(s32[]{:T(128)} %convert_element_type.2, f32[6,8,128]{2,1,0:T(8,128)S(1)} %get-tuple-element.91, f32[6,8,128]{2,1,0:T(8,128)S(1)} %get-tuple-element.91), branch_computations={%region_2.0_spmd, %region_3.0_spmd} | conditional | bytes 98352 | solution.py:693
  22.9 6.3 %collective-permute-start.4 = (f32[6,8,128]{2,1,0:T(8,128)S(1)}, f32[6,8,128]{2,1,0:T(8,128)S(1)}, u32[]{:S(2)}, u32[]{:S(2)}) collective-permute-start(f32[6,8,128]{2,1,0:T(8,128)S(1)} %param.2), channel_id=1, source_target_pairs={{0,1},{1,0},{4,5},{5,4},{8,9},{9,8},{12,13},{13,12},{16,17},{17,16... | collective-permute-start | bytes 73736 | tf_op jit(solution)/shard_map/cond/branch_0_fun/ppermute | solution.py:694
  29.2 2.4 %collective-permute-done.4 = f32[6,8,128]{2,1,0:T(8,128)S(1)} collective-permute-done((f32[6,8,128]{2,1,0:T(8,128)S(1)}, f32[6,8,128]{2,1,0:T(8,128)S(1)}, u32[]{:S(2)}, u32[]{:S(2)}) %collective-permute-start.4) | collective-permute-done | bytes 24608 | tf_op jit(solution)/shard_map/cond/branch_0_fun/ppermute | solution.py:694
  31.6 1.5 %shard_map.43 = (f32[19,10,8,128]{3,2,1,0:T(8,128)S(1)}, f32[5,8,8,128]{3,2,1,0:T(8,128)S(1)}, f32[9,2,8,128]{3,2,1,0:T(8,128)S(1)}, f32[6,8,128]{2,1,0:T(8,128)S(1)}, f32[6,8,128]{2,1,0:T(8,128)S(1)}) custom-call(f32[9,8,8,128]{3,2,1,0:T(8,128)S(1)} %get-tuple-element.87.base_ref, f32[35,8,128]{2,1,0:T(8,128)S(1)} %get-tuple-element.82.recv_b, ...), custom_call_target="tpu_custom_call" | custom-call | flops 20000000 | bytes 2342912 | tf_op jit(solution)/shard_map/pallas_call | solution.py:624
  33.1 2.7 %collective-permute-start.8 = (f32[6,8,128]{2,1,0:T(8,128)S(1)}, f32[6,8,128]{2,1,0:T(8,128)S(1)}, u32[]{:S(2)}, u32[]{:S(2)}) collective-permute-start(f32[6,8,128]{2,1,0:T(8,128)S(1)} %get-tuple-element.99), channel_id=1, source_target_pairs={{1,2},{4,3},{5,6},{8,7},{9,10},{12,11},{13,14},{0,15},{17,18},{20,... | collective-permute-start | bytes 73736 | tf_op jit(solution)/shard_map/ppermute | solution.py:711
  35.8 0.1 shard_map.44
  35.9 0.0 collective-permute-done.9.recv_down
  35.9 1.5 %shard_map.45 = (f32[19,64,128]{2,1,0:T(8,128)}, f32[5,64,128]{2,1,0:T(8,128)}) custom-call(f32[19,2,8,128]{3,2,1,0:T(8,128)S(1)} %get-tuple-element.86.edge_ref, f32[9,2,8,128]{3,2,1,0:T(8,128)S(1)} %get-tuple-element.98.far_ref, f32[6,8,128]{2,1,0:T(8,128)S(1)} %collective-permute-done.9.recv_down, f32[6,8,128]{2,1,0:T(8,128)S(1)} %get-tuple-element.122._.recv_first, ...), custom_call_target="tpu_custom_call" | custom-call | flops 8000000 | bytes 2007040 | tf_op jit(solution)/shard_map/pallas_call | solution.py:624
  37.5 0.0 collective-permute-done.8.recv_up
  37.5 0.1 shard_map.46
  (1 shorter events, 0.0 us)
Async XLA Ops:
  2.3 18.0 %collective-permute-start = (f32[35,8,128]{2,1,0:T(8,128)S(1)}, f32[35,8,128]{2,1,0:T(8,128)S(1)}, u32[]{:S(2)}, u32[]{:S(2)}) collective-permute-start(f32[35,8,128]{2,1,0:T(8,128)S(1)} %get-tuple-element.33), channel_id=1, source_target_pairs={{0,1008},{16,32},{32,16},{48,64},{64,48},{80,96},{96,80},{112,128}... | collective-permute-start | bytes 430088 | tf_op jit(solution)/shard_map/cond/branch_0_fun/ppermute | solution.py:669
  7.7 13.6 %collective-permute-start.1 = (f32[35,8,128]{2,1,0:T(8,128)S(1)}, f32[35,8,128]{2,1,0:T(8,128)S(1)}, u32[]{:S(2)}, u32[]{:S(2)}) collective-permute-start(f32[35,8,128]{2,1,0:T(8,128)S(1)} %get-tuple-element.34), channel_id=1, source_target_pairs={{0,16},{16,0},{32,48},{48,32},{64,80},{80,64},{96,112},{112,96},{1... | collective-permute-start | bytes 430088 | tf_op jit(solution)/shard_map/cond/branch_0_fun/ppermute | solution.py:669
  21.6 14.4 %collective-permute-start.9 = (f32[6,8,128]{2,1,0:T(8,128)S(1)}, f32[6,8,128]{2,1,0:T(8,128)S(1)}, u32[]{:S(2)}, u32[]{:S(2)}) collective-permute-start(f32[6,8,128]{2,1,0:T(8,128)S(1)} %get-tuple-element.103), channel_id=1, source_target_pairs={{2,1},{3,4},{6,5},{7,8},{10,9},{11,12},{14,13},{15,0},{18,17},{19,... | collective-permute-start | bytes 73736 | tf_op jit(solution)/shard_map/ppermute | solution.py:692
  22.9 8.7 %collective-permute-start.4 = (f32[6,8,128]{2,1,0:T(8,128)S(1)}, f32[6,8,128]{2,1,0:T(8,128)S(1)}, u32[]{:S(2)}, u32[]{:S(2)}) collective-permute-start(f32[6,8,128]{2,1,0:T(8,128)S(1)} %param.2), channel_id=1, source_target_pairs={{0,1},{1,0},{4,5},{5,4},{8,9},{9,8},{12,13},{13,12},{16,17},{17,16... | collective-permute-start | bytes 73736 | tf_op jit(solution)/shard_map/cond/branch_0_fun/ppermute | solution.py:694
  33.1 4.4 %collective-permute-start.8 = (f32[6,8,128]{2,1,0:T(8,128)S(1)}, f32[6,8,128]{2,1,0:T(8,128)S(1)}, u32[]{:S(2)}, u32[]{:S(2)}) collective-permute-start(f32[6,8,128]{2,1,0:T(8,128)S(1)} %get-tuple-element.99), channel_id=1, source_target_pairs={{1,2},{4,3},{5,6},{8,7},{9,10},{12,11},{13,14},{0,15},{17,18},{20,... | collective-permute-start | bytes 73736 | tf_op jit(solution)/shard_map/ppermute | solution.py:711

commit v9 on v7

--- a/solution.py
+++ b/solution.py
@@ -413,7 +413,7 @@
             stream(i, value, x + 1)
         return carry
 
-    lax.fori_loop(0, 8, own_row, 0, unroll=4)
+    lax.fori_loop(0, 8, own_row, 0, unroll=8)
 
     for n, i in enumerate(far):
         low = high = jnp.zeros((8, 128), f32)

time: 37.6 us -> 37.6 us (level)
  no operation moved by 1% of the time
where the time goes in v9:
time: 37.6 us; the launch traced here: 37.4 us
  starting transfers between devices  28.7 us (76%)
  Pallas kernels  5.05 us (13%)
  waiting for transfers between devices  2.92 us (8%)
  between operations  0.74 us (2%)
    ppermute x1, starting transfers between devices, body(): recv_a = lax.ppermute(first, 'row', swap(rows, 0))  12.6 us
    ppermute x1, starting transfers between devices, body(): lax.ppermute(m, 'col', part(cols, False))  6.31 us
    ppermute x1, starting transfers between devices, body(): recv_b = lax.ppermute(second, 'row', swap(rows, 1))  5.39 us
    pallas_call x7, Pallas kernels, call(): pl.pallas_call(kernel, out_shape=[jax.ShapeDtypeStruct(s, f32) for s in o...  5.05 us
    ppermute x1, starting transfers between devices, body(): recv_up = lax.ppermute(fourth_again, 'col', up)  3.07 us
    ppermute x1, waiting for transfers between devices, body(): lax.ppermute(m, 'col', part(cols, False))  2.18 us
    ppermute x1, starting transfers between devices, body(): recv_down = lax.ppermute(second, 'col', down)  1.29 us
  transfers between devices with their start and end apart: 5, of which 2 were waited for; matrix products, arithmetic and copies ran while one was open for 0% of the time, Pallas kernels for 9%

profile of v9, /device:TPU:1, one launch (start us, length us, event | category | flops | bytes accessed | tf_op | source)
XLA Modules:
  0.0 37.4 jit_solution(13597692603910945005)
XLA Ops:
  0.6 1.3 %shard_map.41 = (f32[9,8,8,128]{3,2,1,0:T(8,128)S(1)}, f32[35,8,128]{2,1,0:T(8,128)S(1)}, f32[35,8,128]{2,1,0:T(8,128)S(1)}, f32[19,64,128]{2,1,0:T(8,128)S(1)}) custom-call(f32[19,64,128]{2,1,0:T(8,128)} %bitcast.4, f32[5,64,128]{2,1,0:T(8,128)} %bitcast.6), custom_call_target="tpu_custom_call" | custom-call | flops 2000000 | bytes 1990656 | tf_op jit(solution)/shard_map/pallas_call | solution.py:578
  2.0 5.4 %collective-permute-start.2 = (f32[35,8,128]{2,1,0:T(8,128)S(1)}, f32[35,8,128]{2,1,0:T(8,128)S(1)}, u32[]{:S(2)}, u32[]{:S(2)}) collective-permute-start(f32[35,8,128]{2,1,0:T(8,128)S(1)} %get-tuple-element.35), channel_id=1, source_target_pairs={{0,1008},{16,32},{32,16},{48,64},{64,48},{80,96},{96,80},{112,128}... | collective-permute-start | bytes 430088 | tf_op jit(solution)/shard_map/ppermute | solution.py:620
  7.4 12.6 %collective-permute-start.3 = (f32[35,8,128]{2,1,0:T(8,128)S(1)}, f32[35,8,128]{2,1,0:T(8,128)S(1)}, u32[]{:S(2)}, u32[]{:S(2)}) collective-permute-start(f32[35,8,128]{2,1,0:T(8,128)S(1)} %get-tuple-element.36), channel_id=1, source_target_pairs={{0,16},{16,0},{32,48},{48,32},{64,80},{80,64},{96,112},{112,96},{1... | collective-permute-start | bytes 430088 | tf_op jit(solution)/shard_map/ppermute | solution.py:621
  20.0 0.2 shard_map.42.own_ref
  20.2 0.0 collective-permute-done.2.recv_b
  20.2 0.7 %collective-permute-done.3.recv_a = f32[35,8,128]{2,1,0:T(8,128)S(1)} collective-permute-done((f32[35,8,128]{2,1,0:T(8,128)S(1)}, f32[35,8,128]{2,1,0:T(8,128)S(1)}, u32[]{:S(2)}, u32[]{:S(2)}) %collective-permute-start.3) | collective-permute-done | bytes 143392 | tf_op jit(solution)/shard_map/ppermute | solution.py:621
  21.0 0.2 shard_map.43
  21.2 1.3 %collective-permute-start.5 = (f32[6,8,128]{2,1,0:T(8,128)S(1)}, f32[6,8,128]{2,1,0:T(8,128)S(1)}, u32[]{:S(2)}, u32[]{:S(2)}) collective-permute-start(f32[6,8,128]{2,1,0:T(8,128)S(1)} %get-tuple-element.49), channel_id=1, source_target_pairs={{2,1},{3,4},{6,5},{7,8},{10,9},{11,12},{14,13},{15,0},{18,17},{19,... | collective-permute-start | bytes 73736 | tf_op jit(solution)/shard_map/ppermute | solution.py:633
  22.5 8.5 %conditional.2 = (f32[6,8,128]{2,1,0:T(8,128)S(1)}) conditional(s32[]{:T(128)} %convert_element_type.4, f32[6,8,128]{2,1,0:T(8,128)S(1)} %get-tuple-element.40, f32[6,8,128]{2,1,0:T(8,128)S(1)} %get-tuple-element.40), branch_computations={%region_0.0_spmd, %region_1.0_spmd} | conditional | bytes 98352 | solution.py:635
  22.5 6.3 %collective-permute-start = (f32[6,8,128]{2,1,0:T(8,128)S(1)}, f32[6,8,128]{2,1,0:T(8,128)S(1)}, u32[]{:S(2)}, u32[]{:S(2)}) collective-permute-start(f32[6,8,128]{2,1,0:T(8,128)S(1)} %param), channel_id=1, source_target_pairs={{0,1},{1,0},{4,5},{5,4},{8,9},{9,8},{12,13},{13,12},{16,17},{17,16... | collective-permute-start | bytes 73736 | tf_op jit(solution)/shard_map/cond/branch_0_fun/ppermute | solution.py:636
  28.8 2.2 %collective-permute-done = f32[6,8,128]{2,1,0:T(8,128)S(1)} collective-permute-done((f32[6,8,128]{2,1,0:T(8,128)S(1)}, f32[6,8,128]{2,1,0:T(8,128)S(1)}, u32[]{:S(2)}, u32[]{:S(2)}) %collective-permute-start) | collective-permute-done | bytes 24608 | tf_op jit(solution)/shard_map/cond/branch_0_fun/ppermute | solution.py:636
  31.0 1.6 %shard_map.44 = (f32[19,10,8,128]{3,2,1,0:T(8,128)S(1)}, f32[5,8,8,128]{3,2,1,0:T(8,128)S(1)}, f32[9,2,8,128]{3,2,1,0:T(8,128)S(1)}, f32[6,8,128]{2,1,0:T(8,128)S(1)}, f32[6,8,128]{2,1,0:T(8,128)S(1)}) custom-call(f32[9,8,8,128]{3,2,1,0:T(8,128)S(1)} %get-tuple-element.33.base_ref, f32[35,8,128]{2,1,0:T(8,128)S(1)} %collective-permute-done.2.recv_b, ...), custom_call_target="tpu_custom_call" | custom-call | flops 20000000 | bytes 2342912 | tf_op jit(solution)/shard_map/pallas_call | solution.py:578
  32.6 3.1 %collective-permute-start.4 = (f32[6,8,128]{2,1,0:T(8,128)S(1)}, f32[6,8,128]{2,1,0:T(8,128)S(1)}, u32[]{:S(2)}, u32[]{:S(2)}) collective-permute-start(f32[6,8,128]{2,1,0:T(8,128)S(1)} %get-tuple-element.45), channel_id=1, source_target_pairs={{1,2},{4,3},{5,6},{8,7},{9,10},{12,11},{13,14},{0,15},{17,18},{20,... | collective-permute-start | bytes 73736 | tf_op jit(solution)/shard_map/ppermute | solution.py:653
  35.7 0.1 shard_map.45
  35.8 0.0 collective-permute-done.5.recv_down
  35.8 1.5 %shard_map.46 = (f32[19,64,128]{2,1,0:T(8,128)}, f32[5,64,128]{2,1,0:T(8,128)}) custom-call(f32[19,2,8,128]{3,2,1,0:T(8,128)S(1)} %get-tuple-element.37.edge_ref, f32[9,2,8,128]{3,2,1,0:T(8,128)S(1)} %get-tuple-element.44.far_ref, f32[6,8,128]{2,1,0:T(8,128)S(1)} %collective-permute-done.5.recv_down, f32[6,8,128]{2,1,0:T(8,128)S(1)} %get-tuple-element.54._.recv_first, ...), custom_call_target="tpu_custom_call" | custom-call | flops 8000000 | bytes 2007040 | tf_op jit(solution)/shard_map/pallas_call | solution.py:578
  37.3 0.0 collective-permute-done.4.recv_up
  37.3 0.1 shard_map.47
  (1 shorter events, 0.0 us)
Async XLA Ops:
  2.0 18.2 %collective-permute-start.2 = (f32[35,8,128]{2,1,0:T(8,128)S(1)}, f32[35,8,128]{2,1,0:T(8,128)S(1)}, u32[]{:S(2)}, u32[]{:S(2)}) collective-permute-start(f32[35,8,128]{2,1,0:T(8,128)S(1)} %get-tuple-element.35), channel_id=1, source_target_pairs={{0,1008},{16,32},{32,16},{48,64},{64,48},{80,96},{96,80},{112,128}... | collective-permute-start | bytes 430088 | tf_op jit(solution)/shard_map/ppermute | solution.py:620
  7.4 13.6 %collective-permute-start.3 = (f32[35,8,128]{2,1,0:T(8,128)S(1)}, f32[35,8,128]{2,1,0:T(8,128)S(1)}, u32[]{:S(2)}, u32[]{:S(2)}) collective-permute-start(f32[35,8,128]{2,1,0:T(8,128)S(1)} %get-tuple-element.36), channel_id=1, source_target_pairs={{0,16},{16,0},{32,48},{48,32},{64,80},{80,64},{96,112},{112,96},{1... | collective-permute-start | bytes 430088 | tf_op jit(solution)/shard_map/ppermute | solution.py:621
  21.2 14.6 %collective-permute-start.5 = (f32[6,8,128]{2,1,0:T(8,128)S(1)}, f32[6,8,128]{2,1,0:T(8,128)S(1)}, u32[]{:S(2)}, u32[]{:S(2)}) collective-permute-start(f32[6,8,128]{2,1,0:T(8,128)S(1)} %get-tuple-element.49), channel_id=1, source_target_pairs={{2,1},{3,4},{6,5},{7,8},{10,9},{11,12},{14,13},{15,0},{18,17},{19,... | collective-permute-start | bytes 73736 | tf_op jit(solution)/shard_map/ppermute | solution.py:633
  22.5 8.5 %collective-permute-start = (f32[6,8,128]{2,1,0:T(8,128)S(1)}, f32[6,8,128]{2,1,0:T(8,128)S(1)}, u32[]{:S(2)}, u32[]{:S(2)}) collective-permute-start(f32[6,8,128]{2,1,0:T(8,128)S(1)} %param), channel_id=1, source_target_pairs={{0,1},{1,0},{4,5},{5,4},{8,9},{9,8},{12,13},{13,12},{16,17},{17,16... | collective-permute-start | bytes 73736 | tf_op jit(solution)/shard_map/cond/branch_0_fun/ppermute | solution.py:636
  32.6 4.8 %collective-permute-start.4 = (f32[6,8,128]{2,1,0:T(8,128)S(1)}, f32[6,8,128]{2,1,0:T(8,128)S(1)}, u32[]{:S(2)}, u32[]{:S(2)}) collective-permute-start(f32[6,8,128]{2,1,0:T(8,128)S(1)} %get-tuple-element.45), channel_id=1, source_target_pairs={{1,2},{4,3},{5,6},{8,7},{9,10},{12,11},{13,14},{0,15},{17,18},{20,... | collective-permute-start | bytes 73736 | tf_op jit(solution)/shard_map/ppermute | solution.py:653
